TPU v7x, 32 devices: a whole 2x2x4 slice. The times are simulated.
32 devices in a mesh: groups: 2 (over x), seq: 16 (over z, y, core).
Axes of the slice: x: 2, y: 2, z: 4, core: 2. Of those that a mesh axis runs over, the one named last changes fastest.
Arguments:
- queries: bfloat16 [8192, 4096], P(('groups', 'seq')), parts along dimension 0, may hold values from -12 to 12
- keys: bfloat16 [8192, 512], P(('groups', 'seq')), parts along dimension 0, may hold values from -6 to 6
- values: bfloat16 [8192, 512], P(('groups', 'seq')), parts along dimension 0, may hold values from -6 to 6
- grad_out: bfloat16 [8192, 4096], P(('groups', 'seq')), parts along dimension 0, may hold values from -6 to 6
- episode_lengths: int32 [32], P('groups'), parts along dimension 0, may hold values from 1 to 512, 4096 in all
Outputs:
- attn_out: bfloat16 [8192, 4096], P(('groups', 'seq')), parts along dimension 0
- grad_queries: bfloat16 [8192, 4096], P(('groups', 'seq')), parts along dimension 0
- grad_keys: bfloat16 [8192, 512], P(('groups', 'seq')), parts along dimension 0
- grad_values: bfloat16 [8192, 512], P(('groups', 'seq')), parts along dimension 0
There are 2 independent parts, one for each index of `groups`. A program takes and returns all parts, laid end to end along the dimension named above; each array names one. Nothing has to cross between parts.
Inputs may be any that keep to these rules, and one draw needn't show every extreme that they name: `episode_lengths`: the lengths sum to 4096; the largest is exactly 512.
All inputs are finite; a program needn't handle non-finite values.
Results may differ from a plain program's by a relative error of at most 0.015.
Values may be sent and summed in bfloat16 or wider, within the bound.
No kernel may reach another device: no remote copies, remote signals or barrier semaphores. Data moves between devices by JAX's collectives and lax.ppermute only.
A program may use at most 64 MiB of HBM per device.

v0:
```python
import math

import jax
import jax.numpy as jnp
from jax import lax
from jax.sharding import PartitionSpec as P

HEAD_DIM = 128


def shifted(value, axis, steps):
    count = lax.axis_size(axis)
    leading, last = (max(0, -steps), min(count, count - steps))
    return lax.ppermute(value, axis, [(source, source + steps) for source in range(leading, last)])


def episode_of(episode_lengths, position):
    episode_ends = jnp.cumsum(episode_lengths)
    covered = jnp.sum((episode_ends[None, :] <= position[:, None]).astype(jnp.int32), axis=1)
    return jnp.where(position < 0, -1, covered)


def on_device(queries, keys, values, grad_out, episode_lengths):
    row_count = queries.shape[0]
    kv_width = keys.shape[1]
    groups = kv_width // HEAD_DIM
    per_group = queries.shape[1] // kv_width
    head_cols = per_group * HEAD_DIM
    factor = 1.0 / math.sqrt(HEAD_DIM)
    row_start = lax.axis_index("seq") * row_count
    stacked = jnp.stack([keys, values])
    near_rows = shifted(stacked, "seq", 1)
    far_rows = shifted(stacked, "seq", 2)
    key_rows = jnp.concatenate([far_rows[0], near_rows[0], keys], axis=0)
    value_rows = jnp.concatenate([far_rows[1], near_rows[1], values], axis=0)
    query_label = episode_of(episode_lengths, row_start + jnp.arange(row_count, dtype=jnp.int32))
    key_label = episode_of(
        episode_lengths, row_start - 2 * row_count + jnp.arange(3 * row_count, dtype=jnp.int32)
    )
    causal = (
        jnp.arange(3 * row_count, dtype=jnp.int32)[None, :]
        <= (2 * row_count + jnp.arange(row_count, dtype=jnp.int32))[:, None]
    )
    allowed = (query_label[:, None] == key_label[None, :]) & causal

    def one_group(group_index, buffers):
        attended_all, grad_query_all, grad_key_all, grad_value_all = buffers
        query_group = lax.dynamic_slice_in_dim(
            queries, group_index * head_cols, head_cols, 1
        ).reshape(row_count, per_group, HEAD_DIM)
        grad_group = lax.dynamic_slice_in_dim(
            grad_out, group_index * head_cols, head_cols, 1
        ).reshape(row_count, per_group, HEAD_DIM)
        key_group = lax.dynamic_slice_in_dim(key_rows, group_index * HEAD_DIM, HEAD_DIM, 1)
        value_group = lax.dynamic_slice_in_dim(value_rows, group_index * HEAD_DIM, HEAD_DIM, 1)
        scores = (
            jnp.einsum("ihd,jd->hij", query_group, key_group, preferred_element_type=jnp.float32)
            * factor
        )
        masked = jnp.where(allowed[None], scores, -jnp.inf)
        row_max = jnp.max(masked, axis=2, keepdims=True)
        log_total = row_max + jnp.log(jnp.sum(jnp.exp(masked - row_max), axis=2, keepdims=True))
        soft_probs = jnp.exp(masked - log_total)
        weights = soft_probs.astype(jnp.bfloat16)
        out_group = jnp.einsum(
            "hij,jd->ihd", weights, value_group, preferred_element_type=jnp.float32
        ).astype(jnp.bfloat16)
        grad_probs = jnp.einsum(
            "ihd,jd->hij", grad_group, value_group, preferred_element_type=jnp.float32
        )
        row_delta = jnp.einsum(
            "ihd,ihd->hi", grad_group, out_group, preferred_element_type=jnp.float32
        )
        grad_scores = (soft_probs * (grad_probs - row_delta[:, :, None])).astype(jnp.bfloat16)
        grad_query = (
            jnp.einsum("hij,jd->ihd", grad_scores, key_group, preferred_element_type=jnp.float32)
            * factor
        ).astype(jnp.bfloat16)
        grad_key = jnp.einsum(
            "hij,ihd->jd", grad_scores, query_group, preferred_element_type=jnp.float32
        )
        grad_value = jnp.einsum(
            "hij,ihd->jd", weights, grad_group, preferred_element_type=jnp.float32
        )
        attended_all = lax.dynamic_update_slice_in_dim(
            attended_all, out_group.reshape(row_count, head_cols), group_index * head_cols, 1
        )
        grad_query_all = lax.dynamic_update_slice_in_dim(
            grad_query_all, grad_query.reshape(row_count, head_cols), group_index * head_cols, 1
        )
        grad_key_all = lax.dynamic_update_slice_in_dim(
            grad_key_all, grad_key, group_index * HEAD_DIM, 1
        )
        grad_value_all = lax.dynamic_update_slice_in_dim(
            grad_value_all, grad_value, group_index * HEAD_DIM, 1
        )
        return (attended_all, grad_query_all, grad_key_all, grad_value_all)

    initial = (
        jnp.zeros(queries.shape, jnp.bfloat16),
        jnp.zeros(queries.shape, jnp.bfloat16),
        jnp.zeros((3 * row_count, kv_width), jnp.float32),
        jnp.zeros((3 * row_count, kv_width), jnp.float32),
    )
    attn_out, grad_queries, grad_key_all, grad_value_all = lax.fori_loop(
        0, groups, one_group, initial
    )
    partials = jnp.stack([grad_key_all, grad_value_all])
    far_partial = partials[:, :row_count]
    near_partial = partials[:, row_count : 2 * row_count]
    own_partial = partials[:, 2 * row_count :]
    near_back = shifted(near_partial, "seq", -1)
    far_back = shifted(far_partial.astype(jnp.bfloat16), "seq", -2).astype(far_partial.dtype)
    summed = own_partial + near_back + far_back
    grad_keys = (summed[0] * factor).astype(jnp.bfloat16)
    grad_values = summed[1].astype(jnp.bfloat16)
    return (attn_out, grad_queries, grad_keys, grad_values)


def solution(mesh):
    in_specs = (
        P(("groups", "seq"), None),
        P(("groups", "seq"), None),
        P(("groups", "seq"), None),
        P(("groups", "seq"), None),
        P("groups"),
    )
    out_specs = (
        P(("groups", "seq"), None),
        P(("groups", "seq"), None),
        P(("groups", "seq"), None),
        P(("groups", "seq"), None),
    )
    return jax.shard_map(
        on_device, mesh=mesh, in_specs=in_specs, out_specs=out_specs, check_vma=False
    )
```

profile of v0, /device:TPU:0, one launch (start us, length us, event | category | flops | bytes accessed | tf_op | source)
XLA Modules:
  0.0 163.5 jit_solution(7968231499177775054)
XLA Ops:
  1.8 2.4 %collective-permute-start.1 = (bf16[2,256,512]{2,1,0:T(8,128)(2,1)S(1)}, bf16[2,256,512]{2,1,0:T(8,128)(2,1)S(1)}, u32[]{:S(2)}, u32[]{:S(2)}) collective-permute-start(bf16[2,256,512]{2,1,0:T(8,128)(2,1)S(1)} %pad_maximum_fusion.3), channel_id=1, source_target_pairs={{0,1},{1,2},{2,3},{3,4},{4,5},{5,6},{6,7},{7,8},{8,9},{9,10},{10,1... | collective-permute-start | bytes 1572872 | tf_op jit(solution)/shard_map/ppermute | solution.py:14
  4.2 4.4 %collective-permute-start = (bf16[2,256,512]{2,1,0:T(8,128)(2,1)S(1)}, bf16[2,256,512]{2,1,0:T(8,128)(2,1)S(1)}, u32[]{:S(2)}, u32[]{:S(2)}) collective-permute-start(bf16[2,256,512]{2,1,0:T(8,128)(2,1)S(1)} %pad_maximum_fusion.3), channel_id=1, source_target_pairs={{0,2},{1,3},{2,4},{3,5},{4,6},{5,7},{6,8},{7,9},{8,10},{9,11},{10,... | collective-permute-start | bytes 1572872 | tf_op jit(solution)/shard_map/ppermute | solution.py:14
  9.8 11.2 %collective-permute-done = bf16[2,256,512]{2,1,0:T(8,128)(2,1)S(1)} collective-permute-done((bf16[2,256,512]{2,1,0:T(8,128)(2,1)S(1)}, bf16[2,256,512]{2,1,0:T(8,128)(2,1)S(1)}, u32[]{:S(2)}, u32[]{:S(2)}) %collective-permute-start) | collective-permute-done | bytes 524320 | tf_op jit(solution)/shard_map/ppermute | solution.py:14
  22.3 1.4 broadcast.65.clone
  25.1 1.6 broadcast.64.clone2
  26.6 1.6 broadcast.64.clone
  28.2 100.4 %while.20 = (s32[]{:T(128)}, bf16[256,4096]{1,0:T(8,128)(2,1)}, bf16[256,4096]{1,0:T(8,128)(2,1)}, f32[768,512]{1,0:T(8,128)}, f32[768,512]{1,0:T(8,128)}, /*ind...) while((s32[]{:T(128)}, bf16[256,4096]{1,0:T(8,128)(2,1)}, ...), condition=%wide.region_6.7_spmd.clone, body=%wide.region_3.6_spmd.clone.sunk | while | flops 2451369984 | bytes 104035752 | solution.py:105
  31.2 2.0 %fusion.66 = (f32[8,256]{1,0:T(8,128)S(1)}, f32[768,256,8]{1,0,2:T(8,128)S(1)}) fusion(pred[256,768]{0,1:T(8,128)(4,1)S(1)} %fusion.65, bf16[256,8,128]{0,2,1:T(8,128)(2,1)S(1)} %bitcast.133, bf16[768,512]{1,0:T(8,128)(2,1)} %get-tuple-element.422, s32[]{:T(128)S(6)} %select_n.77), kind=kOutput, calls=%fused_computation.8.clone.1 | convolution fusion | flops 407369728 | bytes 7217156 | tf_op jit(solution)/shard_map/while/body/eval_jaxpr/ihd,jd->hij/dot_general | solution.py:57
  35.8 3.4 %fusion.67 = (f32[8,256]{1,0:T(8,128)S(1)}, bf16[128,8,256]{2,0,1:T(8,128)(2,1)}) fusion(bf16[256,1024]{0,1:T(8,128)(2,1)S(1)} %copy.74, f32[768,256,8]{1,0,2:T(8,128)S(1)} %get-tuple-element.374, f32[8,256]{1,0:T(8,128)S(1)} %log_add_fusion.2, pred[256,768]{0,1:T(8,128)(4,1)S(1)} %fusion.65, bf16[768,512]{1,0:T(8,128)(2,1)} %get-tuple-element.421, ...), kind=kOutput, calls=%fused_computation.17.clone.1 | convolution fusion | flops 410253312 | bytes 7749636 | tf_op jit(solution)/shard_map/while/body/eval_jaxpr/hij,jd->ihd/dot_general | solution.py:65
  40.6 5.3 %fusion.71 = f32[768,512]{1,0:T(8,128)} fusion(f32[768,512]{1,0:T(8,128)} %get-tuple-element.402, s32[]{:T(128)S(6)} %select_n.77, bf16[256,8,128]{0,2,1:T(8,128)(2,1)} %bitcast.139, f32[768,256,8]{1,0,2:T(8,128)} %copy-done, f32[8,256]{1,0:T(8,128)S(1)} %log_add_fusion.2, pred[256,768]{0,1:T(8,128)(4,1)S(1)} %fusion.65), kind=kOutput, calls=%fused_computation.13.clone.1 | convolution fusion | flops 408944640 | bytes 7413764 | tf_op jit(solution)/shard_map/while/body/eval_jaxpr/hij,ihd->jd/dot_general | solution.py:82
  45.9 2.8 %fusion.68 = bf16[8,256,768]{1,2,0:T(8,128)(2,1)S(1)} fusion(f32[768,256,8]{1,0,2:T(8,128)S(1)} %bitcast.132, f32[8,256]{1,0:T(8,128)S(1)} %get-tuple-element.376, f32[8,256]{1,0:T(8,128)S(1)} %log_add_fusion.2, pred[256,768]{0,1:T(8,128)(4,1)S(1)} %fusion.65, bf16[256,8,128]{0,2,1:T(8,128)(2,1)S(1)} %bitcast.140, ...), kind=kOutput, calls=%fused_computation.3.clone.1 | convolution fusion | flops 412090368 | bytes 10371076 | tf_op jit(solution)/shard_map/while/body/eval_jaxpr/ihd,jd->hij/dot_general | solution.py:68
  48.7 1.5 fusion.69
  50.3 1.8 %fusion.70 = f32[768,512]{1,0:T(8,128)} fusion(f32[768,512]{1,0:T(8,128)} %get-tuple-element.401, s32[]{:T(128)S(6)} %select_n.77, bf16[8,256,768]{1,2,0:T(8,128)(2,1)S(1)} %fusion.68, bf16[256,8,128]{0,2,1:T(8,128)(2,1)S(1)} %bitcast.134), kind=kOutput, calls=%fused_computation.15.clone.1 | convolution fusion | flops 402653184 | bytes 4063236 | tf_op jit(solution)/shard_map/while/body/eval_jaxpr/hij,ihd->jd/dot_general | solution.py:79
  56.3 2.0 %fusion.66 = (f32[8,256]{1,0:T(8,128)S(1)}, f32[768,256,8]{1,0,2:T(8,128)S(1)}) fusion(pred[256,768]{0,1:T(8,128)(4,1)S(1)} %fusion.65, bf16[256,8,128]{0,2,1:T(8,128)(2,1)S(1)} %bitcast.133, bf16[768,512]{1,0:T(8,128)(2,1)} %get-tuple-element.422, s32[]{:T(128)S(6)} %select_n.77), kind=kOutput, calls=%fused_computation.8.clone.1 | convolution fusion | flops 407369728 | bytes 7217156 | tf_op jit(solution)/shard_map/while/body/eval_jaxpr/ihd,jd->hij/dot_general | solution.py:57
  60.9 3.4 %fusion.67 = (f32[8,256]{1,0:T(8,128)S(1)}, bf16[128,8,256]{2,0,1:T(8,128)(2,1)}) fusion(bf16[256,1024]{0,1:T(8,128)(2,1)S(1)} %copy.74, f32[768,256,8]{1,0,2:T(8,128)S(1)} %get-tuple-element.374, f32[8,256]{1,0:T(8,128)S(1)} %log_add_fusion.2, pred[256,768]{0,1:T(8,128)(4,1)S(1)} %fusion.65, bf16[768,512]{1,0:T(8,128)(2,1)} %get-tuple-element.421, ...), kind=kOutput, calls=%fused_computation.17.clone.1 | convolution fusion | flops 410253312 | bytes 7749636 | tf_op jit(solution)/shard_map/while/body/eval_jaxpr/hij,jd->ihd/dot_general | solution.py:65
  65.7 5.2 %fusion.71 = f32[768,512]{1,0:T(8,128)} fusion(f32[768,512]{1,0:T(8,128)} %get-tuple-element.402, s32[]{:T(128)S(6)} %select_n.77, bf16[256,8,128]{0,2,1:T(8,128)(2,1)} %bitcast.139, f32[768,256,8]{1,0,2:T(8,128)} %copy-done, f32[8,256]{1,0:T(8,128)S(1)} %log_add_fusion.2, pred[256,768]{0,1:T(8,128)(4,1)S(1)} %fusion.65), kind=kOutput, calls=%fused_computation.13.clone.1 | convolution fusion | flops 408944640 | bytes 7413764 | tf_op jit(solution)/shard_map/while/body/eval_jaxpr/hij,ihd->jd/dot_general | solution.py:82
  71.0 2.8 %fusion.68 = bf16[8,256,768]{1,2,0:T(8,128)(2,1)S(1)} fusion(f32[768,256,8]{1,0,2:T(8,128)S(1)} %bitcast.132, f32[8,256]{1,0:T(8,128)S(1)} %get-tuple-element.376, f32[8,256]{1,0:T(8,128)S(1)} %log_add_fusion.2, pred[256,768]{0,1:T(8,128)(4,1)S(1)} %fusion.65, bf16[256,8,128]{0,2,1:T(8,128)(2,1)S(1)} %bitcast.140, ...), kind=kOutput, calls=%fused_computation.3.clone.1 | convolution fusion | flops 412090368 | bytes 10371076 | tf_op jit(solution)/shard_map/while/body/eval_jaxpr/ihd,jd->hij/dot_general | solution.py:68
  73.8 1.5 fusion.69
  75.3 1.8 %fusion.70 = f32[768,512]{1,0:T(8,128)} fusion(f32[768,512]{1,0:T(8,128)} %get-tuple-element.401, s32[]{:T(128)S(6)} %select_n.77, bf16[8,256,768]{1,2,0:T(8,128)(2,1)S(1)} %fusion.68, bf16[256,8,128]{0,2,1:T(8,128)(2,1)S(1)} %bitcast.134), kind=kOutput, calls=%fused_computation.15.clone.1 | convolution fusion | flops 402653184 | bytes 4063236 | tf_op jit(solution)/shard_map/while/body/eval_jaxpr/hij,ihd->jd/dot_general | solution.py:79
  81.3 2.0 %fusion.66 = (f32[8,256]{1,0:T(8,128)S(1)}, f32[768,256,8]{1,0,2:T(8,128)S(1)}) fusion(pred[256,768]{0,1:T(8,128)(4,1)S(1)} %fusion.65, bf16[256,8,128]{0,2,1:T(8,128)(2,1)S(1)} %bitcast.133, bf16[768,512]{1,0:T(8,128)(2,1)} %get-tuple-element.422, s32[]{:T(128)S(6)} %select_n.77), kind=kOutput, calls=%fused_computation.8.clone.1 | convolution fusion | flops 407369728 | bytes 7217156 | tf_op jit(solution)/shard_map/while/body/eval_jaxpr/ihd,jd->hij/dot_general | solution.py:57
  86.0 3.4 %fusion.67 = (f32[8,256]{1,0:T(8,128)S(1)}, bf16[128,8,256]{2,0,1:T(8,128)(2,1)}) fusion(bf16[256,1024]{0,1:T(8,128)(2,1)S(1)} %copy.74, f32[768,256,8]{1,0,2:T(8,128)S(1)} %get-tuple-element.374, f32[8,256]{1,0:T(8,128)S(1)} %log_add_fusion.2, pred[256,768]{0,1:T(8,128)(4,1)S(1)} %fusion.65, bf16[768,512]{1,0:T(8,128)(2,1)} %get-tuple-element.421, ...), kind=kOutput, calls=%fused_computation.17.clone.1 | convolution fusion | flops 410253312 | bytes 7749636 | tf_op jit(solution)/shard_map/while/body/eval_jaxpr/hij,jd->ihd/dot_general | solution.py:65
  90.8 5.3 %fusion.71 = f32[768,512]{1,0:T(8,128)} fusion(f32[768,512]{1,0:T(8,128)} %get-tuple-element.402, s32[]{:T(128)S(6)} %select_n.77, bf16[256,8,128]{0,2,1:T(8,128)(2,1)} %bitcast.139, f32[768,256,8]{1,0,2:T(8,128)} %copy-done, f32[8,256]{1,0:T(8,128)S(1)} %log_add_fusion.2, pred[256,768]{0,1:T(8,128)(4,1)S(1)} %fusion.65), kind=kOutput, calls=%fused_computation.13.clone.1 | convolution fusion | flops 408944640 | bytes 7413764 | tf_op jit(solution)/shard_map/while/body/eval_jaxpr/hij,ihd->jd/dot_general | solution.py:82
  96.1 2.8 %fusion.68 = bf16[8,256,768]{1,2,0:T(8,128)(2,1)S(1)} fusion(f32[768,256,8]{1,0,2:T(8,128)S(1)} %bitcast.132, f32[8,256]{1,0:T(8,128)S(1)} %get-tuple-element.376, f32[8,256]{1,0:T(8,128)S(1)} %log_add_fusion.2, pred[256,768]{0,1:T(8,128)(4,1)S(1)} %fusion.65, bf16[256,8,128]{0,2,1:T(8,128)(2,1)S(1)} %bitcast.140, ...), kind=kOutput, calls=%fused_computation.3.clone.1 | convolution fusion | flops 412090368 | bytes 10371076 | tf_op jit(solution)/shard_map/while/body/eval_jaxpr/ihd,jd->hij/dot_general | solution.py:68
  98.9 1.5 fusion.69
  100.5 1.7 %fusion.70 = f32[768,512]{1,0:T(8,128)} fusion(f32[768,512]{1,0:T(8,128)} %get-tuple-element.401, s32[]{:T(128)S(6)} %select_n.77, bf16[8,256,768]{1,2,0:T(8,128)(2,1)S(1)} %fusion.68, bf16[256,8,128]{0,2,1:T(8,128)(2,1)S(1)} %bitcast.134), kind=kOutput, calls=%fused_computation.15.clone.1 | convolution fusion | flops 402653184 | bytes 4063236 | tf_op jit(solution)/shard_map/while/body/eval_jaxpr/hij,ihd->jd/dot_general | solution.py:79
  106.5 2.0 %fusion.66 = (f32[8,256]{1,0:T(8,128)S(1)}, f32[768,256,8]{1,0,2:T(8,128)S(1)}) fusion(pred[256,768]{0,1:T(8,128)(4,1)S(1)} %fusion.65, bf16[256,8,128]{0,2,1:T(8,128)(2,1)S(1)} %bitcast.133, bf16[768,512]{1,0:T(8,128)(2,1)} %get-tuple-element.422, s32[]{:T(128)S(6)} %select_n.77), kind=kOutput, calls=%fused_computation.8.clone.1 | convolution fusion | flops 407369728 | bytes 7217156 | tf_op jit(solution)/shard_map/while/body/eval_jaxpr/ihd,jd->hij/dot_general | solution.py:57
  111.1 3.4 %fusion.67 = (f32[8,256]{1,0:T(8,128)S(1)}, bf16[128,8,256]{2,0,1:T(8,128)(2,1)}) fusion(bf16[256,1024]{0,1:T(8,128)(2,1)S(1)} %copy.74, f32[768,256,8]{1,0,2:T(8,128)S(1)} %get-tuple-element.374, f32[8,256]{1,0:T(8,128)S(1)} %log_add_fusion.2, pred[256,768]{0,1:T(8,128)(4,1)S(1)} %fusion.65, bf16[768,512]{1,0:T(8,128)(2,1)} %get-tuple-element.421, ...), kind=kOutput, calls=%fused_computation.17.clone.1 | convolution fusion | flops 410253312 | bytes 7749636 | tf_op jit(solution)/shard_map/while/body/eval_jaxpr/hij,jd->ihd/dot_general | solution.py:65
  115.9 5.3 %fusion.71 = f32[768,512]{1,0:T(8,128)} fusion(f32[768,512]{1,0:T(8,128)} %get-tuple-element.402, s32[]{:T(128)S(6)} %select_n.77, bf16[256,8,128]{0,2,1:T(8,128)(2,1)} %bitcast.139, f32[768,256,8]{1,0,2:T(8,128)} %copy-done, f32[8,256]{1,0:T(8,128)S(1)} %log_add_fusion.2, pred[256,768]{0,1:T(8,128)(4,1)S(1)} %fusion.65), kind=kOutput, calls=%fused_computation.13.clone.1 | convolution fusion | flops 408944640 | bytes 7413764 | tf_op jit(solution)/shard_map/while/body/eval_jaxpr/hij,ihd->jd/dot_general | solution.py:82
  121.2 2.8 %fusion.68 = bf16[8,256,768]{1,2,0:T(8,128)(2,1)S(1)} fusion(f32[768,256,8]{1,0,2:T(8,128)S(1)} %bitcast.132, f32[8,256]{1,0:T(8,128)S(1)} %get-tuple-element.376, f32[8,256]{1,0:T(8,128)S(1)} %log_add_fusion.2, pred[256,768]{0,1:T(8,128)(4,1)S(1)} %fusion.65, bf16[256,8,128]{0,2,1:T(8,128)(2,1)S(1)} %bitcast.140, ...), kind=kOutput, calls=%fused_computation.3.clone.1 | convolution fusion | flops 412090368 | bytes 10371076 | tf_op jit(solution)/shard_map/while/body/eval_jaxpr/ihd,jd->hij/dot_general | solution.py:68
  124.0 1.5 fusion.69
  125.6 1.8 %fusion.70 = f32[768,512]{1,0:T(8,128)} fusion(f32[768,512]{1,0:T(8,128)} %get-tuple-element.401, s32[]{:T(128)S(6)} %select_n.77, bf16[8,256,768]{1,2,0:T(8,128)(2,1)S(1)} %fusion.68, bf16[256,8,128]{0,2,1:T(8,128)(2,1)S(1)} %bitcast.134), kind=kOutput, calls=%fused_computation.15.clone.1 | convolution fusion | flops 402653184 | bytes 4063236 | tf_op jit(solution)/shard_map/while/body/eval_jaxpr/hij,ihd->jd/dot_general | solution.py:79
  133.7 27.0 %collective-permute-done.3 = bf16[2,256,512]{2,1,0:T(8,128)(2,1)S(1)} collective-permute-done((bf16[2,256,512]{2,1,0:T(8,128)(2,1)S(1)}, bf16[2,256,512]{2,1,0:T(8,128)(2,1)S(1)}, u32[]{:S(2)}, u32[]{:S(2)}) %collective-permute-start.3) | collective-permute-done | bytes 524320 | tf_op jit(solution)/shard_map/ppermute | solution.py:14
  (113 shorter events, 45.8 us)
Async XLA Ops:
  0.6 20.4 %copy-start.5 = (bf16[256,512]{1,0:T(8,128)(2,1)S(1)}, bf16[256,512]{1,0:T(8,128)(2,1)}, u32[]{:S(2)}) copy-start(bf16[256,512]{1,0:T(8,128)(2,1)} %param.8) | copy-start | bytes 786436
  0.6 20.4 %copy-start.4 = (bf16[256,512]{1,0:T(8,128)(2,1)S(1)}, bf16[256,512]{1,0:T(8,128)(2,1)}, u32[]{:S(2)}) copy-start(bf16[256,512]{1,0:T(8,128)(2,1)} %param.9) | copy-start | bytes 786436
  1.8 8.0 %collective-permute-start.1 = (bf16[2,256,512]{2,1,0:T(8,128)(2,1)S(1)}, bf16[2,256,512]{2,1,0:T(8,128)(2,1)S(1)}, u32[]{:S(2)}, u32[]{:S(2)}) collective-permute-start(bf16[2,256,512]{2,1,0:T(8,128)(2,1)S(1)} %pad_maximum_fusion.3), channel_id=1, source_target_pairs={{0,1},{1,2},{2,3},{3,4},{4,5},{5,6},{6,7},{7,8},{8,9},{9,10},{10,1... | collective-permute-start | bytes 1572872 | tf_op jit(solution)/shard_map/ppermute | solution.py:14
  4.2 16.8 %collective-permute-start = (bf16[2,256,512]{2,1,0:T(8,128)(2,1)S(1)}, bf16[2,256,512]{2,1,0:T(8,128)(2,1)S(1)}, u32[]{:S(2)}, u32[]{:S(2)}) collective-permute-start(bf16[2,256,512]{2,1,0:T(8,128)(2,1)S(1)} %pad_maximum_fusion.3), channel_id=1, source_target_pairs={{0,2},{1,3},{2,4},{3,5},{4,6},{5,7},{6,8},{7,9},{8,10},{9,11},{10,... | collective-permute-start | bytes 1572872 | tf_op jit(solution)/shard_map/ppermute | solution.py:14
  29.7 9.5 %copy-start.2 = (bf16[256,1024]{0,1:T(8,128)(2,1)}, bf16[256,1024]{0,1:T(8,128)(2,1)S(1)}, u32[]{:S(2)}) copy-start(bf16[256,1024]{0,1:T(8,128)(2,1)S(1)} %copy.74) | copy-start | bytes 1572868 | tf_op jit(solution)/shard_map/while
  33.1 2.7 %copy-start = (f32[768,256,8]{1,0,2:T(8,128)}, f32[768,256,8]{1,0,2:T(8,128)S(1)}, u32[]{:S(2)}) copy-start(f32[768,256,8]{1,0,2:T(8,128)S(1)} %get-tuple-element.374) | copy-start | bytes 18874372 | tf_op jit(solution)/shard_map/while
  39.2 6.7 %slice-start = ((s8[6291456]{0:T(1024)(128)(4,1)}), s8[2097152]{0:T(1024)(128)(4,1)S(1)}, s32[]{:S(2)}) async-start(s8[6291456]{0:T(1024)(128)(4,1)} %bitcast.131), calls=%async_computation | async-start | bytes 4194304 | tf_op jit(solution)/shard_map/while
  40.6 5.3 %slice-start.1 = ((s8[6291456]{0:T(1024)(128)(4,1)}), s8[4194304]{0:T(1024)(128)(4,1)S(1)}, s32[]{:S(2)}) async-start(s8[6291456]{0:T(1024)(128)(4,1)} %bitcast.131), calls=%async_computation.1 | async-start | bytes 8388608 | tf_op jit(solution)/shard_map/while
  40.6 5.3 %copy-start.3 = (bf16[256,1024]{0,1:T(8,128)(2,1)S(1)}, bf16[256,1024]{0,1:T(8,128)(2,1)}, u32[]{:S(2)}) copy-start(bf16[256,1024]{0,1:T(8,128)(2,1)} %copy-done.2) | copy-start | bytes 1572868 | tf_op jit(solution)/shard_map/while
  54.8 9.5 %copy-start.2 = (bf16[256,1024]{0,1:T(8,128)(2,1)}, bf16[256,1024]{0,1:T(8,128)(2,1)S(1)}, u32[]{:S(2)}) copy-start(bf16[256,1024]{0,1:T(8,128)(2,1)S(1)} %copy.74) | copy-start | bytes 1572868 | tf_op jit(solution)/shard_map/while
  58.2 2.7 %copy-start = (f32[768,256,8]{1,0,2:T(8,128)}, f32[768,256,8]{1,0,2:T(8,128)S(1)}, u32[]{:S(2)}) copy-start(f32[768,256,8]{1,0,2:T(8,128)S(1)} %get-tuple-element.374) | copy-start | bytes 18874372 | tf_op jit(solution)/shard_map/while
  64.3 6.7 %slice-start = ((s8[6291456]{0:T(1024)(128)(4,1)}), s8[2097152]{0:T(1024)(128)(4,1)S(1)}, s32[]{:S(2)}) async-start(s8[6291456]{0:T(1024)(128)(4,1)} %bitcast.131), calls=%async_computation | async-start | bytes 4194304 | tf_op jit(solution)/shard_map/while
  65.7 5.3 %slice-start.1 = ((s8[6291456]{0:T(1024)(128)(4,1)}), s8[4194304]{0:T(1024)(128)(4,1)S(1)}, s32[]{:S(2)}) async-start(s8[6291456]{0:T(1024)(128)(4,1)} %bitcast.131), calls=%async_computation.1 | async-start | bytes 8388608 | tf_op jit(solution)/shard_map/while
  65.7 5.2 %copy-start.3 = (bf16[256,1024]{0,1:T(8,128)(2,1)S(1)}, bf16[256,1024]{0,1:T(8,128)(2,1)}, u32[]{:S(2)}) copy-start(bf16[256,1024]{0,1:T(8,128)(2,1)} %copy-done.2) | copy-start | bytes 1572868 | tf_op jit(solution)/shard_map/while
  79.8 9.5 %copy-start.2 = (bf16[256,1024]{0,1:T(8,128)(2,1)}, bf16[256,1024]{0,1:T(8,128)(2,1)S(1)}, u32[]{:S(2)}) copy-start(bf16[256,1024]{0,1:T(8,128)(2,1)S(1)} %copy.74) | copy-start | bytes 1572868 | tf_op jit(solution)/shard_map/while
  83.3 2.7 %copy-start = (f32[768,256,8]{1,0,2:T(8,128)}, f32[768,256,8]{1,0,2:T(8,128)S(1)}, u32[]{:S(2)}) copy-start(f32[768,256,8]{1,0,2:T(8,128)S(1)} %get-tuple-element.374) | copy-start | bytes 18874372 | tf_op jit(solution)/shard_map/while
  89.4 6.7 %slice-start = ((s8[6291456]{0:T(1024)(128)(4,1)}), s8[2097152]{0:T(1024)(128)(4,1)S(1)}, s32[]{:S(2)}) async-start(s8[6291456]{0:T(1024)(128)(4,1)} %bitcast.131), calls=%async_computation | async-start | bytes 4194304 | tf_op jit(solution)/shard_map/while
  90.8 5.3 %slice-start.1 = ((s8[6291456]{0:T(1024)(128)(4,1)}), s8[4194304]{0:T(1024)(128)(4,1)S(1)}, s32[]{:S(2)}) async-start(s8[6291456]{0:T(1024)(128)(4,1)} %bitcast.131), calls=%async_computation.1 | async-start | bytes 8388608 | tf_op jit(solution)/shard_map/while
  90.8 5.3 %copy-start.3 = (bf16[256,1024]{0,1:T(8,128)(2,1)S(1)}, bf16[256,1024]{0,1:T(8,128)(2,1)}, u32[]{:S(2)}) copy-start(bf16[256,1024]{0,1:T(8,128)(2,1)} %copy-done.2) | copy-start | bytes 1572868 | tf_op jit(solution)/shard_map/while
  105.0 9.5 %copy-start.2 = (bf16[256,1024]{0,1:T(8,128)(2,1)}, bf16[256,1024]{0,1:T(8,128)(2,1)S(1)}, u32[]{:S(2)}) copy-start(bf16[256,1024]{0,1:T(8,128)(2,1)S(1)} %copy.74) | copy-start | bytes 1572868 | tf_op jit(solution)/shard_map/while
  108.4 2.7 %copy-start = (f32[768,256,8]{1,0,2:T(8,128)}, f32[768,256,8]{1,0,2:T(8,128)S(1)}, u32[]{:S(2)}) copy-start(f32[768,256,8]{1,0,2:T(8,128)S(1)} %get-tuple-element.374) | copy-start | bytes 18874372 | tf_op jit(solution)/shard_map/while
  114.5 6.7 %slice-start = ((s8[6291456]{0:T(1024)(128)(4,1)}), s8[2097152]{0:T(1024)(128)(4,1)S(1)}, s32[]{:S(2)}) async-start(s8[6291456]{0:T(1024)(128)(4,1)} %bitcast.131), calls=%async_computation | async-start | bytes 4194304 | tf_op jit(solution)/shard_map/while
  115.9 5.3 %slice-start.1 = ((s8[6291456]{0:T(1024)(128)(4,1)}), s8[4194304]{0:T(1024)(128)(4,1)S(1)}, s32[]{:S(2)}) async-start(s8[6291456]{0:T(1024)(128)(4,1)} %bitcast.131), calls=%async_computation.1 | async-start | bytes 8388608 | tf_op jit(solution)/shard_map/while
  115.9 5.3 %copy-start.3 = (bf16[256,1024]{0,1:T(8,128)(2,1)S(1)}, bf16[256,1024]{0,1:T(8,128)(2,1)}, u32[]{:S(2)}) copy-start(bf16[256,1024]{0,1:T(8,128)(2,1)} %copy-done.2) | copy-start | bytes 1572868 | tf_op jit(solution)/shard_map/while
  128.6 2.7 %copy-start.1 = (f32[768,512]{1,0:T(8,128)S(1)}, f32[768,512]{1,0:T(8,128)}, u32[]{:S(2)}) copy-start(f32[768,512]{1,0:T(8,128)} %get-tuple-element.179) | copy-start | bytes 4718596
  130.0 30.7 %collective-permute-start.2 = (f32[2,256,512]{2,1,0:T(8,128)S(1)}, f32[2,256,512]{2,1,0:T(8,128)S(1)}, u32[]{:S(2)}, u32[]{:S(2)}) collective-permute-start(f32[2,256,512]{2,1,0:T(8,128)S(1)} %fusion.26), channel_id=1, source_target_pairs={{1,0},{2,1},{3,2},{4,3},{5,4},{6,5},{7,6},{8,7},{9,8},{10,9},{11,1... | collective-permute-start | bytes 3145736 | tf_op jit(solution)/shard_map/ppermute | solution.py:14
  132.4 28.3 %collective-permute-start.3 = (bf16[2,256,512]{2,1,0:T(8,128)(2,1)S(1)}, bf16[2,256,512]{2,1,0:T(8,128)(2,1)S(1)}, u32[]{:S(2)}, u32[]{:S(2)}) collective-permute-start(bf16[2,256,512]{2,1,0:T(8,128)(2,1)S(1)} %fusion.30), channel_id=1, source_target_pairs={{2,0},{3,1},{4,2},{5,3},{6,4},{7,5},{8,6},{9,7},{10,8},{11,9},{12,... | collective-permute-start | bytes 1572872 | tf_op jit(solution)/shard_map/ppermute | solution.py:14
where the time goes:
time: 165 us; the launch traced here: 164 us
  matrix products  67 us (41%)
  waiting for transfers between devices  38.1 us (23%)
  local copies, waits for them, and re-layouts  34.4 us (21%)
  other arithmetic  13.3 us (8%)
  starting transfers between devices  9.41 us (6%)
    ppermute x4, waiting for transfers between devices, shifted(): lax.ppermute(value, axis, [(source, source + steps) for source in range(l...  38.1 us
    dot_general x4, matrix products, one_group(): jnp.einsum('hij,ihd->jd', weights, grad_group, preferred_element_type=jnp...  21 us
    dot_general x4, matrix products, one_group(): jnp.einsum('hij,jd->ihd', weights, value_group, preferred_element_type=jn...  13.6 us
    dot_general x4, matrix products, one_group(): jnp.einsum('ihd,jd->hij', grad_group, value_group, preferred_element_type...  11.3 us
    ppermute x4, starting transfers between devices, shifted(): lax.ppermute(value, axis, [(source, source + steps) for source in range(l...  9.41 us
    dot_general x4, matrix products, one_group(): jnp.einsum('ihd,jd->hij', query_group, key_group, preferred_element_type=...  7.86 us
    dot_general x4, matrix products, one_group(): jnp.einsum('hij,ihd->jd', grad_scores, query_group, preferred_element_typ...  7.04 us
    another operation x5, local copies, waits for them, and re-layouts  6.61 us
  transfers between devices with their start and end apart: 4, of which 2 were waited for; matrix products, arithmetic and copies ran while one was open for 1% of the time, Pallas kernels for 0%

commit v1 on v0

v1 whole, which is shorter than its diff:
```python
import functools
import math

import jax
import jax.numpy as jnp
from jax import lax
from jax.experimental import pallas as pl
from jax.experimental.pallas import tpu as pltpu
from jax.sharding import PartitionSpec as P

HEAD_DIM = 128
TILE = 128
HEADS_AT_ONCE = 4
CHUNKS = 2
NT = (((1,), (1,)), ((), ()))
NN = (((1,), (0,)), ((), ()))
TN = (((0,), (0,)), ((), ()))
FACTOR = 1.0 / math.sqrt(HEAD_DIM)
FACTOR2 = math.log2(math.e) / math.sqrt(HEAD_DIM)
NEVER = -1e30


def matmul(left, right, dims):
    return lax.dot_general(left, right, dims, preferred_element_type=jnp.float32)


def permuted(value, pairs):
    return lax.ppermute(value, "seq", pairs)


def attention_kernel(count, aliased, lengths_ref, first_ref, *refs):
    refs = refs[2:] if aliased else refs
    (q_ref, do_ref, far_k, near_k, own_k, far_v, near_v, own_v) = refs[:8]
    o_ref, dq_ref, back_ref, dk_ref, dv_ref, k_all, v_all, bias, dk_sum, dv_sum = refs[8:]
    rows = q_ref.shape[0]
    heads = q_ref.shape[1] // HEAD_DIM
    tiles = rows // TILE
    band = 2 * rows + TILE
    per_call = min(HEADS_AT_ONCE, heads)
    for place, (k_ref, v_ref) in enumerate(((far_k, far_v), (near_k, near_v), (own_k, own_v))):
        k_all[place * rows : (place + 1) * rows] = k_ref[...]
        v_all[place * rows : (place + 1) * rows] = v_ref[...]

    @pl.when(pl.program_id(0) == 0)
    def _():
        row = lax.broadcasted_iota(jnp.int32, (rows, 1), 0)

        def one(index, carry):
            begin, start = carry
            return begin + lengths_ref[index], jnp.where(row >= begin, begin, start)

        _, start = lax.fori_loop(
            0, count, one, (-first_ref[0], jnp.full((rows, 1), -4 * rows, jnp.int32))
        )
        for tile in range(tiles):
            here = slice(tile * TILE, (tile + 1) * TILE)
            key = lax.broadcasted_iota(jnp.int32, (TILE, band), 1) + (tile * TILE - 2 * rows)
            allowed = (key >= start[here]) & (key <= row[here])
            bias[tile] = jnp.where(allowed, 0.0, NEVER)

    dk_sum[...] = jnp.zeros_like(dk_sum)
    dv_sum[...] = jnp.zeros_like(dv_sum)
    for tile in range(tiles):
        here = slice(tile * TILE, (tile + 1) * TILE)
        keys = slice(tile * TILE, tile * TILE + band)
        k = k_all[keys]
        v = v_all[keys]
        for first in range(0, heads, per_call):
            cols = [slice((first + x) * HEAD_DIM, (first + x + 1) * HEAD_DIM) for x in range(per_call)]
            q = jnp.concatenate([q_ref[here, c] for c in cols], 0)
            do = jnp.concatenate([do_ref[here, c] for c in cols], 0)
            s = matmul(q, k, NT).reshape(per_call, TILE, band)
            s = (s * FACTOR2 + bias[tile][None]).reshape(per_call * TILE, band)
            e = jnp.exp2(s - jnp.max(s, 1, keepdims=True))
            prob = e * (1.0 / jnp.sum(e, 1, keepdims=True))
            weight = prob.astype(jnp.bfloat16)
            out = matmul(weight, v, NN).astype(jnp.bfloat16)
            dp = matmul(do, v, NT)
            delta = jnp.sum(out.astype(jnp.float32) * do.astype(jnp.float32), 1, keepdims=True)
            ds = (prob * (dp - delta)).astype(jnp.bfloat16)
            dq = (matmul(ds, k, NN) * FACTOR).astype(jnp.bfloat16)
            for x, c in enumerate(cols):
                o_ref[here, c] = out[x * TILE : (x + 1) * TILE]
                dq_ref[here, c] = dq[x * TILE : (x + 1) * TILE]
            dv_sum[keys] += matmul(weight, do, TN)
            dk_sum[keys] += matmul(ds, q, TN)
    dk_ref[...] = dk_sum[2 * rows :] * FACTOR
    dv_ref[...] = dv_sum[2 * rows :]
    for place in range(2):
        span = slice(place * rows, (place + 1) * rows)
        back_ref[place, 0] = (dk_sum[span] * FACTOR).astype(jnp.bfloat16)
        back_ref[place, 1] = dv_sum[span].astype(jnp.bfloat16)


def attention(chunk, groups, lengths, first, q, do, far, near, own_k, own_v, carried):
    rows, width = q.shape
    head_cols = width // (own_k.shape[1] // HEAD_DIM)
    base = chunk * groups
    kv = pl.BlockSpec((rows, HEAD_DIM), lambda g: (0, base + g))
    wide = pl.BlockSpec((rows, head_cols), lambda g: (0, base + g))
    sent_k = pl.BlockSpec((rows, HEAD_DIM), lambda g: (0, g))
    sent_v = pl.BlockSpec((rows, HEAD_DIM), lambda g: (0, groups + g))
    part = pl.BlockSpec((rows, HEAD_DIM), lambda g: (0, g))
    smem = pl.BlockSpec(memory_space=pltpu.SMEM)
    kept = pl.BlockSpec(memory_space=pl.ANY)
    aliased = carried is not None
    carried = carried if aliased else ()
    return pl.pallas_call(
        functools.partial(attention_kernel, lengths.shape[0], aliased),
        grid=(groups,),
        in_specs=[smem, smem] + [kept] * len(carried) + [wide, wide, sent_k, sent_k, kv, sent_v, sent_v, kv],
        out_specs=[
            wide,
            wide,
            pl.BlockSpec((2, 2, rows, HEAD_DIM), lambda g: (0, 0, 0, g)),
            part,
            part,
        ],
        out_shape=[
            jax.ShapeDtypeStruct(q.shape, jnp.bfloat16),
            jax.ShapeDtypeStruct(q.shape, jnp.bfloat16),
            jax.ShapeDtypeStruct((2, 2, rows, groups * HEAD_DIM), jnp.bfloat16),
            jax.ShapeDtypeStruct((rows, groups * HEAD_DIM), jnp.float32),
            jax.ShapeDtypeStruct((rows, groups * HEAD_DIM), jnp.float32),
        ],
        scratch_shapes=[
            pltpu.VMEM((3 * rows, HEAD_DIM), jnp.bfloat16),
            pltpu.VMEM((3 * rows, HEAD_DIM), jnp.bfloat16),
            pltpu.VMEM((rows // TILE, TILE, 2 * rows + TILE), jnp.float32),
            pltpu.VMEM((3 * rows, HEAD_DIM), jnp.float32),
            pltpu.VMEM((3 * rows, HEAD_DIM), jnp.float32),
        ],
        input_output_aliases={2: 0, 3: 1} if aliased else {},
        compiler_params=pltpu.CompilerParams(vmem_limit_bytes=48 * 1024 * 1024),
        cost_estimate=pl.CostEstimate(
            flops=12 * rows * 3 * rows * head_cols * groups,
            bytes_accessed=8 * rows * head_cols * groups,
            transcendentals=0,
        ),
        name="attention",
    )(lengths, first, *carried, q, do, far, near, own_k, far, near, own_v)


def on_device(queries, keys, values, grad_out, episode_lengths):
    rows = queries.shape[0]
    groups = keys.shape[1] // HEAD_DIM
    count = lax.axis_size("seq")
    place = lax.axis_index("seq")
    odd = place % 2 == 1
    first = jnp.reshape(place * rows, (1,)).astype(jnp.int32)
    ahead = [(source, source + 2) for source in range(count - 2)]
    behind = [(source + 2, source) for source in range(count - 2)]
    swap = [(source, source ^ 1) for source in range(count)]
    chunks = CHUNKS if groups % CHUNKS == 0 else 1
    per_chunk = groups // chunks
    cols = per_chunk * HEAD_DIM

    own = []
    for chunk in range(chunks):
        span = slice(chunk * cols, (chunk + 1) * cols)
        own.append(jnp.concatenate([keys[:, span], values[:, span]], axis=1))
    far = [permuted(block, ahead) for block in own]
    carried = None
    grads = []
    for chunk in range(chunks):
        near = permuted(jnp.where(odd, far[chunk], own[chunk]), swap)
        attn_out, grad_queries, back, dk, dv = attention(
            chunk, per_chunk, episode_lengths, first, queries, grad_out, far[chunk], near, keys, values, carried
        )
        carried = (attn_out, grad_queries)
        beside = permuted(back[1], swap)
        zero = jnp.zeros_like(beside)
        onward = back[0].astype(jnp.float32) + jnp.where(odd, beside, zero).astype(jnp.float32)
        returned = permuted(onward.astype(jnp.bfloat16), behind)
        extra = returned.astype(jnp.float32) + jnp.where(odd, zero, beside).astype(jnp.float32)
        grads.append(((dk + extra[0]).astype(jnp.bfloat16), (dv + extra[1]).astype(jnp.bfloat16)))
    grad_keys = jnp.concatenate([pair[0] for pair in grads], axis=1)
    grad_values = jnp.concatenate([pair[1] for pair in grads], axis=1)
    return (attn_out, grad_queries, grad_keys, grad_values)


def solution(mesh):
    split = P(("groups", "seq"), None)
    return jax.shard_map(
        on_device,
        mesh=mesh,
        in_specs=(split, split, split, split, P("groups")),
        out_specs=(split, split, split, split),
        check_vma=False,
    )
```

time: 165 us -> 67.6 us (0.41)
  matrix products: 67 us -> 0 us
  local copies, waits for them, and re-layouts: 34.4 us -> 1.34 us
  Pallas kernels: 0 us -> 28 us
  waiting for transfers between devices: 38.1 us -> 20.5 us
  other arithmetic: 13.3 us -> 5.1 us
  starting transfers between devices: 9.41 us -> 11.6 us
    dot_general x24 -> x0, matrix products: 67 us -> none  [the longest x4 21 us: one_group(): jnp.einsum('hij,ihd->jd', weights, grad_group, preferred_element_type=jnp...]
    pallas_call x0 -> x2, Pallas kernels: none -> 28 us  [attention(): pl.pallas_call(functools.partial(attention_kernel, lengths.shape[0], alia...]
    ppermute x4 -> x8, waiting for transfers between devices: 38.1 us -> 20.5 us  [permuted(): return lax.ppermute(value, 'seq', pairs)]
    dynamic_slice x16 -> x0, local copies, waits for them, and re-layouts: 11.1 us -> none  [the longest x8 5.9 us: one_group(): lax.dynamic_slice_in_dim(queries, group_index * head_cols, head_cols, 1)]
    dynamic_update_slice x12 -> x0, local copies, waits for them, and re-layouts: 10.6 us -> none  [the longest x4 5.58 us: one_group(): lax.dynamic_update_slice_in_dim(attended_all, out_group.reshape(row_count...]
    another operation x5 -> x0, local copies, waits for them, and re-layouts: 6.61 us -> none
    while x40 -> x0, local copies, waits for them, and re-layouts: 5.4 us -> none
    reduce_sum x6 -> x0, other arithmetic: 5.34 us -> none  [the longest x4 5.16 us: one_group(): jnp.sum(jnp.exp(masked - row_max), axis=2, keepdims=True)]
  transfers between devices with their start and end apart: 4 -> 8, of which waited for: 2 -> 5; matrix products, arithmetic and copies ran while one was open for 1% -> 4% of each run, Pallas kernels for 0% -> 42%
where the time goes in v1:
time: 67.6 us; the launch traced here: 67.4 us
  Pallas kernels  28 us (41%)
  waiting for transfers between devices  20.5 us (30%)
  starting transfers between devices  11.6 us (17%)
  other arithmetic  5.1 us (8%)
  local copies, waits for them, and re-layouts  1.34 us (2%)
  between operations  0.82 us (1%)
    pallas_call x2, Pallas kernels, attention(): pl.pallas_call(functools.partial(attention_kernel, lengths.shape[0], alia...  28 us
    ppermute x8, waiting for transfers between devices, permuted(): return lax.ppermute(value, 'seq', pairs)  20.5 us
    ppermute x8, starting transfers between devices, permuted(): return lax.ppermute(value, 'seq', pairs)  11.6 us
    select_n x2, other arithmetic, on_device(): near = permuted(jnp.where(odd, far[chunk], own[chunk]), swap)  1.74 us
    concatenate x2, other arithmetic, on_device(): own.append(jnp.concatenate([keys[:, span], values[:, span]], axis=1))  1.46 us
  transfers between devices with their start and end apart: 8, of which 5 were waited for; matrix products, arithmetic and copies ran while one was open for 4% of the time, Pallas kernels for 42%

profile of v1, /device:TPU:0, one launch (start us, length us, event | category | flops | bytes accessed | tf_op | source)
XLA Modules:
  0.0 67.4 jit_solution(15559378986995184668)
XLA Ops:
  0.7 1.3 %fusion.10 = (bf16[256,256]{1,0:T(8,128)(2,1)S(1)}, bf16[256,256]{1,0:T(8,128)(2,1)S(1)}, bf16[256,256]{1,0:T(8,128)(2,1)S(1)}, bf16[256,256]{1,0:T(8,128)(2,1)S(1)}) fusion(bf16[256,512]{1,0:T(8,128)(2,1)} %refs_6_.1, bf16[256,512]{1,0:T(8,128)(2,1)} %refs_9_.1), kind=kLoop, calls=%fused_computation.26 | loop fusion | bytes 1048576 | tf_op jit(solution)/shard_map/slice | solution.py:161
  2.0 0.0 copy-start.4
  2.0 0.7 %pad_maximum_fusion = bf16[256,512]{1,0:T(8,128)(2,1)} fusion(bf16[256,256]{1,0:T(8,128)(2,1)S(1)} %get-tuple-element.32, bf16[256,256]{1,0:T(8,128)(2,1)S(1)} %get-tuple-element.29), kind=kLoop, calls=%fused_computation.18 | loop fusion | flops 524288 | bytes 524288 | tf_op jit(solution)/shard_map/concatenate | solution.py:161
  2.7 4.9 %collective-permute-start = (bf16[256,512]{1,0:T(8,128)(2,1)}, bf16[256,512]{1,0:T(8,128)(2,1)S(1)}, u32[]{:S(2)}, u32[]{:S(2)}) collective-permute-start(bf16[256,512]{1,0:T(8,128)(2,1)} %pad_maximum_fusion), channel_id=1, source_target_pairs={{0,2},{1,3},{2,4},{3,5},{4,6},{5,7},{6,8},{7,9},{8,10},{9,11},{10,... | collective-permute-start | bytes 786440 | tf_op jit(solution)/shard_map/ppermute | solution.py:28
  7.6 0.7 %pad_maximum_fusion.1 = bf16[256,512]{1,0:T(8,128)(2,1)} fusion(bf16[256,256]{1,0:T(8,128)(2,1)S(1)} %get-tuple-element.33, bf16[256,256]{1,0:T(8,128)(2,1)S(1)} %get-tuple-element.28), kind=kLoop, calls=%fused_computation.19 | loop fusion | flops 524288 | bytes 524288 | tf_op jit(solution)/shard_map/concatenate | solution.py:161
  8.3 3.4 %collective-permute-start.2 = (bf16[256,512]{1,0:T(8,128)(2,1)}, bf16[256,512]{1,0:T(8,128)(2,1)S(1)}, u32[]{:S(2)}, u32[]{:S(2)}) collective-permute-start(bf16[256,512]{1,0:T(8,128)(2,1)} %pad_maximum_fusion.1), channel_id=1, source_target_pairs={{0,2},{1,3},{2,4},{3,5},{4,6},{5,7},{6,8},{7,9},{8,10},{9,11},{10,... | collective-permute-start | bytes 786440 | tf_op jit(solution)/shard_map/ppermute | solution.py:28
  11.8 2.8 %collective-permute-done.refs_2_.refs_5_ = bf16[256,512]{1,0:T(8,128)(2,1)S(1)} collective-permute-done((bf16[256,512]{1,0:T(8,128)(2,1)}, bf16[256,512]{1,0:T(8,128)(2,1)S(1)}, u32[]{:S(2)}, u32[]{:S(2)}) %collective-permute-start) | collective-permute-done | bytes 262176 | tf_op jit(solution)/shard_map/ppermute | solution.py:28
  14.6 0.8 %broadcast_select_fusion.1 = bf16[256,512]{1,0:T(8,128)(2,1)} fusion(bf16[256,512]{1,0:T(8,128)(2,1)S(1)} %collective-permute-done.refs_2_.refs_5_, pred[]{:T(512)S(6)} %eq.5, bf16[256,256]{1,0:T(8,128)(2,1)S(1)} %get-tuple-element.32, bf16[256,256]{1,0:T(8,128)(2,1)S(1)} %get-tuple-element.29), kind=kLoop, calls=%fused_computation.25 | loop fusion | flops 655360 | bytes 786433 | tf_op jit(solution)/shard_map/jit(_where)/select_n | solution.py:166
  15.3 0.0 collective-permute-start.1
  15.3 3.7 %collective-permute-done.2.refs_4_.refs_7_ = bf16[256,512]{1,0:T(8,128)(2,1)S(1)} collective-permute-done((bf16[256,512]{1,0:T(8,128)(2,1)}, bf16[256,512]{1,0:T(8,128)(2,1)S(1)}, u32[]{:S(2)}, u32[]{:S(2)}) %collective-permute-start.2) | collective-permute-done | bytes 262176 | tf_op jit(solution)/shard_map/ppermute | solution.py:28
  19.1 1.0 %broadcast_select_fusion = bf16[256,512]{1,0:T(8,128)(2,1)S(1)} fusion(bf16[256,512]{1,0:T(8,128)(2,1)S(1)} %collective-permute-done.2.refs_4_.refs_7_, pred[]{:T(512)S(6)} %eq.5, bf16[256,256]{1,0:T(8,128)(2,1)} %copy-done.4, bf16[256,256]{1,0:T(8,128)(2,1)S(1)} %get-tuple-element.28), kind=kLoop, calls=%fused_computation.24 | loop fusion | flops 655360 | bytes 786433 | tf_op jit(solution)/shard_map/jit(_where)/select_n | solution.py:166
  20.0 0.1 collective-permute-start.3
  20.1 0.0 collective-permute-done.1.refs_3_.refs_6_
  20.2 14.0 %attention.2 = (bf16[256,4096]{1,0:T(8,128)(2,1)}, bf16[256,4096]{1,0:T(8,128)(2,1)}, bf16[2,2,256,256]{3,2,1,0:T(8,128)(2,1)S(1)}, f32[256,256]{1,0:T(8,128)S(1)}, f32[256,256]{1,0:T(8,128)S(1)}) custom-call(s32[16]{0:T(128)S(1)} %copy-done.3, s32[1]{0:T(128)} %bitcast.first_ref, bf16[256,4096]{1,0:T(8,128)(2,1)S(1)} %copy-done.2, ...), custom_call_target="tpu_custom_call" | custom-call | flops 4831838208 | bytes 4194304 | tf_op jit(solution)/shard_map/attention/pallas_call | solution.py:108
  34.2 0.5 collective-permute-start.4
  34.7 0.0 collective-permute-done.3.refs_5_.refs_8_
  34.7 14.0 %attention.3 = (bf16[256,4096]{1,0:T(8,128)(2,1)}, bf16[256,4096]{1,0:T(8,128)(2,1)}, bf16[2,2,256,256]{3,2,1,0:T(8,128)(2,1)S(1)}, f32[256,256]{1,0:T(8,128)S(1)}, f32[256,256]{1,0:T(8,128)S(1)}) custom-call(s32[16]{0:T(128)S(1)} %copy-done.3, s32[1]{0:T(128)} %bitcast.first_ref, ...), custom_call_target="tpu_custom_call", output_to_operand_aliasing={{0}: (2, {}), {1}: (3, {})} | custom-call | flops 4831838208 | bytes 4194304 | tf_op jit(solution)/shard_map/attention/pallas_call | solution.py:108
  48.8 0.1 collective-permute-start.6
  48.9 0.0 collective-permute-done.4
  48.9 0.1 fusion.1
  49.0 1.3 %collective-permute-start.5 = (bf16[2,256,256]{2,1,0:T(8,128)(2,1)S(1)}, bf16[2,256,256]{2,1,0:T(8,128)(2,1)S(1)}, u32[]{:S(2)}, u32[]{:S(2)}) collective-permute-start(bf16[2,256,256]{2,1,0:T(8,128)(2,1)S(1)} %fusion.1), channel_id=1, source_target_pairs={{2,0},{3,1},{4,2},{5,3},{6,4},{7,5},{8,6},{9,7},{10,8},{11,9},{12,... | collective-permute-start | bytes 786440 | tf_op jit(solution)/shard_map/ppermute | solution.py:28
  50.3 0.1 collective-permute-done.6
  50.4 0.1 fusion
  50.4 1.3 %collective-permute-start.7 = (bf16[2,256,256]{2,1,0:T(8,128)(2,1)S(1)}, bf16[2,256,256]{2,1,0:T(8,128)(2,1)S(1)}, u32[]{:S(2)}, u32[]{:S(2)}) collective-permute-start(bf16[2,256,256]{2,1,0:T(8,128)(2,1)S(1)} %fusion), channel_id=1, source_target_pairs={{2,0},{3,1},{4,2},{5,3},{6,4},{7,5},{8,6},{9,7},{10,8},{11,9},{12,... | collective-permute-start | bytes 786440 | tf_op jit(solution)/shard_map/ppermute | solution.py:28
  51.7 8.7 %collective-permute-done.5 = bf16[2,256,256]{2,1,0:T(8,128)(2,1)S(1)} collective-permute-done((bf16[2,256,256]{2,1,0:T(8,128)(2,1)S(1)}, bf16[2,256,256]{2,1,0:T(8,128)(2,1)S(1)}, u32[]{:S(2)}, u32[]{:S(2)}) %collective-permute-start.5) | collective-permute-done | bytes 262176 | tf_op jit(solution)/shard_map/ppermute | solution.py:28
  60.4 0.1 convert_add_fusion.3
  60.5 0.1 fusion.5
  60.6 5.2 %collective-permute-done.7 = bf16[2,256,256]{2,1,0:T(8,128)(2,1)S(1)} collective-permute-done((bf16[2,256,256]{2,1,0:T(8,128)(2,1)S(1)}, bf16[2,256,256]{2,1,0:T(8,128)(2,1)S(1)}, u32[]{:S(2)}, u32[]{:S(2)}) %collective-permute-start.7) | collective-permute-done | bytes 262176 | tf_op jit(solution)/shard_map/ppermute | solution.py:28
  65.8 0.1 convert_add_fusion.2
  65.9 0.1 fusion.3
  65.9 0.7 %pad_maximum_fusion.3 = bf16[256,512]{1,0:T(8,128)(2,1)} fusion(bf16[256,256]{1,0:T(8,128)(2,1)S(1)} %get-tuple-element.26, bf16[256,256]{1,0:T(8,128)(2,1)S(1)} %get-tuple-element.24), kind=kLoop, calls=%fused_computation.21 | loop fusion | flops 524288 | bytes 524288 | tf_op jit(solution)/shard_map/concatenate | solution.py:178
  66.7 0.7 %pad_maximum_fusion.2 = bf16[256,512]{1,0:T(8,128)(2,1)} fusion(bf16[256,256]{1,0:T(8,128)(2,1)S(1)} %get-tuple-element.27, bf16[256,256]{1,0:T(8,128)(2,1)S(1)} %get-tuple-element.25), kind=kLoop, calls=%fused_computation.20 | loop fusion | flops 524288 | bytes 524288 | tf_op jit(solution)/shard_map/concatenate | solution.py:177
  (11 shorter events, 0.1 us)
Async XLA Ops:
  0.6 19.5 %copy-start.1 = (bf16[256,512]{1,0:T(8,128)(2,1)S(1)}, bf16[256,512]{1,0:T(8,128)(2,1)}, u32[]{:S(2)}) copy-start(bf16[256,512]{1,0:T(8,128)(2,1)} %refs_9_.1) | copy-start | bytes 786436
  0.6 19.5 %copy-start = (bf16[256,512]{1,0:T(8,128)(2,1)S(1)}, bf16[256,512]{1,0:T(8,128)(2,1)}, u32[]{:S(2)}) copy-start(bf16[256,512]{1,0:T(8,128)(2,1)} %refs_6_.1) | copy-start | bytes 786436
  0.7 19.5 %copy-start.3 = (s32[16]{0:T(128)S(1)}, s32[16]{0:T(128)}, u32[]{:S(2)}) copy-start(s32[16]{0:T(128)} %lengths_ref.3) | copy-start | bytes 196
  0.7 19.5 %copy-start.2 = (bf16[256,4096]{1,0:T(8,128)(2,1)S(1)}, bf16[256,4096]{1,0:T(8,128)(2,1)}, u32[]{:S(2)}) copy-start(bf16[256,4096]{1,0:T(8,128)(2,1)} %refs_2_.1) | copy-start | bytes 6291460
  2.0 5.6 %copy-start.4 = (bf16[256,256]{1,0:T(8,128)(2,1)}, bf16[256,256]{1,0:T(8,128)(2,1)S(1)}, u32[]{:S(2)}) copy-start(bf16[256,256]{1,0:T(8,128)(2,1)S(1)} %get-tuple-element.33) | copy-start | bytes 393220
  2.7 11.9 %collective-permute-start = (bf16[256,512]{1,0:T(8,128)(2,1)}, bf16[256,512]{1,0:T(8,128)(2,1)S(1)}, u32[]{:S(2)}, u32[]{:S(2)}) collective-permute-start(bf16[256,512]{1,0:T(8,128)(2,1)} %pad_maximum_fusion), channel_id=1, source_target_pairs={{0,2},{1,3},{2,4},{3,5},{4,6},{5,7},{6,8},{7,9},{8,10},{9,11},{10,... | collective-permute-start | bytes 786440 | tf_op jit(solution)/shard_map/ppermute | solution.py:28
  8.3 10.7 %collective-permute-start.2 = (bf16[256,512]{1,0:T(8,128)(2,1)}, bf16[256,512]{1,0:T(8,128)(2,1)S(1)}, u32[]{:S(2)}, u32[]{:S(2)}) collective-permute-start(bf16[256,512]{1,0:T(8,128)(2,1)} %pad_maximum_fusion.1), channel_id=1, source_target_pairs={{0,2},{1,3},{2,4},{3,5},{4,6},{5,7},{6,8},{7,9},{8,10},{9,11},{10,... | collective-permute-start | bytes 786440 | tf_op jit(solution)/shard_map/ppermute | solution.py:28
  15.3 4.8 %collective-permute-start.1 = (bf16[256,512]{1,0:T(8,128)(2,1)}, bf16[256,512]{1,0:T(8,128)(2,1)S(1)}, u32[]{:S(2)}, u32[]{:S(2)}) collective-permute-start(bf16[256,512]{1,0:T(8,128)(2,1)} %broadcast_select_fusion.1), channel_id=1, source_target_pairs={{0,1},{1,0},{2,3},{3,2},{4,5},{5,4},{6,7},{7,6},{8,9},{9,8},{10,11... | collective-permute-start | bytes 786440 | tf_op jit(solution)/shard_map/ppermute | solution.py:28
  20.0 14.7 %collective-permute-start.3 = (bf16[256,512]{1,0:T(8,128)(2,1)S(1)}, bf16[256,512]{1,0:T(8,128)(2,1)S(1)}, u32[]{:S(2)}, u32[]{:S(2)}) collective-permute-start(bf16[256,512]{1,0:T(8,128)(2,1)S(1)} %broadcast_select_fusion), channel_id=1, source_target_pairs={{0,1},{1,0},{2,3},{3,2},{4,5},{5,4},{6,7},{7,6},{8,9},{9,8},{10,11... | collective-permute-start | bytes 786440 | tf_op jit(solution)/shard_map/ppermute | solution.py:28
  34.2 14.7 %collective-permute-start.4 = (bf16[2,256,256]{2,1,0:T(8,128)(2,1)S(1)}, bf16[2,256,256]{2,1,0:T(8,128)(2,1)S(1)}, u32[]{:S(2)}, u32[]{:S(2)}) collective-permute-start(bf16[2,256,256]{2,1,0:T(8,128)(2,1)S(1)} %slice_bitcast_fusion.5), channel_id=1, source_target_pairs={{0,1},{1,0},{2,3},{3,2},{4,5},{5,4},{6,7},{7,6},{8,9},{9,8},{10,11... | collective-permute-start | bytes 786440 | tf_op jit(solution)/shard_map/ppermute | solution.py:28
  48.8 1.6 %collective-permute-start.6 = (bf16[2,256,256]{2,1,0:T(8,128)(2,1)S(1)}, bf16[2,256,256]{2,1,0:T(8,128)(2,1)S(1)}, u32[]{:S(2)}, u32[]{:S(2)}) collective-permute-start(bf16[2,256,256]{2,1,0:T(8,128)(2,1)S(1)} %slice_bitcast_fusion.4), channel_id=1, source_target_pairs={{0,1},{1,0},{2,3},{3,2},{4,5},{5,4},{6,7},{7,6},{8,9},{9,8},{10,11... | collective-permute-start | bytes 786440 | tf_op jit(solution)/shard_map/ppermute | solution.py:28
  49.0 11.4 %collective-permute-start.5 = (bf16[2,256,256]{2,1,0:T(8,128)(2,1)S(1)}, bf16[2,256,256]{2,1,0:T(8,128)(2,1)S(1)}, u32[]{:S(2)}, u32[]{:S(2)}) collective-permute-start(bf16[2,256,256]{2,1,0:T(8,128)(2,1)S(1)} %fusion.1), channel_id=1, source_target_pairs={{2,0},{3,1},{4,2},{5,3},{6,4},{7,5},{8,6},{9,7},{10,8},{11,9},{12,... | collective-permute-start | bytes 786440 | tf_op jit(solution)/shard_map/ppermute | solution.py:28
  50.4 15.3 %collective-permute-start.7 = (bf16[2,256,256]{2,1,0:T(8,128)(2,1)S(1)}, bf16[2,256,256]{2,1,0:T(8,128)(2,1)S(1)}, u32[]{:S(2)}, u32[]{:S(2)}) collective-permute-start(bf16[2,256,256]{2,1,0:T(8,128)(2,1)S(1)} %fusion), channel_id=1, source_target_pairs={{2,0},{3,1},{4,2},{5,3},{6,4},{7,5},{8,6},{9,7},{10,8},{11,9},{12,... | collective-permute-start | bytes 786440 | tf_op jit(solution)/shard_map/ppermute | solution.py:28

commit v2 on v1

v2 whole, which is shorter than its diff:
```python
import functools
import math

import jax
import jax.numpy as jnp
from jax import lax
from jax.experimental import pallas as pl
from jax.experimental.pallas import tpu as pltpu
from jax.sharding import PartitionSpec as P

HEAD_DIM = 128
TILE = 128
HEADS_AT_ONCE = 4
SPLIT = (2, 2)
NT = (((1,), (1,)), ((), ()))
NN = (((1,), (0,)), ((), ()))
TN = (((0,), (0,)), ((), ()))
FACTOR = 1.0 / math.sqrt(HEAD_DIM)
FACTOR2 = math.log2(math.e) / math.sqrt(HEAD_DIM)
NEVER = -1e30
VMEM_LIMIT = 40 * 1024 * 1024
SMALL_LIMIT = 6 * 1024 * 1024


def matmul(left, right, dims):
    return lax.dot_general(left, right, dims, preferred_element_type=jnp.float32)


def permuted(value, pairs):
    return lax.ppermute(value, "seq", pairs)


def in_hbm(value):
    return pltpu.with_memory_space_constraint(value, pltpu.HBM)


def pack_kernel(starts, sizes, k_ref, v_ref, *outs):
    for out, start, size in zip(outs, starts, sizes):
        out[:, :size] = k_ref[:, start : start + size]
        out[:, size:] = v_ref[:, start : start + size]


def packed(keys, values, starts, sizes):
    rows = keys.shape[0]
    return pl.pallas_call(
        functools.partial(pack_kernel, starts, sizes),
        grid=(1,),
        in_specs=[pl.BlockSpec(keys.shape, lambda i: (0, 0))] * 2,
        out_specs=[pl.BlockSpec((rows, 2 * size), lambda i: (0, 0)) for size in sizes],
        out_shape=[jax.ShapeDtypeStruct((rows, 2 * size), keys.dtype) for size in sizes],
        compiler_params=pltpu.CompilerParams(vmem_limit_bytes=SMALL_LIMIT),
        name="pack_keys_values",
    )(keys, values)


def mask_kernel(count, lengths_ref, first_ref, bias_ref):
    tiles, _, band = bias_ref.shape
    rows = tiles * TILE
    row = lax.broadcasted_iota(jnp.int32, (rows, 1), 0)

    def one(index, carry):
        begin, start = carry
        return begin + lengths_ref[index], jnp.where(row >= begin, begin, start)

    _, start = lax.fori_loop(
        0, count, one, (-first_ref[0], jnp.full((rows, 1), -4 * rows, jnp.int32))
    )
    for tile in range(tiles):
        here = slice(tile * TILE, (tile + 1) * TILE)
        key = lax.broadcasted_iota(jnp.int32, (TILE, band), 1) + (tile * TILE - 2 * rows)
        allowed = (key >= start[here]) & (key <= row[here])
        bias_ref[tile] = jnp.where(allowed, 0.0, NEVER)


def masks(rows, lengths, first):
    smem = pl.BlockSpec(memory_space=pltpu.SMEM)
    return pl.pallas_call(
        functools.partial(mask_kernel, lengths.shape[0]),
        in_specs=[smem, smem],
        out_specs=pl.BlockSpec(memory_space=pltpu.VMEM),
        out_shape=jax.ShapeDtypeStruct((rows // TILE, TILE, 2 * rows + TILE), jnp.float32),
        compiler_params=pltpu.CompilerParams(vmem_limit_bytes=SMALL_LIMIT),
        name="masks",
    )(lengths, first)


def gather_rows(all_ref, parts):
    rows = parts[0].shape[0]
    for place, part in enumerate(parts):
        all_ref[place * rows : (place + 1) * rows] = part[...]


def unit_slices(unit, per_call, band):
    tile, first = unit
    here = slice(tile * TILE, (tile + 1) * TILE)
    keys = slice(tile * TILE, tile * TILE + band)
    cols = [slice((first + x) * HEAD_DIM, (first + x + 1) * HEAD_DIM) for x in range(per_call)]
    return here, keys, cols


def stacked(ref, here, cols):
    return jnp.concatenate([ref[here, c] for c in cols], 0)


def attention_kernel(aliased, *refs):
    refs = refs[2:] if aliased else refs
    (bias, q_ref, do_ref, far_k, near_k, own_k, far_v, near_v, own_v) = refs[:9]
    o_ref, dq_ref, back_ref, own_ref, k_all, v_all, dk_sum, dv_sum = refs[9:]
    rows = q_ref.shape[0]
    heads = q_ref.shape[1] // HEAD_DIM
    band = 2 * rows + TILE
    per_call = min(HEADS_AT_ONCE, heads)
    gather_rows(k_all, (far_k, near_k, own_k))
    gather_rows(v_all, (far_v, near_v, own_v))
    dk_sum[...] = jnp.zeros_like(dk_sum)
    dv_sum[...] = jnp.zeros_like(dv_sum)
    units = [(tile, first) for tile in range(rows // TILE) for first in range(0, heads, per_call)]

    def scores(unit):
        here, keys, cols = unit_slices(unit, per_call, band)
        return matmul(stacked(q_ref, here, cols), k_all[keys], NT)

    def softmax(unit, s):
        s = s.reshape(per_call, TILE, band) * FACTOR2 + bias[unit[0]][None]
        s = s.reshape(per_call * TILE, band)
        e = jnp.exp2(s - jnp.max(s, 1, keepdims=True))
        return e * (1.0 / jnp.sum(e, 1, keepdims=True))

    def score_grads(unit, prob, weight):
        here, keys, cols = unit_slices(unit, per_call, band)
        do = stacked(do_ref, here, cols)
        out = matmul(weight, v_all[keys], NN).astype(jnp.bfloat16)
        for x, c in enumerate(cols):
            o_ref[here, c] = out[x * TILE : (x + 1) * TILE]
        dp = matmul(do, v_all[keys], NT)
        delta = jnp.sum(out.astype(jnp.float32) * do.astype(jnp.float32), 1, keepdims=True)
        return (prob * (dp - delta)).astype(jnp.bfloat16)

    def sums(unit, weight, ds):
        here, keys, cols = unit_slices(unit, per_call, band)
        dq = (matmul(ds, k_all[keys], NN) * FACTOR).astype(jnp.bfloat16)
        for x, c in enumerate(cols):
            dq_ref[here, c] = dq[x * TILE : (x + 1) * TILE]
        dv_sum[:, keys] += matmul(stacked(do_ref, here, cols), weight, TN)
        dk_sum[:, keys] += matmul(stacked(q_ref, here, cols), ds, TN)

    ahead = scores(units[0])
    before = None
    for index, unit in enumerate(units):
        now = ahead
        if index + 1 < len(units):
            ahead = scores(units[index + 1])
        prob = softmax(unit, now)
        weight = prob.astype(jnp.bfloat16)
        if before is not None:
            sums(*before)
        before = (unit, weight, score_grads(unit, prob, weight))
    sums(*before)

    own_ref[0] = dk_sum[:, 2 * rows :].T * FACTOR
    own_ref[1] = dv_sum[:, 2 * rows :].T
    for place in range(2):
        span = slice(place * rows, (place + 1) * rows)
        back_ref[place, 0] = (dk_sum[:, span].T * FACTOR).astype(jnp.bfloat16)
        back_ref[place, 1] = dv_sum[:, span].T.astype(jnp.bfloat16)


def attention(base, groups, bias, q, do, far, near, own_k, own_v, carried):
    rows, width = q.shape
    head_cols = width // (own_k.shape[1] // HEAD_DIM)
    own = pl.BlockSpec((rows, HEAD_DIM), lambda g: (0, base + g))
    sent_k = pl.BlockSpec((rows, HEAD_DIM), lambda g: (0, g))
    sent_v = pl.BlockSpec((rows, HEAD_DIM), lambda g: (0, groups + g))
    wide = pl.BlockSpec((rows, head_cols), lambda g: (0, base + g))
    aliased = carried is not None
    carried = carried if aliased else ()
    return pl.pallas_call(
        functools.partial(attention_kernel, aliased),
        grid=(groups,),
        in_specs=[pl.BlockSpec(memory_space=pl.ANY)] * len(carried)
        + [pl.BlockSpec(bias.shape, lambda g: (0, 0, 0)), wide, wide]
        + [sent_k, sent_k, own, sent_v, sent_v, own],
        out_specs=[
            wide,
            wide,
            pl.BlockSpec((2, 2, rows, HEAD_DIM), lambda g: (0, 0, 0, g)),
            pl.BlockSpec((2, rows, HEAD_DIM), lambda g: (0, 0, g)),
        ],
        out_shape=[
            jax.ShapeDtypeStruct(q.shape, jnp.bfloat16),
            jax.ShapeDtypeStruct(q.shape, jnp.bfloat16),
            jax.ShapeDtypeStruct((2, 2, rows, groups * HEAD_DIM), jnp.bfloat16),
            jax.ShapeDtypeStruct((2, rows, groups * HEAD_DIM), jnp.float32),
        ],
        scratch_shapes=[
            pltpu.VMEM((3 * rows, HEAD_DIM), jnp.bfloat16),
            pltpu.VMEM((3 * rows, HEAD_DIM), jnp.bfloat16),
            pltpu.VMEM((HEAD_DIM, 3 * rows), jnp.float32),
            pltpu.VMEM((HEAD_DIM, 3 * rows), jnp.float32),
        ],
        input_output_aliases={0: 0, 1: 1} if aliased else {},
        compiler_params=pltpu.CompilerParams(vmem_limit_bytes=VMEM_LIMIT),
        name="attention",
    )(*carried, bias, q, do, far, near, own_k, far, near, own_v)


def finish_kernel(aliased, *refs):
    refs = refs[2:] if aliased else refs
    kept_ref, returned_ref, gk_ref, gv_ref = refs
    gk_ref[...] = (kept_ref[0] + returned_ref[0].astype(jnp.float32)).astype(jnp.bfloat16)
    gv_ref[...] = (kept_ref[1] + returned_ref[1].astype(jnp.float32)).astype(jnp.bfloat16)


def finished(chunk, shape, kept, returned, carried):
    aliased = carried is not None
    carried = carried if aliased else ()
    out = pl.BlockSpec((shape[0], kept.shape[2]), lambda i: (0, chunk))
    return pl.pallas_call(
        functools.partial(finish_kernel, aliased),
        grid=(1,),
        in_specs=[pl.BlockSpec(memory_space=pl.ANY)] * len(carried)
        + [pl.BlockSpec(kept.shape, lambda i: (0, 0, 0))] * 2,
        out_specs=[out, out],
        out_shape=[jax.ShapeDtypeStruct(shape, jnp.bfloat16)] * 2,
        input_output_aliases={0: 0, 1: 1} if aliased else {},
        compiler_params=pltpu.CompilerParams(vmem_limit_bytes=SMALL_LIMIT),
        name="finish_keys_values",
    )(*carried, kept, returned)


def on_device(queries, keys, values, grad_out, episode_lengths):
    rows = queries.shape[0]
    groups = keys.shape[1] // HEAD_DIM
    count = lax.axis_size("seq")
    place = lax.axis_index("seq").astype(jnp.int32)
    odd = lax.bitwise_and(place, jnp.int32(1))
    first = jnp.reshape(place * rows, (1,))
    ahead = [(source, (source + 2) % count) for source in range(count)]
    behind = [((source + 2) % count, source) for source in range(count)]
    swap = [(source, source ^ 1) for source in range(count)]
    split = SPLIT if sum(SPLIT) == groups else (groups,)
    bases = [sum(split[:index]) for index in range(len(split))]

    own = list(packed(keys, values, [b * HEAD_DIM for b in bases], [s * HEAD_DIM for s in split]))
    far = [permuted(block, ahead) for block in own]
    bias = masks(rows, episode_lengths, first)
    own[0], bias = lax.optimization_barrier((own[0], bias))
    q_here, do_here, k_here, v_here = (in_hbm(x) for x in (queries, grad_out, keys, values))
    carried = grads = None
    parts = []
    for index, (base, size) in enumerate(zip(bases, split)):
        near = permuted(jnp.where(odd == 1, far[index], own[index]), swap)
        attn_out, grad_queries, back, kept = attention(
            base, size, bias, q_here, do_here, far[index], near, k_here, v_here, carried
        )
        carried = (attn_out, grad_queries)
        if parts:
            back, parts[-1][1] = lax.optimization_barrier((back, parts[-1][1]))
        beside = permuted(back[1], swap)
        none = jnp.zeros_like(beside)
        onward = back[0].astype(jnp.float32) + jnp.where(odd == 1, beside, none).astype(jnp.float32)
        kept = kept + jnp.where(odd == 1, none, beside).astype(jnp.float32)
        parts.append([kept, permuted(onward.astype(jnp.bfloat16), behind)])
    for base, size, (kept, returned) in zip(bases, split, parts):
        grads = finished(base // size, keys.shape, kept, returned, grads)
    return (attn_out, grad_queries, *grads)


def solution(mesh):
    split = P(("groups", "seq"), None)
    return jax.shard_map(
        on_device,
        mesh=mesh,
        in_specs=(split, split, split, split, P("groups")),
        out_specs=(split, split, split, split),
        check_vma=False,
    )
```

time: 67.6 us -> 55.4 us (0.82)
  other arithmetic: 5.1 us -> 0.28 us
  starting transfers between devices: 11.6 us -> 7.43 us
  Pallas kernels: 28 us -> 25.2 us
  waiting for transfers between devices: 20.5 us -> 18.9 us
  local copies, waits for them, and re-layouts: 1.34 us -> 2.59 us
    ppermute x8, starting transfers between devices: 11.6 us -> 7.43 us  [permuted(): return lax.ppermute(value, 'seq', pairs)]
    concatenate x4 -> x0, other arithmetic: 2.9 us -> none  [the longest x2 1.46 us: on_device(): own.append(jnp.concatenate([keys[:, span], values[:, span]], axis=1))]
    pallas_call x2 -> x6, Pallas kernels: 28 us -> 25.2 us  [the longest x2 22.6 us: attention(): pl.pallas_call(functools.partial(attention_kernel, aliased), grid=(groups...]
    unnamed x10 -> x6, local copies, waits for them, and re-layouts: 0.02 us -> 2.55 us
    select_n x2, other arithmetic: 1.74 us -> 0.06 us  [on_device(): near = permuted(jnp.where(odd == 1, far[index], own[index]), swap)]
    ppermute x8, waiting for transfers between devices: 20.5 us -> 18.9 us  [permuted(): return lax.ppermute(value, 'seq', pairs)]
    slice x1 -> x0, local copies, waits for them, and re-layouts: 1.28 us -> none  [on_device(): own.append(jnp.concatenate([keys[:, span], values[:, span]], axis=1))]
  transfers between devices with their start and end apart: 8 -> 8, of which waited for: 5 -> 5; matrix products, arithmetic and copies ran while one was open for 4% -> 0% of each run, Pallas kernels for 42% -> 44%
where the time goes in v2:
time: 55.4 us; the launch traced here: 55.1 us
  Pallas kernels  25.2 us (45%)
  waiting for transfers between devices  18.9 us (34%)
  starting transfers between devices  7.43 us (13%)
  local copies, waits for them, and re-layouts  2.59 us (5%)
  between operations  0.71 us (1%)
    pallas_call x2, Pallas kernels, attention(): pl.pallas_call(functools.partial(attention_kernel, aliased), grid=(groups...  22.6 us
    ppermute x8, waiting for transfers between devices, permuted(): return lax.ppermute(value, 'seq', pairs)  18.9 us
    ppermute x8, starting transfers between devices, permuted(): return lax.ppermute(value, 'seq', pairs)  7.43 us
    unnamed x6, local copies, waits for them, and re-layouts  2.55 us
    pallas_call x2, Pallas kernels, finished(): pl.pallas_call(functools.partial(finish_kernel, aliased), grid=(1,), in_s...  1.46 us
  transfers between devices with their start and end apart: 8, of which 5 were waited for; matrix products, arithmetic and copies ran while one was open for 0% of the time, Pallas kernels for 44%

profile of v2, /device:TPU:0, one launch (start us, length us, event | category | flops | bytes accessed | tf_op | source)
XLA Modules:
  0.0 55.1 jit_solution(16805399776263882418)
XLA Ops:
  0.6 0.0 copy-start
  0.6 0.9 %copy-done = bf16[256,512]{1,0:T(8,128)(2,1)S(1)} copy-done((bf16[256,512]{1,0:T(8,128)(2,1)S(1)}, bf16[256,512]{1,0:T(8,128)(2,1)}, u32[]{:S(2)}) %copy-start) | copy-done | bytes 262168
  1.6 0.0 copy-start.1
  1.6 0.9 %copy-done.1 = bf16[256,512]{1,0:T(8,128)(2,1)S(1)} copy-done((bf16[256,512]{1,0:T(8,128)(2,1)S(1)}, bf16[256,512]{1,0:T(8,128)(2,1)}, u32[]{:S(2)}) %copy-start.1) | copy-done | bytes 262168
  2.6 3.0 %collective-permute-start = (bf16[256,512]{1,0:T(8,128)(2,1)S(1)}, bf16[256,512]{1,0:T(8,128)(2,1)S(1)}, u32[]{:S(2)}, u32[]{:S(2)}) collective-permute-start(bf16[256,512]{1,0:T(8,128)(2,1)S(1)} %get-tuple-element.24), channel_id=1, source_target_pairs={{0,2},{1,3},{2,4},{3,5},{4,6},{5,7},{6,8},{7,9},{8,10},{9,11},{10,... | collective-permute-start | bytes 786440 | tf_op jit(solution)/shard_map/ppermute | solution.py:30
  5.6 0.0 copy-start.2
  5.6 0.7 %copy-done.2 = s32[16]{0:T(128)S(1)} copy-done((s32[16]{0:T(128)S(1)}, s32[16]{0:T(128)}, u32[]{:S(2)}) %copy-start.2) | copy-done | bytes 88
  6.2 1.1 %masks.1.refs_0_.refs_2_ = f32[2,128,640]{2,1,0:T(8,128)S(1)} custom-call(s32[16]{0:T(128)S(1)} %copy-done.2, s32[1]{0:T(128)} %bitcast.first_ref), custom_call_target="tpu_custom_call" | custom-call | tf_op jit(solution)/shard_map/masks/pallas_call | solution.py:77
  7.3 7.6 %collective-permute-done.refs_3_.refs_6_ = bf16[256,512]{1,0:T(8,128)(2,1)S(1)} collective-permute-done((bf16[256,512]{1,0:T(8,128)(2,1)S(1)}, bf16[256,512]{1,0:T(8,128)(2,1)S(1)}, u32[]{:S(2)}, u32[]{:S(2)}) %collective-permute-start) | collective-permute-done | bytes 262176 | tf_op jit(solution)/shard_map/ppermute | solution.py:30
  15.0 0.1 collective-permute-start.1
  15.0 0.1 collective-permute-start.2
  15.1 1.5 %collective-permute-done.1.refs_4_.refs_7_ = bf16[256,512]{1,0:T(8,128)(2,1)S(1)} collective-permute-done((bf16[256,512]{1,0:T(8,128)(2,1)S(1)}, bf16[256,512]{1,0:T(8,128)(2,1)S(1)}, u32[]{:S(2)}, u32[]{:S(2)}) %collective-permute-start.1) | collective-permute-done | bytes 262176 | tf_op jit(solution)/shard_map/ppermute | solution.py:30
  16.6 11.3 %attention.2 = (bf16[256,4096]{1,0:T(8,128)(2,1)}, bf16[256,4096]{1,0:T(8,128)(2,1)}, bf16[2,2,256,256]{3,2,1,0:T(8,128)(2,1)S(1)}, f32[2,256,256]{2,1,0:T(8,128)S(1)}) custom-call(f32[2,128,640]{2,1,0:T(8,128)S(1)} %masks.1.refs_0_.refs_2_, bf16[256,4096]{1,0:T(8,128)(2,1)} %refs_3_.1, bf16[256,4096]{1,0:T(8,128)(2,1)} %refs_4_.1, ...), custom_call_target="tpu_custom_call" | custom-call | tf_op jit(solution)/shard_map/attention/pallas_call | solution.py:177
  27.9 0.2 collective-permute-start.4
  28.1 0.0 collective-permute-done.2.refs_5_.refs_8_
  28.1 0.4 collective-permute-start.3
  28.6 0.9 %collective-permute-done.4 = bf16[2,256,256]{2,1,0:T(8,128)(2,1)S(1)} collective-permute-done((bf16[2,256,256]{2,1,0:T(8,128)(2,1)S(1)}, bf16[2,256,256]{2,1,0:T(8,128)(2,1)S(1)}, u32[]{:S(2)}, u32[]{:S(2)}) %collective-permute-start.4) | collective-permute-done | bytes 262176 | tf_op jit(solution)/shard_map/ppermute | solution.py:30
  29.5 0.1 fusion.1
  29.6 3.3 %collective-permute-start.5 = (bf16[2,256,256]{2,1,0:T(8,128)(2,1)S(1)}, bf16[2,256,256]{2,1,0:T(8,128)(2,1)S(1)}, u32[]{:S(2)}, u32[]{:S(2)}) collective-permute-start(bf16[2,256,256]{2,1,0:T(8,128)(2,1)S(1)} %get-tuple-element.42), channel_id=1, source_target_pairs={{2,0},{3,1},{4,2},{5,3},{6,4},{7,5},{8,6},{9,7},{10,8},{11,9},{12,... | collective-permute-start | bytes 786440 | tf_op jit(solution)/shard_map/ppermute | solution.py:30
  32.9 0.0 collective-permute-done.3.refs_6_.refs_9_
  32.9 11.3 %attention.3 = (bf16[256,4096]{1,0:T(8,128)(2,1)}, bf16[256,4096]{1,0:T(8,128)(2,1)}, bf16[2,2,256,256]{3,2,1,0:T(8,128)(2,1)S(1)}, f32[2,256,256]{2,1,0:T(8,128)S(1)}) custom-call(bf16[256,4096]{1,0:T(8,128)(2,1)} %get-tuple-element.25.refs_0_, bf16[256,4096]{1,0:T(8,128)(2,1)} %get-tuple-element.26.refs_1_, ...), custom_call_target="tpu_custom_call", output_to_operand_aliasing={{0}: (0, {}), {1}: (1, {})} | custom-call | tf_op jit(solution)/shard_map/attention/pallas_call | solution.py:177
  44.2 0.0 collective-permute-done.5.refs_1_
  44.3 0.1 collective-permute-start.6
  44.3 1.5 %collective-permute-done.6 = bf16[2,256,256]{2,1,0:T(8,128)(2,1)S(1)} collective-permute-done((bf16[2,256,256]{2,1,0:T(8,128)(2,1)S(1)}, bf16[2,256,256]{2,1,0:T(8,128)(2,1)S(1)}, u32[]{:S(2)}, u32[]{:S(2)}) %collective-permute-start.6) | collective-permute-done | bytes 262176 | tf_op jit(solution)/shard_map/ppermute | solution.py:30
  45.9 0.1 fusion
  46.0 0.2 collective-permute-start.7
  46.2 0.7 %finish_keys_values.2 = (bf16[256,512]{1,0:T(8,128)(2,1)}, bf16[256,512]{1,0:T(8,128)(2,1)}) custom-call(f32[2,256,256]{2,1,0:T(8,128)S(1)} %get-tuple-element.43.refs_0_, bf16[2,256,256]{2,1,0:T(8,128)(2,1)S(1)} %collective-permute-done.5.refs_1_), custom_call_target="tpu_custom_call" | custom-call | tf_op jit(solution)/shard_map/finish_keys_values/pallas_call | solution.py:218
  47.0 7.4 %collective-permute-done.7.refs_3_ = bf16[2,256,256]{2,1,0:T(8,128)(2,1)S(1)} collective-permute-done((bf16[2,256,256]{2,1,0:T(8,128)(2,1)S(1)}, bf16[2,256,256]{2,1,0:T(8,128)(2,1)S(1)}, u32[]{:S(2)}, u32[]{:S(2)}) %collective-permute-start.7) | collective-permute-done | bytes 262176 | tf_op jit(solution)/shard_map/ppermute | solution.py:30
  54.4 0.7 %finish_keys_values.3 = (bf16[256,512]{1,0:T(8,128)(2,1)}, bf16[256,512]{1,0:T(8,128)(2,1)}) custom-call(bf16[256,512]{1,0:T(8,128)(2,1)} %get-tuple-element.34.refs_0_, bf16[256,512]{1,0:T(8,128)(2,1)} %get-tuple-element.35.refs_1_, f32[2,256,256]{2,1,0:T(8,128)S(1)} %get-tuple-element.41.refs_2_, ...), custom_call_target="tpu_custom_call", output_to_operand_aliasing={{0}: (0, {}), {1}: (1, {})} | custom-call | tf_op jit(solution)/shard_map/finish_keys_values/pallas_call | solution.py:218
  (5 shorter events, 0.1 us)
Async XLA Ops:
  0.6 1.0 %copy-start = (bf16[256,512]{1,0:T(8,128)(2,1)S(1)}, bf16[256,512]{1,0:T(8,128)(2,1)}, u32[]{:S(2)}) copy-start(bf16[256,512]{1,0:T(8,128)(2,1)} %refs_7_.1) | copy-start | bytes 786436
  1.6 0.9 %copy-start.1 = (bf16[256,512]{1,0:T(8,128)(2,1)S(1)}, bf16[256,512]{1,0:T(8,128)(2,1)}, u32[]{:S(2)}) copy-start(bf16[256,512]{1,0:T(8,128)(2,1)} %refs_10_.1) | copy-start | bytes 786436
  2.6 12.4 %collective-permute-start = (bf16[256,512]{1,0:T(8,128)(2,1)S(1)}, bf16[256,512]{1,0:T(8,128)(2,1)S(1)}, u32[]{:S(2)}, u32[]{:S(2)}) collective-permute-start(bf16[256,512]{1,0:T(8,128)(2,1)S(1)} %get-tuple-element.24), channel_id=1, source_target_pairs={{0,2},{1,3},{2,4},{3,5},{4,6},{5,7},{6,8},{7,9},{8,10},{9,11},{10,... | collective-permute-start | bytes 786440 | tf_op jit(solution)/shard_map/ppermute | solution.py:30
  5.6 0.7 %copy-start.2 = (s32[16]{0:T(128)S(1)}, s32[16]{0:T(128)}, u32[]{:S(2)}) copy-start(s32[16]{0:T(128)} %lengths_ref.1) | copy-start | bytes 196
  15.0 1.6 %collective-permute-start.1 = (bf16[256,512]{1,0:T(8,128)(2,1)S(1)}, bf16[256,512]{1,0:T(8,128)(2,1)S(1)}, u32[]{:S(2)}, u32[]{:S(2)}) collective-permute-start(bf16[256,512]{1,0:T(8,128)(2,1)S(1)} %broadcast_select_fusion.1), channel_id=1, source_target_pairs={{0,1},{1,0},{2,3},{3,2},{4,5},{5,4},{6,7},{7,6},{8,9},{9,8},{10,11... | collective-permute-start | bytes 786440 | tf_op jit(solution)/shard_map/ppermute | solution.py:30
  15.0 13.1 %collective-permute-start.2 = (bf16[256,512]{1,0:T(8,128)(2,1)S(1)}, bf16[256,512]{1,0:T(8,128)(2,1)S(1)}, u32[]{:S(2)}, u32[]{:S(2)}) collective-permute-start(bf16[256,512]{1,0:T(8,128)(2,1)S(1)} %get-tuple-element.27), channel_id=1, source_target_pairs={{0,2},{1,3},{2,4},{3,5},{4,6},{5,7},{6,8},{7,9},{8,10},{9,11},{10,... | collective-permute-start | bytes 786440 | tf_op jit(solution)/shard_map/ppermute | solution.py:30
  27.9 1.6 %collective-permute-start.4 = (bf16[2,256,256]{2,1,0:T(8,128)(2,1)S(1)}, bf16[2,256,256]{2,1,0:T(8,128)(2,1)S(1)}, u32[]{:S(2)}, u32[]{:S(2)}) collective-permute-start(bf16[2,256,256]{2,1,0:T(8,128)(2,1)S(1)} %slice_bitcast_fusion.1), channel_id=1, source_target_pairs={{0,1},{1,0},{2,3},{3,2},{4,5},{5,4},{6,7},{7,6},{8,9},{9,8},{10,11... | collective-permute-start | bytes 786440 | tf_op jit(solution)/shard_map/ppermute | solution.py:30
  28.1 4.8 %collective-permute-start.3 = (bf16[256,512]{1,0:T(8,128)(2,1)S(1)}, bf16[256,512]{1,0:T(8,128)(2,1)S(1)}, u32[]{:S(2)}, u32[]{:S(2)}) collective-permute-start(bf16[256,512]{1,0:T(8,128)(2,1)S(1)} %broadcast_select_fusion), channel_id=1, source_target_pairs={{0,1},{1,0},{2,3},{3,2},{4,5},{5,4},{6,7},{7,6},{8,9},{9,8},{10,11... | collective-permute-start | bytes 786440 | tf_op jit(solution)/shard_map/ppermute | solution.py:30
  29.6 14.6 %collective-permute-start.5 = (bf16[2,256,256]{2,1,0:T(8,128)(2,1)S(1)}, bf16[2,256,256]{2,1,0:T(8,128)(2,1)S(1)}, u32[]{:S(2)}, u32[]{:S(2)}) collective-permute-start(bf16[2,256,256]{2,1,0:T(8,128)(2,1)S(1)} %get-tuple-element.42), channel_id=1, source_target_pairs={{2,0},{3,1},{4,2},{5,3},{6,4},{7,5},{8,6},{9,7},{10,8},{11,9},{12,... | collective-permute-start | bytes 786440 | tf_op jit(solution)/shard_map/ppermute | solution.py:30
  44.3 1.6 %collective-permute-start.6 = (bf16[2,256,256]{2,1,0:T(8,128)(2,1)S(1)}, bf16[2,256,256]{2,1,0:T(8,128)(2,1)S(1)}, u32[]{:S(2)}, u32[]{:S(2)}) collective-permute-start(bf16[2,256,256]{2,1,0:T(8,128)(2,1)S(1)} %slice_bitcast_fusion), channel_id=1, source_target_pairs={{0,1},{1,0},{2,3},{3,2},{4,5},{5,4},{6,7},{7,6},{8,9},{9,8},{10,11... | collective-permute-start | bytes 786440 | tf_op jit(solution)/shard_map/ppermute | solution.py:30
  46.0 8.4 %collective-permute-start.7 = (bf16[2,256,256]{2,1,0:T(8,128)(2,1)S(1)}, bf16[2,256,256]{2,1,0:T(8,128)(2,1)S(1)}, u32[]{:S(2)}, u32[]{:S(2)}) collective-permute-start(bf16[2,256,256]{2,1,0:T(8,128)(2,1)S(1)} %get-tuple-element.40), channel_id=1, source_target_pairs={{2,0},{3,1},{4,2},{5,3},{6,4},{7,5},{8,6},{9,7},{10,8},{11,9},{12,... | collective-permute-start | bytes 786440 | tf_op jit(solution)/shard_map/ppermute | solution.py:30

commit v3 on v2

v3 whole, which is shorter than its diff:
```python
import functools
import math

import jax
import jax.numpy as jnp
from jax import lax
from jax.experimental import pallas as pl
from jax.experimental.pallas import tpu as pltpu
from jax.sharding import PartitionSpec as P

HEAD_DIM = 128
TILE = 128
HEADS_AT_ONCE = 4
SENT = (2, 2)
CALLS = (2, 2)
RETURNED = (2, 2)
NT = (((1,), (1,)), ((), ()))
NN = (((1,), (0,)), ((), ()))
TN = (((0,), (0,)), ((), ()))
FACTOR = 1.0 / math.sqrt(HEAD_DIM)
FACTOR2 = math.log2(math.e) / math.sqrt(HEAD_DIM)
NEVER = -1e30
VMEM_LIMIT = 20 * 1024 * 1024
QUERY_LIMIT = 12 * 1024 * 1024
SMALL_LIMIT = 6 * 1024 * 1024


def matmul(left, right, dims):
    return lax.dot_general(left, right, dims, preferred_element_type=jnp.float32)


def permuted(value, pairs):
    return lax.ppermute(value, "seq", pairs)


def in_hbm(value):
    return pltpu.with_memory_space_constraint(value, pltpu.HBM)


def pack_kernel(starts, sizes, k_ref, v_ref, *outs):
    for out, start, size in zip(outs, starts, sizes):
        out[:, :size] = k_ref[:, start : start + size]
        out[:, size:] = v_ref[:, start : start + size]


def packed(keys, values, starts, sizes):
    rows = keys.shape[0]
    return pl.pallas_call(
        functools.partial(pack_kernel, starts, sizes),
        grid=(1,),
        in_specs=[pl.BlockSpec(keys.shape, lambda i: (0, 0))] * 2,
        out_specs=[pl.BlockSpec((rows, 2 * size), lambda i: (0, 0)) for size in sizes],
        out_shape=[jax.ShapeDtypeStruct((rows, 2 * size), keys.dtype) for size in sizes],
        compiler_params=pltpu.CompilerParams(vmem_limit_bytes=SMALL_LIMIT),
        name="pack_keys_values",
    )(keys, values)


def mask_kernel(count, lengths_ref, first_ref, bias_ref):
    tiles, _, band = bias_ref.shape
    rows = tiles * TILE
    row = lax.broadcasted_iota(jnp.int32, (rows, 1), 0)

    def one(index, carry):
        begin, start = carry
        return begin + lengths_ref[index], jnp.where(row >= begin, begin, start)

    _, start = lax.fori_loop(
        0, count, one, (-first_ref[0], jnp.full((rows, 1), -4 * rows, jnp.int32))
    )
    for tile in range(tiles):
        here = slice(tile * TILE, (tile + 1) * TILE)
        key = lax.broadcasted_iota(jnp.int32, (TILE, band), 1) + (tile * TILE - 2 * rows)
        allowed = (key >= start[here]) & (key <= row[here])
        bias_ref[tile] = jnp.where(allowed, 0.0, NEVER)


def masks(rows, lengths, first):
    smem = pl.BlockSpec(memory_space=pltpu.SMEM)
    return pl.pallas_call(
        functools.partial(mask_kernel, lengths.shape[0]),
        in_specs=[smem, smem],
        out_specs=pl.BlockSpec(memory_space=pltpu.VMEM),
        out_shape=jax.ShapeDtypeStruct((rows // TILE, TILE, 2 * rows + TILE), jnp.float32),
        compiler_params=pltpu.CompilerParams(vmem_limit_bytes=SMALL_LIMIT),
        name="masks",
    )(lengths, first)


def lanes(block, width=HEAD_DIM):
    return pl.ds(pl.multiple_of(block * width, width), width)


def attention_kernel(base, skipped, first_ref, bias, q_hbm, do_hbm, far, near, own, *refs):
    o_ref, ds_ref, back_ref, own_ref, q_ref, do_ref, k_all, v_all, dk_sum, dv_sum, sems = refs
    group = pl.program_id(0)
    groups, tiles, _, _ = ds_ref.shape
    rows = far.shape[0]
    sent = far.shape[1] // (2 * HEAD_DIM)
    wide = q_ref.shape[2]
    heads = wide // HEAD_DIM
    per_call = min(HEADS_AT_ONCE, heads)

    def fetches(index):
        span = pl.ds((base + index) * wide, wide)
        return [
            pltpu.make_async_copy(whole.at[:, span], held.at[index], sems.at[index, place])
            for place, (whole, held) in enumerate(((q_hbm, q_ref), (do_hbm, do_ref)))
        ]

    @pl.when(group == 0)
    def _():
        for index in range(groups):
            for fetch in fetches(index):
                fetch.start()

    k_col = lanes(skipped + group)
    v_col = lanes(sent + skipped + group)
    for place, part in enumerate((far, near, own)):
        k_all[place * rows : (place + 1) * rows] = part[:, k_col]
        v_all[place * rows : (place + 1) * rows] = part[:, v_col]
    for index in range(groups):

        @pl.when(group == index)
        def _():
            for fetch in fetches(index):
                fetch.wait()

    def all_units(lowest):
        dk_sum[...] = jnp.zeros_like(dk_sum)
        dv_sum[...] = jnp.zeros_like(dv_sum)
        units = [(tile, first) for tile in range(tiles) for first in range(0, heads, per_call)]

        def places(unit):
            tile, first = unit
            here = slice(tile * TILE, (tile + 1) * TILE)
            keys = slice(max(tile * TILE, lowest), tile * TILE + 2 * rows + TILE)
            cols = [slice((first + x) * HEAD_DIM, (first + x + 1) * HEAD_DIM) for x in range(per_call)]
            return here, keys, cols

        def stacked(ref, unit):
            here, _, cols = places(unit)
            return jnp.concatenate([ref[group, here, c] for c in cols], 0)

        def scores(unit):
            return matmul(stacked(q_ref, unit), k_all[places(unit)[1]], NT)

        def softmax(unit, s):
            _, keys, _ = places(unit)
            width = keys.stop - keys.start
            shut = bias[unit[0], :, keys.start - unit[0] * TILE :]
            s = s.reshape(per_call, TILE, width) * FACTOR2 + shut[None]
            s = s.reshape(per_call * TILE, width)
            e = jnp.exp2(s - jnp.max(s, 1, keepdims=True))
            return e * (1.0 / jnp.sum(e, 1, keepdims=True))

        def score_grads(unit, prob, weight):
            here, keys, cols = places(unit)
            do = stacked(do_ref, unit)
            out = matmul(weight, v_all[keys], NN).astype(jnp.bfloat16)
            for x, c in enumerate(cols):
                o_ref[group, here, c] = out[x * TILE : (x + 1) * TILE]
            dp = matmul(do, v_all[keys], NT)
            delta = jnp.sum(out.astype(jnp.float32) * do.astype(jnp.float32), 1, keepdims=True)
            ds = (prob * (dp - delta)).astype(jnp.bfloat16)
            tile, first = unit
            ds_ref[group, tile, first * TILE : (first + per_call) * TILE, keys.start - tile * TILE :] = ds
            return ds

        def sums(unit, weight, ds):
            _, keys, _ = places(unit)
            dv_sum[:, keys] += matmul(stacked(do_ref, unit), weight, TN)
            dk_sum[:, keys] += matmul(stacked(q_ref, unit), ds, TN)

        ahead = scores(units[0])
        before = None
        for index, unit in enumerate(units):
            now = ahead
            if index + 1 < len(units):
                ahead = scores(units[index + 1])
            prob = softmax(unit, now)
            weight = prob.astype(jnp.bfloat16)
            if before is not None:
                sums(*before)
            before = (unit, weight, score_grads(unit, prob, weight))
        sums(*before)
        if lowest:
            for tile in range(tiles):
                gap = max(0, lowest - tile * TILE)
                ds_ref[group, tile, :, :gap] = jnp.zeros((heads * TILE, gap), jnp.bfloat16)

        here = lanes(group)
        own_ref[0, :, here] = dk_sum[:, 2 * rows :].T * FACTOR
        own_ref[1, :, here] = dv_sum[:, 2 * rows :].T
        for place in range(2):
            span = slice(place * rows, (place + 1) * rows)
            back_ref[place, 0, :, here] = (dk_sum[:, span].T * FACTOR).astype(jnp.bfloat16)
            back_ref[place, 1, :, here] = dv_sum[:, span].T.astype(jnp.bfloat16)

    @pl.when(first_ref[0] >= 2 * rows)
    def _():
        all_units(0)

    @pl.when(first_ref[0] < 2 * rows)
    def _():
        all_units(rows)


def attention(base, groups, skipped, head_cols, first, bias, q, do, far, near, own):
    rows = q.shape[0]
    tiles, _, band = bias.shape
    whole = pl.BlockSpec(memory_space=pltpu.VMEM)
    far_away = pl.BlockSpec(memory_space=pltpu.HBM)
    return pl.pallas_call(
        functools.partial(attention_kernel, base, skipped),
        grid=(groups,),
        in_specs=[pl.BlockSpec(memory_space=pltpu.SMEM), whole, far_away, far_away, whole, whole, whole],
        out_specs=[whole] * 4,
        out_shape=[
            jax.ShapeDtypeStruct((groups, rows, head_cols), jnp.bfloat16),
            jax.ShapeDtypeStruct((groups, tiles, head_cols // HEAD_DIM * TILE, band), jnp.bfloat16),
            jax.ShapeDtypeStruct((2, 2, rows, groups * HEAD_DIM), jnp.bfloat16),
            jax.ShapeDtypeStruct((2, rows, groups * HEAD_DIM), jnp.float32),
        ],
        scratch_shapes=[
            pltpu.VMEM((groups, rows, head_cols), jnp.bfloat16),
            pltpu.VMEM((groups, rows, head_cols), jnp.bfloat16),
            pltpu.VMEM((3 * rows, HEAD_DIM), jnp.bfloat16),
            pltpu.VMEM((3 * rows, HEAD_DIM), jnp.bfloat16),
            pltpu.VMEM((HEAD_DIM, 3 * rows), jnp.float32),
            pltpu.VMEM((HEAD_DIM, 3 * rows), jnp.float32),
            pltpu.SemaphoreType.DMA((groups, 2)),
        ],
        compiler_params=pltpu.CompilerParams(vmem_limit_bytes=VMEM_LIMIT),
        name="attention",
    )(first, bias, q, do, far, near, own)


def query_kernel(calls, skips, *refs):
    o_out, dq_out, k_all = refs[-3:]
    group = pl.program_id(0)
    rows = o_out.shape[0]
    heads = o_out.shape[1] // HEAD_DIM
    base = 0
    for index, (size, skipped) in enumerate(zip(calls, skips)):
        o_ref, ds_ref, far, near, own = refs[5 * index : 5 * index + 5]

        @pl.when((group >= base) & (group < base + size))
        def _(base=base, skipped=skipped, o_ref=o_ref, ds_ref=ds_ref, parts=(far, near, own)):
            here = group - base
            o_out[...] = o_ref[here]
            for place, part in enumerate(parts):
                k_all[place * rows : (place + 1) * rows] = part[:, lanes(skipped + here)]
            for tile in range(ds_ref.shape[1]):
                k = k_all[tile * TILE : tile * TILE + ds_ref.shape[3]]
                dq = (matmul(ds_ref[here, tile], k, NN) * FACTOR).astype(jnp.bfloat16)
                for x in range(heads):
                    dq_out[tile * TILE : (tile + 1) * TILE, x * HEAD_DIM : (x + 1) * HEAD_DIM] = dq[
                        x * TILE : (x + 1) * TILE
                    ]

        base += size


def query_grads(calls, skips, shape, parts):
    rows, width = shape
    flat = [array for part in parts for array in part]
    out = pl.BlockSpec((rows, width // sum(calls)), lambda g: (0, g))
    return pl.pallas_call(
        functools.partial(query_kernel, calls, skips),
        grid=(sum(calls),),
        in_specs=[pl.BlockSpec(memory_space=pltpu.VMEM)] * len(flat),
        out_specs=[out, out],
        out_shape=[jax.ShapeDtypeStruct(shape, jnp.bfloat16)] * 2,
        scratch_shapes=[pltpu.VMEM((3 * rows, HEAD_DIM), jnp.bfloat16)],
        compiler_params=pltpu.CompilerParams(vmem_limit_bytes=QUERY_LIMIT),
        name="query_grads",
    )(*flat)


def finish_kernel(base, aliased, *refs):
    refs = refs[2:] if aliased else refs
    kept_ref, returned_ref, gk_ref, gv_ref, total, sems = refs
    span = pl.ds(base * HEAD_DIM, kept_ref.shape[2])
    copies = []
    for index, out in enumerate((gk_ref, gv_ref)):
        total[index] = (kept_ref[index] + returned_ref[index].astype(jnp.float32)).astype(jnp.bfloat16)
        copies.append(pltpu.make_async_copy(total.at[index], out.at[:, span], sems.at[index]))
        copies[-1].start()
    for copy in copies:
        copy.wait()


def finished(base, shape, kept, returned, carried):
    aliased = carried is not None
    carried = carried if aliased else ()
    kept_place = pl.BlockSpec(memory_space=pl.ANY)
    whole = pl.BlockSpec(memory_space=pltpu.VMEM)
    return pl.pallas_call(
        functools.partial(finish_kernel, base, aliased),
        in_specs=[kept_place] * len(carried) + [whole, whole],
        out_specs=[pl.BlockSpec(memory_space=pltpu.HBM)] * 2,
        out_shape=[jax.ShapeDtypeStruct(shape, jnp.bfloat16)] * 2,
        scratch_shapes=[
            pltpu.VMEM((2, shape[0], kept.shape[2]), jnp.bfloat16),
            pltpu.SemaphoreType.DMA((2,)),
        ],
        input_output_aliases={0: 0, 1: 1} if aliased else {},
        compiler_params=pltpu.CompilerParams(vmem_limit_bytes=SMALL_LIMIT),
        name="finish_keys_values",
    )(*carried, kept, returned)


def on_device(queries, keys, values, grad_out, episode_lengths):
    rows = queries.shape[0]
    groups = keys.shape[1] // HEAD_DIM
    count = lax.axis_size("seq")
    place = lax.axis_index("seq").astype(jnp.int32)
    odd = lax.bitwise_and(place, jnp.int32(1))
    first = jnp.reshape(place * rows, (1,))
    ahead = [(source, (source + 2) % count) for source in range(count)]
    behind = [((source + 2) % count, source) for source in range(count)]
    swap = [(source, source ^ 1) for source in range(count)]
    known = groups == sum(SENT)
    sent = SENT if known else (groups,)
    calls = CALLS if known else (groups,)
    returns = RETURNED if known else (groups,)
    starts = [sum(sent[:index]) for index in range(len(sent))]

    q_here, do_here, k_here, v_here = (in_hbm(x) for x in (queries, grad_out, keys, values))
    own = list(packed(k_here, v_here, [b * HEAD_DIM for b in starts], [s * HEAD_DIM for s in sent]))
    far = [permuted(block, ahead) for block in own]
    bias = masks(rows, episode_lengths, first)
    own[0], bias = lax.optimization_barrier((own[0], bias))
    near = [permuted(jnp.where(odd == 1, there, here), swap) for there, here in zip(far, own)]
    grads = None
    parts = []
    waiting = []
    stored = []
    skips = []
    base = begun = 0
    for size in calls:
        chunk = max(index for index, start in enumerate(starts) if start <= base)
        skips.append(base - starts[chunk])
        out, ds, back, kept = attention(
            base, size, skips[-1], queries.shape[1] // groups, first, bias, q_here, do_here, far[chunk], near[chunk], own[chunk]
        )
        stored.append((out, ds, far[chunk], near[chunk], own[chunk]))
        waiting.append((back, kept))
        base += size
        if base < begun + returns[len(parts)]:
            continue
        back = jnp.concatenate([pair[0] for pair in waiting], axis=3)
        kept = jnp.concatenate([pair[1] for pair in waiting], axis=2)
        waiting = []
        if parts:
            back, parts[-1][2] = lax.optimization_barrier((back, parts[-1][2]))
        beside = permuted(back[1], swap)
        none = jnp.zeros_like(beside)
        onward = back[0].astype(jnp.float32) + jnp.where(odd == 1, beside, none).astype(jnp.float32)
        kept = kept + jnp.where(odd == 1, none, beside).astype(jnp.float32)
        parts.append([begun, kept, permuted(onward.astype(jnp.bfloat16), behind)])
        begun = base
    attn_out, grad_queries = query_grads(calls, skips, queries.shape, stored)
    for begun, kept, returned in parts:
        grads = finished(begun, keys.shape, kept, returned, grads)
    return (attn_out, grad_queries, *grads)


def solution(mesh):
    split = P(("groups", "seq"), None)
    return jax.shard_map(
        on_device,
        mesh=mesh,
        in_specs=(split, split, split, split, P("groups")),
        out_specs=(split, split, split, split),
        check_vma=False,
    )
```

time: 55.4 us -> 50.7 us (0.915)
  waiting for transfers between devices: 18.9 us -> 12.8 us
  starting transfers between devices: 7.43 us -> 11.8 us
  local copies, waits for them, and re-layouts: 2.59 us -> 0.69 us
  Pallas kernels: 25.2 us -> 24 us
    ppermute x8, waiting for transfers between devices: 18.9 us -> 12.8 us  [permuted(): return lax.ppermute(value, 'seq', pairs)]
    ppermute x8, starting transfers between devices: 7.43 us -> 11.8 us  [permuted(): return lax.ppermute(value, 'seq', pairs)]
    pallas_call x4 -> x5, Pallas kernels: 24.1 us -> 21.8 us  [the longest x2 15.7 us: attention(): pl.pallas_call(functools.partial(attention_kernel, base, skipped), grid=(...]
    unnamed x6 -> x2, local copies, waits for them, and re-layouts: 2.55 us -> 0.65 us
    pallas_call x1, Pallas kernels: 0.03 us -> 1.06 us  [packed(): pl.pallas_call(functools.partial(pack_kernel, starts, sizes), grid=(1,),...]
where the time goes in v3:
time: 50.7 us; the launch traced here: 50.5 us
  Pallas kernels  24 us (47%)
  waiting for transfers between devices  12.8 us (25%)
  starting transfers between devices  11.8 us (23%)
  between operations  0.91 us (2%)
  local copies, waits for them, and re-layouts  0.69 us (1%)
    pallas_call x2, Pallas kernels, attention(): pl.pallas_call(functools.partial(attention_kernel, base, skipped), grid=(...  15.7 us
    ppermute x8, waiting for transfers between devices, permuted(): return lax.ppermute(value, 'seq', pairs)  12.8 us
    ppermute x8, starting transfers between devices, permuted(): return lax.ppermute(value, 'seq', pairs)  11.8 us
    pallas_call x1, Pallas kernels, query_grads(): pl.pallas_call(functools.partial(query_kernel, calls, skips), grid=(sum(c...  4.65 us
    pallas_call x2, Pallas kernels, finished(): pl.pallas_call(functools.partial(finish_kernel, base, aliased), in_specs=...  1.48 us
    pallas_call x1, Pallas kernels, masks(): pl.pallas_call(functools.partial(mask_kernel, lengths.shape[0]), in_specs...  1.09 us
    pallas_call x1, Pallas kernels, packed(): pl.pallas_call(functools.partial(pack_kernel, starts, sizes), grid=(1,),...  1.06 us
  transfers between devices with their start and end apart: 8, of which 5 were waited for; matrix products, arithmetic and copies ran while one was open for 0% of the time, Pallas kernels for 44%

profile of v3, /device:TPU:0, one launch (start us, length us, event | category | flops | bytes accessed | tf_op | source)
XLA Modules:
  0.0 50.5 jit_solution(16483036589961974466)
XLA Ops:
  0.6 1.1 %pack_keys_values.1 = (bf16[256,512]{1,0:T(8,128)(2,1)S(1)}, bf16[256,512]{1,0:T(8,128)(2,1)S(1)}) custom-call(bf16[256,512]{1,0:T(8,128)(2,1)} %k_ref.1, bf16[256,512]{1,0:T(8,128)(2,1)} %v_ref.1), custom_call_target="tpu_custom_call" | custom-call | tf_op jit(solution)/shard_map/pack_keys_values/pallas_call | solution.py:48
  1.7 3.0 %collective-permute-start = (bf16[256,512]{1,0:T(8,128)(2,1)S(1)}, bf16[256,512]{1,0:T(8,128)(2,1)S(1)}, u32[]{:S(2)}, u32[]{:S(2)}) collective-permute-start(bf16[256,512]{1,0:T(8,128)(2,1)S(1)} %get-tuple-element.26.own.refs_4_), channel_id=1, source_target_pairs={{0,2},{1,3},{2,4},{3,5},{4,6},{5,7},{6,8},{7,9},{8,10},{9,11},{10,... | collective-permute-start | bytes 786440 | tf_op jit(solution)/shard_map/ppermute | solution.py:33
  4.7 0.0 copy-start
  4.7 0.7 %copy-done = s32[16]{0:T(128)S(1)} copy-done((s32[16]{0:T(128)S(1)}, s32[16]{0:T(128)}, u32[]{:S(2)}) %copy-start) | copy-done | bytes 88
  5.4 1.1 %masks.1.bias = f32[2,128,640]{2,1,0:T(8,128)S(1)} custom-call(s32[16]{0:T(128)S(1)} %copy-done, s32[1]{0:T(128)} %bitcast.first_ref), custom_call_target="tpu_custom_call" | custom-call | tf_op jit(solution)/shard_map/masks/pallas_call | solution.py:80
  6.5 7.6 %collective-permute-done.far.refs_2_ = bf16[256,512]{1,0:T(8,128)(2,1)S(1)} collective-permute-done((bf16[256,512]{1,0:T(8,128)(2,1)S(1)}, bf16[256,512]{1,0:T(8,128)(2,1)S(1)}, u32[]{:S(2)}, u32[]{:S(2)}) %collective-permute-start) | collective-permute-done | bytes 262176 | tf_op jit(solution)/shard_map/ppermute | solution.py:33
  14.1 0.1 collective-permute-start.1
  14.2 0.1 collective-permute-start.2
  14.2 1.5 %collective-permute-done.1.near.refs_3_ = bf16[256,512]{1,0:T(8,128)(2,1)S(1)} collective-permute-done((bf16[256,512]{1,0:T(8,128)(2,1)S(1)}, bf16[256,512]{1,0:T(8,128)(2,1)S(1)}, u32[]{:S(2)}, u32[]{:S(2)}) %collective-permute-start.1) | collective-permute-done | bytes 262176 | tf_op jit(solution)/shard_map/ppermute | solution.py:33
  15.7 7.9 %attention.2 = (bf16[2,256,1024]{2,1,0:T(8,128)(2,1)S(1)}, bf16[2,2,1024,640]{3,2,1,0:T(8,128)(2,1)S(1)}, bf16[2,2,256,256]{3,2,1,0:T(8,128)(2,1)S(1)}, f32[2,256,256]{2,1,0:T(8,128)S(1)}) custom-call(s32[1]{0:T(128)} %bitcast.first_ref, f32[2,128,640]{2,1,0:T(8,128)S(1)} %masks.1.bias, bf16[256,4096]{1,0:T(8,128)(2,1)} %q_hbm.3, bf16[256,4096]{1,0:T(8,128)(2,1)} %do_hbm.3, ...), custom_call_target="tpu_custom_call" | custom-call | tf_op jit(solution)/shard_map/attention/pallas_call | solution.py:214
  23.6 0.2 collective-permute-start.4
  23.8 1.8 %collective-permute-done.2.far.refs_7_ = bf16[256,512]{1,0:T(8,128)(2,1)S(1)} collective-permute-done((bf16[256,512]{1,0:T(8,128)(2,1)S(1)}, bf16[256,512]{1,0:T(8,128)(2,1)S(1)}, u32[]{:S(2)}, u32[]{:S(2)}) %collective-permute-start.2) | collective-permute-done | bytes 262176 | tf_op jit(solution)/shard_map/ppermute | solution.py:33
  25.6 0.1 collective-permute-start.3
  25.7 0.0 collective-permute-done.4
  25.7 0.1 fusion.1
  25.8 5.1 %collective-permute-start.5 = (bf16[2,256,256]{2,1,0:T(8,128)(2,1)S(1)}, bf16[2,256,256]{2,1,0:T(8,128)(2,1)S(1)}, u32[]{:S(2)}, u32[]{:S(2)}) collective-permute-start(bf16[2,256,256]{2,1,0:T(8,128)(2,1)S(1)} %get-tuple-element.46), channel_id=1, source_target_pairs={{2,0},{3,1},{4,2},{5,3},{6,4},{7,5},{8,6},{9,7},{10,8},{11,9},{12,... | collective-permute-start | bytes 786440 | tf_op jit(solution)/shard_map/ppermute | solution.py:33
  30.9 0.0 collective-permute-done.3.near.refs_8_
  30.9 7.8 %attention.3 = (bf16[2,256,1024]{2,1,0:T(8,128)(2,1)S(1)}, bf16[2,2,1024,640]{3,2,1,0:T(8,128)(2,1)S(1)}, bf16[2,2,256,256]{3,2,1,0:T(8,128)(2,1)S(1)}, f32[2,256,256]{2,1,0:T(8,128)S(1)}) custom-call(s32[1]{0:T(128)} %bitcast.first_ref, f32[2,128,640]{2,1,0:T(8,128)S(1)} %masks.1.bias, bf16[256,4096]{1,0:T(8,128)(2,1)} %q_hbm.3, bf16[256,4096]{1,0:T(8,128)(2,1)} %do_hbm.3, ...), custom_call_target="tpu_custom_call" | custom-call | tf_op jit(solution)/shard_map/attention/pallas_call | solution.py:214
  38.8 0.0 collective-permute-done.5.refs_1_
  38.8 0.1 collective-permute-start.6
  38.9 1.5 %collective-permute-done.6 = bf16[2,256,256]{2,1,0:T(8,128)(2,1)S(1)} collective-permute-done((bf16[2,256,256]{2,1,0:T(8,128)(2,1)S(1)}, bf16[2,256,256]{2,1,0:T(8,128)(2,1)S(1)}, u32[]{:S(2)}, u32[]{:S(2)}) %collective-permute-start.6) | collective-permute-done | bytes 262176 | tf_op jit(solution)/shard_map/ppermute | solution.py:33
  40.4 0.1 fusion
  40.5 3.3 %collective-permute-start.7 = (bf16[2,256,256]{2,1,0:T(8,128)(2,1)S(1)}, bf16[2,256,256]{2,1,0:T(8,128)(2,1)S(1)}, u32[]{:S(2)}, u32[]{:S(2)}) collective-permute-start(bf16[2,256,256]{2,1,0:T(8,128)(2,1)S(1)} %get-tuple-element.44), channel_id=1, source_target_pairs={{2,0},{3,1},{4,2},{5,3},{6,4},{7,5},{8,6},{9,7},{10,8},{11,9},{12,... | collective-permute-start | bytes 786440 | tf_op jit(solution)/shard_map/ppermute | solution.py:33
  43.8 4.6 %query_grads.1 = (bf16[256,4096]{1,0:T(8,128)(2,1)}, bf16[256,4096]{1,0:T(8,128)(2,1)}) custom-call(bf16[2,256,1024]{2,1,0:T(8,128)(2,1)S(1)} %get-tuple-element.27.refs_0_, bf16[2,2,1024,640]{3,2,1,0:T(8,128)(2,1)S(1)} %get-tuple-element.28.refs_1_, bf16[256,512]{1,0:T(8,128)(2,1)S(1)} %collective-permute-done.far.refs_2_, ...), custom_call_target="tpu_custom_call" | custom-call | tf_op jit(solution)/shard_map/query_grads/pallas_call | solution.py:269
  48.4 0.7 %finish_keys_values.2 = (bf16[256,512]{1,0:T(8,128)(2,1)}, bf16[256,512]{1,0:T(8,128)(2,1)}) custom-call(f32[2,256,256]{2,1,0:T(8,128)S(1)} %get-tuple-element.47.refs_0_, bf16[2,256,256]{2,1,0:T(8,128)(2,1)S(1)} %collective-permute-done.5.refs_1_), custom_call_target="tpu_custom_call" | custom-call | tf_op jit(solution)/shard_map/finish_keys_values/pallas_call | solution.py:299
  49.2 0.5 collective-permute-done.7.refs_3_
  49.6 0.7 %finish_keys_values.3 = (bf16[256,512]{1,0:T(8,128)(2,1)}, bf16[256,512]{1,0:T(8,128)(2,1)}) custom-call(bf16[256,512]{1,0:T(8,128)(2,1)} %get-tuple-element.38.refs_0_, bf16[256,512]{1,0:T(8,128)(2,1)} %get-tuple-element.39.refs_1_, f32[2,256,256]{2,1,0:T(8,128)S(1)} %get-tuple-element.45.refs_2_, ...), custom_call_target="tpu_custom_call", output_to_operand_aliasing={{0}: (0, {}), {1}: (1, {})} | custom-call | tf_op jit(solution)/shard_map/finish_keys_values/pallas_call | solution.py:299
  (4 shorter events, 0.1 us)
Async XLA Ops:
  1.7 12.4 %collective-permute-start = (bf16[256,512]{1,0:T(8,128)(2,1)S(1)}, bf16[256,512]{1,0:T(8,128)(2,1)S(1)}, u32[]{:S(2)}, u32[]{:S(2)}) collective-permute-start(bf16[256,512]{1,0:T(8,128)(2,1)S(1)} %get-tuple-element.26.own.refs_4_), channel_id=1, source_target_pairs={{0,2},{1,3},{2,4},{3,5},{4,6},{5,7},{6,8},{7,9},{8,10},{9,11},{10,... | collective-permute-start | bytes 786440 | tf_op jit(solution)/shard_map/ppermute | solution.py:33
  4.7 0.7 %copy-start = (s32[16]{0:T(128)S(1)}, s32[16]{0:T(128)}, u32[]{:S(2)}) copy-start(s32[16]{0:T(128)} %lengths_ref.1) | copy-start | bytes 196
  14.1 1.6 %collective-permute-start.1 = (bf16[256,512]{1,0:T(8,128)(2,1)S(1)}, bf16[256,512]{1,0:T(8,128)(2,1)S(1)}, u32[]{:S(2)}, u32[]{:S(2)}) collective-permute-start(bf16[256,512]{1,0:T(8,128)(2,1)S(1)} %broadcast_select_fusion.1), channel_id=1, source_target_pairs={{0,1},{1,0},{2,3},{3,2},{4,5},{5,4},{6,7},{7,6},{8,9},{9,8},{10,11... | collective-permute-start | bytes 786440 | tf_op jit(solution)/shard_map/ppermute | solution.py:33
  14.2 11.4 %collective-permute-start.2 = (bf16[256,512]{1,0:T(8,128)(2,1)S(1)}, bf16[256,512]{1,0:T(8,128)(2,1)S(1)}, u32[]{:S(2)}, u32[]{:S(2)}) collective-permute-start(bf16[256,512]{1,0:T(8,128)(2,1)S(1)} %get-tuple-element.29.own.refs_9_), channel_id=1, source_target_pairs={{0,2},{1,3},{2,4},{3,5},{4,6},{5,7},{6,8},{7,9},{8,10},{9,11},{10,... | collective-permute-start | bytes 786440 | tf_op jit(solution)/shard_map/ppermute | solution.py:33
  23.6 2.1 %collective-permute-start.4 = (bf16[2,256,256]{2,1,0:T(8,128)(2,1)S(1)}, bf16[2,256,256]{2,1,0:T(8,128)(2,1)S(1)}, u32[]{:S(2)}, u32[]{:S(2)}) collective-permute-start(bf16[2,256,256]{2,1,0:T(8,128)(2,1)S(1)} %slice_bitcast_fusion.1), channel_id=1, source_target_pairs={{0,1},{1,0},{2,3},{3,2},{4,5},{5,4},{6,7},{7,6},{8,9},{9,8},{10,11... | collective-permute-start | bytes 786440 | tf_op jit(solution)/shard_map/ppermute | solution.py:33
  25.6 5.3 %collective-permute-start.3 = (bf16[256,512]{1,0:T(8,128)(2,1)S(1)}, bf16[256,512]{1,0:T(8,128)(2,1)S(1)}, u32[]{:S(2)}, u32[]{:S(2)}) collective-permute-start(bf16[256,512]{1,0:T(8,128)(2,1)S(1)} %broadcast_select_fusion), channel_id=1, source_target_pairs={{0,1},{1,0},{2,3},{3,2},{4,5},{5,4},{6,7},{7,6},{8,9},{9,8},{10,11... | collective-permute-start | bytes 786440 | tf_op jit(solution)/shard_map/ppermute | solution.py:33
  25.8 12.9 %collective-permute-start.5 = (bf16[2,256,256]{2,1,0:T(8,128)(2,1)S(1)}, bf16[2,256,256]{2,1,0:T(8,128)(2,1)S(1)}, u32[]{:S(2)}, u32[]{:S(2)}) collective-permute-start(bf16[2,256,256]{2,1,0:T(8,128)(2,1)S(1)} %get-tuple-element.46), channel_id=1, source_target_pairs={{2,0},{3,1},{4,2},{5,3},{6,4},{7,5},{8,6},{9,7},{10,8},{11,9},{12,... | collective-permute-start | bytes 786440 | tf_op jit(solution)/shard_map/ppermute | solution.py:33
  38.8 1.6 %collective-permute-start.6 = (bf16[2,256,256]{2,1,0:T(8,128)(2,1)S(1)}, bf16[2,256,256]{2,1,0:T(8,128)(2,1)S(1)}, u32[]{:S(2)}, u32[]{:S(2)}) collective-permute-start(bf16[2,256,256]{2,1,0:T(8,128)(2,1)S(1)} %slice_bitcast_fusion), channel_id=1, source_target_pairs={{0,1},{1,0},{2,3},{3,2},{4,5},{5,4},{6,7},{7,6},{8,9},{9,8},{10,11... | collective-permute-start | bytes 786440 | tf_op jit(solution)/shard_map/ppermute | solution.py:33
  40.5 9.1 %collective-permute-start.7 = (bf16[2,256,256]{2,1,0:T(8,128)(2,1)S(1)}, bf16[2,256,256]{2,1,0:T(8,128)(2,1)S(1)}, u32[]{:S(2)}, u32[]{:S(2)}) collective-permute-start(bf16[2,256,256]{2,1,0:T(8,128)(2,1)S(1)} %get-tuple-element.44), channel_id=1, source_target_pairs={{2,0},{3,1},{4,2},{5,3},{6,4},{7,5},{8,6},{9,7},{10,8},{11,9},{12,... | collective-permute-start | bytes 786440 | tf_op jit(solution)/shard_map/ppermute | solution.py:33

commit v4 on v3

--- a/solution.py
+++ b/solution.py
@@ -22,7 +22,7 @@
 NEVER = -1e30
 VMEM_LIMIT = 20 * 1024 * 1024
 QUERY_LIMIT = 12 * 1024 * 1024
-SMALL_LIMIT = 6 * 1024 * 1024
+SMALL_LIMIT = 8 * 1024 * 1024
 
 
 def matmul(left, right, dims):
@@ -56,7 +56,13 @@
     )(keys, values)
 
 
-def mask_kernel(count, lengths_ref, first_ref, bias_ref):
+def prepare_kernel(count, lengths_ref, first_ref, q_hbm, do_hbm, bias_ref, q_ref, do_ref, sems):
+    fetches = [
+        pltpu.make_async_copy(whole, held, sems.at[index])
+        for index, (whole, held) in enumerate(((q_hbm, q_ref), (do_hbm, do_ref)))
+    ]
+    for fetch in fetches:
+        fetch.start()
     tiles, _, band = bias_ref.shape
     rows = tiles * TILE
     row = lax.broadcasted_iota(jnp.int32, (rows, 1), 0)
@@ -73,58 +79,48 @@
         key = lax.broadcasted_iota(jnp.int32, (TILE, band), 1) + (tile * TILE - 2 * rows)
         allowed = (key >= start[here]) & (key <= row[here])
         bias_ref[tile] = jnp.where(allowed, 0.0, NEVER)
-
-
-def masks(rows, lengths, first):
+    for fetch in fetches:
+        fetch.wait()
+
+
+def prepared(lengths, first, q, do):
+    rows = q.shape[0]
     smem = pl.BlockSpec(memory_space=pltpu.SMEM)
-    return pl.pallas_call(
-        functools.partial(mask_kernel, lengths.shape[0]),
-        in_specs=[smem, smem],
-        out_specs=pl.BlockSpec(memory_space=pltpu.VMEM),
-        out_shape=jax.ShapeDtypeStruct((rows // TILE, TILE, 2 * rows + TILE), jnp.float32),
+    far_away = pl.BlockSpec(memory_space=pltpu.HBM)
+    whole = pl.BlockSpec(memory_space=pltpu.VMEM)
+    return pl.pallas_call(
+        functools.partial(prepare_kernel, lengths.shape[0]),
+        in_specs=[smem, smem, far_away, far_away],
+        out_specs=[whole] * 3,
+        out_shape=[
+            jax.ShapeDtypeStruct((rows // TILE, TILE, 2 * rows + TILE), jnp.float32),
+            jax.ShapeDtypeStruct(q.shape, q.dtype),
+            jax.ShapeDtypeStruct(do.shape, do.dtype),
+        ],
+        scratch_shapes=[pltpu.SemaphoreType.DMA((2,))],
         compiler_params=pltpu.CompilerParams(vmem_limit_bytes=SMALL_LIMIT),
-        name="masks",
-    )(lengths, first)
+        name="prepare",
+    )(lengths, first, q, do)
 
 
 def lanes(block, width=HEAD_DIM):
     return pl.ds(pl.multiple_of(block * width, width), width)
 
 
-def attention_kernel(base, skipped, first_ref, bias, q_hbm, do_hbm, far, near, own, *refs):
-    o_ref, ds_ref, back_ref, own_ref, q_ref, do_ref, k_all, v_all, dk_sum, dv_sum, sems = refs
+def attention_kernel(base, skipped, first_ref, bias, q_ref, do_ref, far, near, own, *refs):
+    o_ref, ds_ref, back_ref, own_ref, k_all, v_all, dk_sum, dv_sum = refs
     group = pl.program_id(0)
     groups, tiles, _, _ = ds_ref.shape
     rows = far.shape[0]
     sent = far.shape[1] // (2 * HEAD_DIM)
-    wide = q_ref.shape[2]
+    wide = o_ref.shape[2]
     heads = wide // HEAD_DIM
     per_call = min(HEADS_AT_ONCE, heads)
-
-    def fetches(index):
-        span = pl.ds((base + index) * wide, wide)
-        return [
-            pltpu.make_async_copy(whole.at[:, span], held.at[index], sems.at[index, place])
-            for place, (whole, held) in enumerate(((q_hbm, q_ref), (do_hbm, do_ref)))
-        ]
-
-    @pl.when(group == 0)
-    def _():
-        for index in range(groups):
-            for fetch in fetches(index):
-                fetch.start()
-
     k_col = lanes(skipped + group)
     v_col = lanes(sent + skipped + group)
     for place, part in enumerate((far, near, own)):
         k_all[place * rows : (place + 1) * rows] = part[:, k_col]
         v_all[place * rows : (place + 1) * rows] = part[:, v_col]
-    for index in range(groups):
-
-        @pl.when(group == index)
-        def _():
-            for fetch in fetches(index):
-                fetch.wait()
 
     def all_units(lowest):
         dk_sum[...] = jnp.zeros_like(dk_sum)
@@ -140,7 +136,8 @@
 
         def stacked(ref, unit):
             here, _, cols = places(unit)
-            return jnp.concatenate([ref[group, here, c] for c in cols], 0)
+            first = (base + group) * heads
+            return jnp.concatenate([ref[here, lanes(first + c.start // HEAD_DIM)] for c in cols], 0)
 
         def scores(unit):
             return matmul(stacked(q_ref, unit), k_all[places(unit)[1]], NT)
@@ -210,11 +207,10 @@
     rows = q.shape[0]
     tiles, _, band = bias.shape
     whole = pl.BlockSpec(memory_space=pltpu.VMEM)
-    far_away = pl.BlockSpec(memory_space=pltpu.HBM)
     return pl.pallas_call(
         functools.partial(attention_kernel, base, skipped),
         grid=(groups,),
-        in_specs=[pl.BlockSpec(memory_space=pltpu.SMEM), whole, far_away, far_away, whole, whole, whole],
+        in_specs=[pl.BlockSpec(memory_space=pltpu.SMEM), whole, whole, whole, whole, whole, whole],
         out_specs=[whole] * 4,
         out_shape=[
             jax.ShapeDtypeStruct((groups, rows, head_cols), jnp.bfloat16),
@@ -223,13 +219,10 @@
             jax.ShapeDtypeStruct((2, rows, groups * HEAD_DIM), jnp.float32),
         ],
         scratch_shapes=[
-            pltpu.VMEM((groups, rows, head_cols), jnp.bfloat16),
-            pltpu.VMEM((groups, rows, head_cols), jnp.bfloat16),
             pltpu.VMEM((3 * rows, HEAD_DIM), jnp.bfloat16),
             pltpu.VMEM((3 * rows, HEAD_DIM), jnp.bfloat16),
             pltpu.VMEM((HEAD_DIM, 3 * rows), jnp.float32),
             pltpu.VMEM((HEAD_DIM, 3 * rows), jnp.float32),
-            pltpu.SemaphoreType.DMA((groups, 2)),
         ],
         compiler_params=pltpu.CompilerParams(vmem_limit_bytes=VMEM_LIMIT),
         name="attention",
@@ -237,42 +230,46 @@
 
 
 def query_kernel(calls, skips, *refs):
-    o_out, dq_out, k_all = refs[-3:]
-    group = pl.program_id(0)
-    rows = o_out.shape[0]
-    heads = o_out.shape[1] // HEAD_DIM
-    base = 0
-    for index, (size, skipped) in enumerate(zip(calls, skips)):
-        o_ref, ds_ref, far, near, own = refs[5 * index : 5 * index + 5]
-
-        @pl.when((group >= base) & (group < base + size))
-        def _(base=base, skipped=skipped, o_ref=o_ref, ds_ref=ds_ref, parts=(far, near, own)):
-            here = group - base
-            o_out[...] = o_ref[here]
-            for place, part in enumerate(parts):
-                k_all[place * rows : (place + 1) * rows] = part[:, lanes(skipped + here)]
-            for tile in range(ds_ref.shape[1]):
-                k = k_all[tile * TILE : tile * TILE + ds_ref.shape[3]]
-                dq = (matmul(ds_ref[here, tile], k, NN) * FACTOR).astype(jnp.bfloat16)
-                for x in range(heads):
-                    dq_out[tile * TILE : (tile + 1) * TILE, x * HEAD_DIM : (x + 1) * HEAD_DIM] = dq[
-                        x * TILE : (x + 1) * TILE
-                    ]
-
-        base += size
+    o_out, dq_out, k_all, held, sems = refs[-5:]
+    rows = held.shape[0]
+    wide = held.shape[1] // sum(calls)
+    groups = [(index, here) for index, size in enumerate(calls) for here in range(size)]
+    copies = []
+    for place, (index, here) in enumerate(groups):
+        cols = pl.ds(place * wide, wide)
+        copies.append(pltpu.make_async_copy(refs[5 * index].at[here], o_out.at[:, cols], sems.at[place, 0]))
+        copies[-1].start()
+    for place, (index, here) in enumerate(groups):
+        _, ds_ref, *parts = refs[5 * index : 5 * index + 5]
+        column = slice((skips[index] + here) * HEAD_DIM, (skips[index] + here + 1) * HEAD_DIM)
+        for spot, part in enumerate(parts):
+            k_all[spot * rows : (spot + 1) * rows] = part[:, column]
+        for tile in range(ds_ref.shape[1]):
+            k = k_all[tile * TILE : tile * TILE + ds_ref.shape[3]]
+            dq = (matmul(ds_ref[here, tile], k, NN) * FACTOR).astype(jnp.bfloat16)
+            for x in range(wide // HEAD_DIM):
+                start = place * wide + x * HEAD_DIM
+                held[tile * TILE : (tile + 1) * TILE, start : start + HEAD_DIM] = dq[x * TILE : (x + 1) * TILE]
+        cols = pl.ds(place * wide, wide)
+        copies.append(pltpu.make_async_copy(held.at[:, cols], dq_out.at[:, cols], sems.at[place, 1]))
+        copies[-1].start()
+    for copy in copies:
+        copy.wait()
 
 
 def query_grads(calls, skips, shape, parts):
     rows, width = shape
     flat = [array for part in parts for array in part]
-    out = pl.BlockSpec((rows, width // sum(calls)), lambda g: (0, g))
     return pl.pallas_call(
         functools.partial(query_kernel, calls, skips),
-        grid=(sum(calls),),
         in_specs=[pl.BlockSpec(memory_space=pltpu.VMEM)] * len(flat),
-        out_specs=[out, out],
+        out_specs=[pl.BlockSpec(memory_space=pltpu.HBM)] * 2,
         out_shape=[jax.ShapeDtypeStruct(shape, jnp.bfloat16)] * 2,
-        scratch_shapes=[pltpu.VMEM((3 * rows, HEAD_DIM), jnp.bfloat16)],
+        scratch_shapes=[
+            pltpu.VMEM((3 * rows, HEAD_DIM), jnp.bfloat16),
+            pltpu.VMEM(shape, jnp.bfloat16),
+            pltpu.SemaphoreType.DMA((sum(calls), 2)),
+        ],
         compiler_params=pltpu.CompilerParams(vmem_limit_bytes=QUERY_LIMIT),
         name="query_grads",
     )(*flat)
@@ -330,7 +327,7 @@
     q_here, do_here, k_here, v_here = (in_hbm(x) for x in (queries, grad_out, keys, values))
     own = list(packed(k_here, v_here, [b * HEAD_DIM for b in starts], [s * HEAD_DIM for s in sent]))
     far = [permuted(block, ahead) for block in own]
-    bias = masks(rows, episode_lengths, first)
+    bias, q_here, do_here = prepared(episode_lengths, first, q_here, do_here)
     own[0], bias = lax.optimization_barrier((own[0], bias))
     near = [permuted(jnp.where(odd == 1, there, here), swap) for there, here in zip(far, own)]
     grads = None

time: 50.7 us -> 49.9 us (0.984)
  Pallas kernels: 24 us -> 23.1 us
    pallas_call x2, Pallas kernels: 15.7 us -> 14 us  [attention(): pl.pallas_call(functools.partial(attention_kernel, base, skipped), grid=(...]
    pallas_call x2, Pallas kernels: 5.73 us -> 6.61 us  [the longest x1 3.83 us: query_grads(): pl.pallas_call(functools.partial(query_kernel, calls, skips), in_specs=[p...]
  transfers between devices with their start and end apart: 8 -> 8, of which waited for: 5 -> 5; matrix products, arithmetic and copies ran while one was open for 0% -> 0% of each run, Pallas kernels for 44% -> 43%
where the time goes in v4:
time: 49.9 us; the launch traced here: 49.8 us
  Pallas kernels  23.1 us (46%)
  waiting for transfers between devices  12.8 us (26%)
  starting transfers between devices  11.9 us (24%)
  between operations  0.92 us (2%)
  local copies, waits for them, and re-layouts  0.69 us (1%)
    pallas_call x2, Pallas kernels, attention(): pl.pallas_call(functools.partial(attention_kernel, base, skipped), grid=(...  14 us
    ppermute x8, waiting for transfers between devices, permuted(): return lax.ppermute(value, 'seq', pairs)  12.8 us
    ppermute x8, starting transfers between devices, permuted(): return lax.ppermute(value, 'seq', pairs)  11.9 us
    pallas_call x1, Pallas kernels, query_grads(): pl.pallas_call(functools.partial(query_kernel, calls, skips), in_specs=[p...  3.83 us
    pallas_call x1, Pallas kernels, prepared(): pl.pallas_call(functools.partial(prepare_kernel, lengths.shape[0]), in_sp...  2.78 us
    pallas_call x2, Pallas kernels, finished(): pl.pallas_call(functools.partial(finish_kernel, base, aliased), in_specs=...  1.48 us
    pallas_call x1, Pallas kernels, packed(): pl.pallas_call(functools.partial(pack_kernel, starts, sizes), grid=(1,),...  1.06 us
  transfers between devices with their start and end apart: 8, of which 5 were waited for; matrix products, arithmetic and copies ran while one was open for 0% of the time, Pallas kernels for 43%

profile of v4, /device:TPU:0, one launch (start us, length us, event | category | flops | bytes accessed | tf_op | source)
XLA Modules:
  0.0 49.8 jit_solution(16686989233721104966)
XLA Ops:
  0.6 1.1 %pack_keys_values.1 = (bf16[256,512]{1,0:T(8,128)(2,1)S(1)}, bf16[256,512]{1,0:T(8,128)(2,1)S(1)}) custom-call(bf16[256,512]{1,0:T(8,128)(2,1)} %k_ref.1, bf16[256,512]{1,0:T(8,128)(2,1)} %v_ref.1), custom_call_target="tpu_custom_call" | custom-call | tf_op jit(solution)/shard_map/pack_keys_values/pallas_call | solution.py:48
  1.7 3.0 %collective-permute-start = (bf16[256,512]{1,0:T(8,128)(2,1)S(1)}, bf16[256,512]{1,0:T(8,128)(2,1)S(1)}, u32[]{:S(2)}, u32[]{:S(2)}) collective-permute-start(bf16[256,512]{1,0:T(8,128)(2,1)S(1)} %get-tuple-element.32.own.refs_4_), channel_id=1, source_target_pairs={{0,2},{1,3},{2,4},{3,5},{4,6},{5,7},{6,8},{7,9},{8,10},{9,11},{10,... | collective-permute-start | bytes 786440 | tf_op jit(solution)/shard_map/ppermute | solution.py:33
  4.7 0.0 copy-start
  4.7 0.7 %copy-done = s32[16]{0:T(128)S(1)} copy-done((s32[16]{0:T(128)S(1)}, s32[16]{0:T(128)}, u32[]{:S(2)}) %copy-start) | copy-done | bytes 88
  5.4 2.8 %prepare.1 = (f32[2,128,640]{2,1,0:T(8,128)S(1)}, bf16[256,4096]{1,0:T(8,128)(2,1)S(1)}, bf16[256,4096]{1,0:T(8,128)(2,1)S(1)}) custom-call(s32[16]{0:T(128)S(1)} %copy-done, s32[1]{0:T(128)} %bitcast.first_ref, bf16[256,4096]{1,0:T(8,128)(2,1)} %q_hbm.1, bf16[256,4096]{1,0:T(8,128)(2,1)} %do_hbm.1), custom_call_target="tpu_custom_call" | custom-call | tf_op jit(solution)/shard_map/prepare/pallas_call | solution.py:91
  8.2 5.9 %collective-permute-done.far.refs_2_ = bf16[256,512]{1,0:T(8,128)(2,1)S(1)} collective-permute-done((bf16[256,512]{1,0:T(8,128)(2,1)S(1)}, bf16[256,512]{1,0:T(8,128)(2,1)S(1)}, u32[]{:S(2)}, u32[]{:S(2)}) %collective-permute-start) | collective-permute-done | bytes 262176 | tf_op jit(solution)/shard_map/ppermute | solution.py:33
  14.1 0.1 collective-permute-start.1
  14.2 0.1 collective-permute-start.2
  14.2 1.5 %collective-permute-done.1.near.refs_3_ = bf16[256,512]{1,0:T(8,128)(2,1)S(1)} collective-permute-done((bf16[256,512]{1,0:T(8,128)(2,1)S(1)}, bf16[256,512]{1,0:T(8,128)(2,1)S(1)}, u32[]{:S(2)}, u32[]{:S(2)}) %collective-permute-start.1) | collective-permute-done | bytes 262176 | tf_op jit(solution)/shard_map/ppermute | solution.py:33
  15.7 7.0 %attention.2 = (bf16[2,256,1024]{2,1,0:T(8,128)(2,1)S(1)}, bf16[2,2,1024,640]{3,2,1,0:T(8,128)(2,1)S(1)}, bf16[2,2,256,256]{3,2,1,0:T(8,128)(2,1)S(1)}, f32[2,256,256]{2,1,0:T(8,128)S(1)}) custom-call(s32[1]{0:T(128)} %bitcast.first_ref, f32[2,128,640]{2,1,0:T(8,128)S(1)} %get-tuple-element.29.bias, bf16[256,4096]{1,0:T(8,128)(2,1)S(1)} %get-tuple-element.30.q_ref, ...), custom_call_target="tpu_custom_call" | custom-call | tf_op jit(solution)/shard_map/attention/pallas_call | solution.py:210
  22.7 0.2 collective-permute-start.4
  22.9 2.7 %collective-permute-done.2.far.refs_7_ = bf16[256,512]{1,0:T(8,128)(2,1)S(1)} collective-permute-done((bf16[256,512]{1,0:T(8,128)(2,1)S(1)}, bf16[256,512]{1,0:T(8,128)(2,1)S(1)}, u32[]{:S(2)}, u32[]{:S(2)}) %collective-permute-start.2) | collective-permute-done | bytes 262176 | tf_op jit(solution)/shard_map/ppermute | solution.py:33
  25.6 0.1 collective-permute-start.3
  25.7 0.0 collective-permute-done.4
  25.7 0.1 fusion.1
  25.8 4.3 %collective-permute-start.5 = (bf16[2,256,256]{2,1,0:T(8,128)(2,1)S(1)}, bf16[2,256,256]{2,1,0:T(8,128)(2,1)S(1)}, u32[]{:S(2)}, u32[]{:S(2)}) collective-permute-start(bf16[2,256,256]{2,1,0:T(8,128)(2,1)S(1)} %get-tuple-element.52), channel_id=1, source_target_pairs={{2,0},{3,1},{4,2},{5,3},{6,4},{7,5},{8,6},{9,7},{10,8},{11,9},{12,... | collective-permute-start | bytes 786440 | tf_op jit(solution)/shard_map/ppermute | solution.py:33
  30.1 0.0 collective-permute-done.3.near.refs_8_
  30.1 7.0 %attention.3 = (bf16[2,256,1024]{2,1,0:T(8,128)(2,1)S(1)}, bf16[2,2,1024,640]{3,2,1,0:T(8,128)(2,1)S(1)}, bf16[2,2,256,256]{3,2,1,0:T(8,128)(2,1)S(1)}, f32[2,256,256]{2,1,0:T(8,128)S(1)}) custom-call(s32[1]{0:T(128)} %bitcast.first_ref, f32[2,128,640]{2,1,0:T(8,128)S(1)} %get-tuple-element.29.bias, bf16[256,4096]{1,0:T(8,128)(2,1)S(1)} %get-tuple-element.30.q_ref, ...), custom_call_target="tpu_custom_call" | custom-call | tf_op jit(solution)/shard_map/attention/pallas_call | solution.py:210
  37.1 0.0 collective-permute-done.5.refs_1_
  37.2 0.1 collective-permute-start.6
  37.2 1.5 %collective-permute-done.6 = bf16[2,256,256]{2,1,0:T(8,128)(2,1)S(1)} collective-permute-done((bf16[2,256,256]{2,1,0:T(8,128)(2,1)S(1)}, bf16[2,256,256]{2,1,0:T(8,128)(2,1)S(1)}, u32[]{:S(2)}, u32[]{:S(2)}) %collective-permute-start.6) | collective-permute-done | bytes 262176 | tf_op jit(solution)/shard_map/ppermute | solution.py:33
  38.8 0.1 fusion
  38.9 4.1 %collective-permute-start.7 = (bf16[2,256,256]{2,1,0:T(8,128)(2,1)S(1)}, bf16[2,256,256]{2,1,0:T(8,128)(2,1)S(1)}, u32[]{:S(2)}, u32[]{:S(2)}) collective-permute-start(bf16[2,256,256]{2,1,0:T(8,128)(2,1)S(1)} %get-tuple-element.50), channel_id=1, source_target_pairs={{2,0},{3,1},{4,2},{5,3},{6,4},{7,5},{8,6},{9,7},{10,8},{11,9},{12,... | collective-permute-start | bytes 786440 | tf_op jit(solution)/shard_map/ppermute | solution.py:33
  43.0 3.8 %query_grads.1 = (bf16[256,4096]{1,0:T(8,128)(2,1)}, bf16[256,4096]{1,0:T(8,128)(2,1)}) custom-call(bf16[2,256,1024]{2,1,0:T(8,128)(2,1)S(1)} %get-tuple-element.33.refs_0_, bf16[2,2,1024,640]{3,2,1,0:T(8,128)(2,1)S(1)} %get-tuple-element.34.refs_1_, bf16[256,512]{1,0:T(8,128)(2,1)S(1)} %collective-permute-done.far.refs_2_, ...), custom_call_target="tpu_custom_call" | custom-call | tf_op jit(solution)/shard_map/query_grads/pallas_call | solution.py:263
  46.8 0.7 %finish_keys_values.2 = (bf16[256,512]{1,0:T(8,128)(2,1)}, bf16[256,512]{1,0:T(8,128)(2,1)}) custom-call(f32[2,256,256]{2,1,0:T(8,128)S(1)} %get-tuple-element.53.refs_0_, bf16[2,256,256]{2,1,0:T(8,128)(2,1)S(1)} %collective-permute-done.5.refs_1_), custom_call_target="tpu_custom_call" | custom-call | tf_op jit(solution)/shard_map/finish_keys_values/pallas_call | solution.py:296
  47.6 1.3 %collective-permute-done.7.refs_3_ = bf16[2,256,256]{2,1,0:T(8,128)(2,1)S(1)} collective-permute-done((bf16[2,256,256]{2,1,0:T(8,128)(2,1)S(1)}, bf16[2,256,256]{2,1,0:T(8,128)(2,1)S(1)}, u32[]{:S(2)}, u32[]{:S(2)}) %collective-permute-start.7) | collective-permute-done | bytes 262176 | tf_op jit(solution)/shard_map/ppermute | solution.py:33
  48.9 0.7 %finish_keys_values.3 = (bf16[256,512]{1,0:T(8,128)(2,1)}, bf16[256,512]{1,0:T(8,128)(2,1)}) custom-call(bf16[256,512]{1,0:T(8,128)(2,1)} %get-tuple-element.44.refs_0_, bf16[256,512]{1,0:T(8,128)(2,1)} %get-tuple-element.45.refs_1_, f32[2,256,256]{2,1,0:T(8,128)S(1)} %get-tuple-element.51.refs_2_, ...), custom_call_target="tpu_custom_call", output_to_operand_aliasing={{0}: (0, {}), {1}: (1, {})} | custom-call | tf_op jit(solution)/shard_map/finish_keys_values/pallas_call | solution.py:296
  (4 shorter events, 0.1 us)
Async XLA Ops:
  1.7 12.4 %collective-permute-start = (bf16[256,512]{1,0:T(8,128)(2,1)S(1)}, bf16[256,512]{1,0:T(8,128)(2,1)S(1)}, u32[]{:S(2)}, u32[]{:S(2)}) collective-permute-start(bf16[256,512]{1,0:T(8,128)(2,1)S(1)} %get-tuple-element.32.own.refs_4_), channel_id=1, source_target_pairs={{0,2},{1,3},{2,4},{3,5},{4,6},{5,7},{6,8},{7,9},{8,10},{9,11},{10,... | collective-permute-start | bytes 786440 | tf_op jit(solution)/shard_map/ppermute | solution.py:33
  4.7 0.7 %copy-start = (s32[16]{0:T(128)S(1)}, s32[16]{0:T(128)}, u32[]{:S(2)}) copy-start(s32[16]{0:T(128)} %lengths_ref.1) | copy-start | bytes 196
  14.1 1.6 %collective-permute-start.1 = (bf16[256,512]{1,0:T(8,128)(2,1)S(1)}, bf16[256,512]{1,0:T(8,128)(2,1)S(1)}, u32[]{:S(2)}, u32[]{:S(2)}) collective-permute-start(bf16[256,512]{1,0:T(8,128)(2,1)S(1)} %broadcast_select_fusion.1), channel_id=1, source_target_pairs={{0,1},{1,0},{2,3},{3,2},{4,5},{5,4},{6,7},{7,6},{8,9},{9,8},{10,11... | collective-permute-start | bytes 786440 | tf_op jit(solution)/shard_map/ppermute | solution.py:33
  14.2 11.4 %collective-permute-start.2 = (bf16[256,512]{1,0:T(8,128)(2,1)S(1)}, bf16[256,512]{1,0:T(8,128)(2,1)S(1)}, u32[]{:S(2)}, u32[]{:S(2)}) collective-permute-start(bf16[256,512]{1,0:T(8,128)(2,1)S(1)} %get-tuple-element.35.own.refs_9_), channel_id=1, source_target_pairs={{0,2},{1,3},{2,4},{3,5},{4,6},{5,7},{6,8},{7,9},{8,10},{9,11},{10,... | collective-permute-start | bytes 786440 | tf_op jit(solution)/shard_map/ppermute | solution.py:33
  22.7 3.0 %collective-permute-start.4 = (bf16[2,256,256]{2,1,0:T(8,128)(2,1)S(1)}, bf16[2,256,256]{2,1,0:T(8,128)(2,1)S(1)}, u32[]{:S(2)}, u32[]{:S(2)}) collective-permute-start(bf16[2,256,256]{2,1,0:T(8,128)(2,1)S(1)} %slice_bitcast_fusion.1), channel_id=1, source_target_pairs={{0,1},{1,0},{2,3},{3,2},{4,5},{5,4},{6,7},{7,6},{8,9},{9,8},{10,11... | collective-permute-start | bytes 786440 | tf_op jit(solution)/shard_map/ppermute | solution.py:33
  25.6 4.5 %collective-permute-start.3 = (bf16[256,512]{1,0:T(8,128)(2,1)S(1)}, bf16[256,512]{1,0:T(8,128)(2,1)S(1)}, u32[]{:S(2)}, u32[]{:S(2)}) collective-permute-start(bf16[256,512]{1,0:T(8,128)(2,1)S(1)} %broadcast_select_fusion), channel_id=1, source_target_pairs={{0,1},{1,0},{2,3},{3,2},{4,5},{5,4},{6,7},{7,6},{8,9},{9,8},{10,11... | collective-permute-start | bytes 786440 | tf_op jit(solution)/shard_map/ppermute | solution.py:33
  25.8 11.3 %collective-permute-start.5 = (bf16[2,256,256]{2,1,0:T(8,128)(2,1)S(1)}, bf16[2,256,256]{2,1,0:T(8,128)(2,1)S(1)}, u32[]{:S(2)}, u32[]{:S(2)}) collective-permute-start(bf16[2,256,256]{2,1,0:T(8,128)(2,1)S(1)} %get-tuple-element.52), channel_id=1, source_target_pairs={{2,0},{3,1},{4,2},{5,3},{6,4},{7,5},{8,6},{9,7},{10,8},{11,9},{12,... | collective-permute-start | bytes 786440 | tf_op jit(solution)/shard_map/ppermute | solution.py:33
  37.2 1.6 %collective-permute-start.6 = (bf16[2,256,256]{2,1,0:T(8,128)(2,1)S(1)}, bf16[2,256,256]{2,1,0:T(8,128)(2,1)S(1)}, u32[]{:S(2)}, u32[]{:S(2)}) collective-permute-start(bf16[2,256,256]{2,1,0:T(8,128)(2,1)S(1)} %slice_bitcast_fusion), channel_id=1, source_target_pairs={{0,1},{1,0},{2,3},{3,2},{4,5},{5,4},{6,7},{7,6},{8,9},{9,8},{10,11... | collective-permute-start | bytes 786440 | tf_op jit(solution)/shard_map/ppermute | solution.py:33
  38.9 10.0 %collective-permute-start.7 = (bf16[2,256,256]{2,1,0:T(8,128)(2,1)S(1)}, bf16[2,256,256]{2,1,0:T(8,128)(2,1)S(1)}, u32[]{:S(2)}, u32[]{:S(2)}) collective-permute-start(bf16[2,256,256]{2,1,0:T(8,128)(2,1)S(1)} %get-tuple-element.50), channel_id=1, source_target_pairs={{2,0},{3,1},{4,2},{5,3},{6,4},{7,5},{8,6},{9,7},{10,8},{11,9},{12,... | collective-permute-start | bytes 786440 | tf_op jit(solution)/shard_map/ppermute | solution.py:33

commit v5 on v4

--- a/solution.py
+++ b/solution.py
@@ -11,9 +11,9 @@
 HEAD_DIM = 128
 TILE = 128
 HEADS_AT_ONCE = 4
-SENT = (2, 2)
-CALLS = (2, 2)
-RETURNED = (2, 2)
+SENT = (1, 3)
+CALLS = (1, 3)
+RETURNED = (1, 3)
 NT = (((1,), (1,)), ((), ()))
 NN = (((1,), (0,)), ((), ()))
 TN = (((0,), (0,)), ((), ()))
@@ -37,20 +37,26 @@
     return pltpu.with_memory_space_constraint(value, pltpu.HBM)
 
 
-def pack_kernel(starts, sizes, k_ref, v_ref, *outs):
-    for out, start, size in zip(outs, starts, sizes):
-        out[:, :size] = k_ref[:, start : start + size]
-        out[:, size:] = v_ref[:, start : start + size]
+def pack_kernel(starts, sizes, k_hbm, v_hbm, *refs):
+    outs, sems = refs[:-1], refs[-1]
+    copies = []
+    for index, (start, size) in enumerate(zip(starts, sizes)):
+        for place, whole in enumerate((k_hbm, v_hbm)):
+            held = outs[index].at[:, pl.ds(place * size, size)]
+            copies.append(pltpu.make_async_copy(whole.at[:, pl.ds(start, size)], held, sems.at[index, place]))
+            copies[-1].start()
+    for copy in copies:
+        copy.wait()
 
 
 def packed(keys, values, starts, sizes):
     rows = keys.shape[0]
     return pl.pallas_call(
         functools.partial(pack_kernel, starts, sizes),
-        grid=(1,),
-        in_specs=[pl.BlockSpec(keys.shape, lambda i: (0, 0))] * 2,
-        out_specs=[pl.BlockSpec((rows, 2 * size), lambda i: (0, 0)) for size in sizes],
+        in_specs=[pl.BlockSpec(memory_space=pltpu.HBM)] * 2,
+        out_specs=[pl.BlockSpec(memory_space=pltpu.VMEM)] * len(sizes),
         out_shape=[jax.ShapeDtypeStruct((rows, 2 * size), keys.dtype) for size in sizes],
+        scratch_shapes=[pltpu.SemaphoreType.DMA((len(sizes), 2))],
         compiler_params=pltpu.CompilerParams(vmem_limit_bytes=SMALL_LIMIT),
         name="pack_keys_values",
     )(keys, values)
@@ -151,7 +157,7 @@
             e = jnp.exp2(s - jnp.max(s, 1, keepdims=True))
             return e * (1.0 / jnp.sum(e, 1, keepdims=True))
 
-        def score_grads(unit, prob, weight):
+        def score_grads(unit, weight):
             here, keys, cols = places(unit)
             do = stacked(do_ref, unit)
             out = matmul(weight, v_all[keys], NN).astype(jnp.bfloat16)
@@ -159,7 +165,7 @@
                 o_ref[group, here, c] = out[x * TILE : (x + 1) * TILE]
             dp = matmul(do, v_all[keys], NT)
             delta = jnp.sum(out.astype(jnp.float32) * do.astype(jnp.float32), 1, keepdims=True)
-            ds = (prob * (dp - delta)).astype(jnp.bfloat16)
+            ds = weight * (dp - delta).astype(jnp.bfloat16)
             tile, first = unit
             ds_ref[group, tile, first * TILE : (first + per_call) * TILE, keys.start - tile * TILE :] = ds
             return ds
@@ -175,11 +181,10 @@
             now = ahead
             if index + 1 < len(units):
                 ahead = scores(units[index + 1])
-            prob = softmax(unit, now)
-            weight = prob.astype(jnp.bfloat16)
+            weight = softmax(unit, now).astype(jnp.bfloat16)
             if before is not None:
                 sums(*before)
-            before = (unit, weight, score_grads(unit, prob, weight))
+            before = (unit, weight, score_grads(unit, weight))
         sums(*before)
         if lowest:
             for tile in range(tiles):
@@ -325,7 +330,7 @@
     starts = [sum(sent[:index]) for index in range(len(sent))]
 
     q_here, do_here, k_here, v_here = (in_hbm(x) for x in (queries, grad_out, keys, values))
-    own = list(packed(k_here, v_here, [b * HEAD_DIM for b in starts], [s * HEAD_DIM for s in sent]))
+    own = list(packed(k_here, v_here, [start * HEAD_DIM for start in starts], [size * HEAD_DIM for size in sent]))
     far = [permuted(block, ahead) for block in own]
     bias, q_here, do_here = prepared(episode_lengths, first, q_here, do_here)
     own[0], bias = lax.optimization_barrier((own[0], bias))

time: 49.9 us -> 48.4 us (0.970)
  waiting for transfers between devices: 12.8 us -> 12 us
    ppermute x8, waiting for transfers between devices: 12.8 us -> 12 us  [permuted(): return lax.ppermute(value, 'seq', pairs)]
where the time goes in v5:
time: 48.4 us; the launch traced here: 48.3 us
  Pallas kernels  22.7 us (47%)
  waiting for transfers between devices  12 us (25%)
  starting transfers between devices  11.6 us (24%)
  between operations  0.91 us (2%)
  local copies, waits for them, and re-layouts  0.71 us (1%)
    pallas_call x2, Pallas kernels, attention(): pl.pallas_call(functools.partial(attention_kernel, base, skipped), grid=(...  13.5 us
    ppermute x8, waiting for transfers between devices, permuted(): return lax.ppermute(value, 'seq', pairs)  12 us
    ppermute x8, starting transfers between devices, permuted(): return lax.ppermute(value, 'seq', pairs)  11.6 us
    pallas_call x1, Pallas kernels, query_grads(): pl.pallas_call(functools.partial(query_kernel, calls, skips), in_specs=[p...  3.84 us
    pallas_call x1, Pallas kernels, prepared(): pl.pallas_call(functools.partial(prepare_kernel, lengths.shape[0]), in_sp...  2.78 us
    pallas_call x2, Pallas kernels, finished(): pl.pallas_call(functools.partial(finish_kernel, base, aliased), in_specs=...  1.47 us
    pallas_call x1, Pallas kernels, packed(): pl.pallas_call(functools.partial(pack_kernel, starts, sizes), in_specs=[p...  1.13 us
  transfers between devices with their start and end apart: 8, of which 5 were waited for; matrix products, arithmetic and copies ran while one was open for 0% of the time, Pallas kernels for 43%

profile of v5, /device:TPU:0, one launch (start us, length us, event | category | flops | bytes accessed | tf_op | source)
XLA Modules:
  0.0 48.3 jit_solution(15455211997246690018)
XLA Ops:
  0.6 1.1 %pack_keys_values.1 = (bf16[256,256]{1,0:T(8,128)(2,1)S(1)}, bf16[256,768]{1,0:T(8,128)(2,1)S(1)}) custom-call(bf16[256,512]{1,0:T(8,128)(2,1)} %k_hbm.1, bf16[256,512]{1,0:T(8,128)(2,1)} %v_hbm.1), custom_call_target="tpu_custom_call" | custom-call | tf_op jit(solution)/shard_map/pack_keys_values/pallas_call | solution.py:54
  1.8 3.0 %collective-permute-start = (bf16[256,256]{1,0:T(8,128)(2,1)S(1)}, bf16[256,256]{1,0:T(8,128)(2,1)S(1)}, u32[]{:S(2)}, u32[]{:S(2)}) collective-permute-start(bf16[256,256]{1,0:T(8,128)(2,1)S(1)} %get-tuple-element.32.own.refs_4_), channel_id=1, source_target_pairs={{0,2},{1,3},{2,4},{3,5},{4,6},{5,7},{6,8},{7,9},{8,10},{9,11},{10,... | collective-permute-start | bytes 393224 | tf_op jit(solution)/shard_map/ppermute | solution.py:33
  4.8 1.5 %collective-permute-start.2 = (bf16[256,768]{1,0:T(8,128)(2,1)S(1)}, bf16[256,768]{1,0:T(8,128)(2,1)S(1)}, u32[]{:S(2)}, u32[]{:S(2)}) collective-permute-start(bf16[256,768]{1,0:T(8,128)(2,1)S(1)} %get-tuple-element.35.own.refs_9_), channel_id=1, source_target_pairs={{0,2},{1,3},{2,4},{3,5},{4,6},{5,7},{6,8},{7,9},{8,10},{9,11},{10,... | collective-permute-start | bytes 1179656 | tf_op jit(solution)/shard_map/ppermute | solution.py:33
  6.3 0.0 copy-start
  6.3 0.7 %copy-done = s32[16]{0:T(128)S(1)} copy-done((s32[16]{0:T(128)S(1)}, s32[16]{0:T(128)}, u32[]{:S(2)}) %copy-start) | copy-done | bytes 88
  7.0 2.8 %prepare.1 = (f32[2,128,640]{2,1,0:T(8,128)S(1)}, bf16[256,4096]{1,0:T(8,128)(2,1)S(1)}, bf16[256,4096]{1,0:T(8,128)(2,1)S(1)}) custom-call(s32[16]{0:T(128)S(1)} %copy-done, s32[1]{0:T(128)} %bitcast.first_ref, bf16[256,4096]{1,0:T(8,128)(2,1)} %q_hbm.1, bf16[256,4096]{1,0:T(8,128)(2,1)} %do_hbm.1), custom_call_target="tpu_custom_call" | custom-call | tf_op jit(solution)/shard_map/prepare/pallas_call | solution.py:97
  9.8 2.4 %collective-permute-done.far.refs_2_ = bf16[256,256]{1,0:T(8,128)(2,1)S(1)} collective-permute-done((bf16[256,256]{1,0:T(8,128)(2,1)S(1)}, bf16[256,256]{1,0:T(8,128)(2,1)S(1)}, u32[]{:S(2)}, u32[]{:S(2)}) %collective-permute-start) | collective-permute-done | bytes 131104 | tf_op jit(solution)/shard_map/ppermute | solution.py:33
  12.2 0.1 collective-permute-start.1
  12.2 1.3 %collective-permute-done.1.near.refs_3_ = bf16[256,256]{1,0:T(8,128)(2,1)S(1)} collective-permute-done((bf16[256,256]{1,0:T(8,128)(2,1)S(1)}, bf16[256,256]{1,0:T(8,128)(2,1)S(1)}, u32[]{:S(2)}, u32[]{:S(2)}) %collective-permute-start.1) | collective-permute-done | bytes 131104 | tf_op jit(solution)/shard_map/ppermute | solution.py:33
  13.6 3.3 %attention.2 = (bf16[1,256,1024]{2,1,0:T(8,128)(2,1)S(1)}, bf16[1,2,1024,640]{3,2,1,0:T(8,128)(2,1)S(1)}, bf16[2,2,256,128]{3,2,1,0:T(8,128)(2,1)S(1)}, f32[2,256,128]{2,1,0:T(8,128)S(1)}) custom-call(s32[1]{0:T(128)} %bitcast.first_ref, f32[2,128,640]{2,1,0:T(8,128)S(1)} %get-tuple-element.29.bias, bf16[256,4096]{1,0:T(8,128)(2,1)S(1)} %get-tuple-element.30.q_ref, ...), custom_call_target="tpu_custom_call" | custom-call | tf_op jit(solution)/shard_map/attention/pallas_call | solution.py:215
  17.0 0.2 collective-permute-start.4
  17.2 2.6 %collective-permute-done.2.far.refs_7_ = bf16[256,768]{1,0:T(8,128)(2,1)S(1)} collective-permute-done((bf16[256,768]{1,0:T(8,128)(2,1)S(1)}, bf16[256,768]{1,0:T(8,128)(2,1)S(1)}, u32[]{:S(2)}, u32[]{:S(2)}) %collective-permute-start.2) | collective-permute-done | bytes 393248 | tf_op jit(solution)/shard_map/ppermute | solution.py:33
  19.8 0.1 collective-permute-start.3
  19.9 0.0 collective-permute-done.4
  19.9 0.1 fusion.1
  20.0 2.0 %collective-permute-start.5 = (bf16[2,256,128]{2,1,0:T(8,128)(2,1)S(1)}, bf16[2,256,128]{2,1,0:T(8,128)(2,1)S(1)}, u32[]{:S(2)}, u32[]{:S(2)}) collective-permute-start(bf16[2,256,128]{2,1,0:T(8,128)(2,1)S(1)} %get-tuple-element.52), channel_id=1, source_target_pairs={{2,0},{3,1},{4,2},{5,3},{6,4},{7,5},{8,6},{9,7},{10,8},{11,9},{12,... | collective-permute-start | bytes 393224 | tf_op jit(solution)/shard_map/ppermute | solution.py:33
  21.9 0.0 collective-permute-done.3.near.refs_8_
  21.9 10.1 %attention.3 = (bf16[3,256,1024]{2,1,0:T(8,128)(2,1)S(1)}, bf16[3,2,1024,640]{3,2,1,0:T(8,128)(2,1)S(1)}, bf16[2,2,256,384]{3,2,1,0:T(8,128)(2,1)S(1)}, f32[2,256,384]{2,1,0:T(8,128)S(1)}) custom-call(s32[1]{0:T(128)} %bitcast.first_ref, f32[2,128,640]{2,1,0:T(8,128)S(1)} %get-tuple-element.29.bias, bf16[256,4096]{1,0:T(8,128)(2,1)S(1)} %get-tuple-element.30.q_ref, ...), custom_call_target="tpu_custom_call" | custom-call | tf_op jit(solution)/shard_map/attention/pallas_call | solution.py:215
  32.1 0.0 collective-permute-done.5.refs_1_
  32.1 0.3 collective-permute-start.6
  32.4 1.5 %collective-permute-done.6 = bf16[2,256,384]{2,1,0:T(8,128)(2,1)S(1)} collective-permute-done((bf16[2,256,384]{2,1,0:T(8,128)(2,1)S(1)}, bf16[2,256,384]{2,1,0:T(8,128)(2,1)S(1)}, u32[]{:S(2)}, u32[]{:S(2)}) %collective-permute-start.6) | collective-permute-done | bytes 393248 | tf_op jit(solution)/shard_map/ppermute | solution.py:33
  33.9 0.2 fusion
  34.1 4.5 %collective-permute-start.7 = (bf16[2,256,384]{2,1,0:T(8,128)(2,1)S(1)}, bf16[2,256,384]{2,1,0:T(8,128)(2,1)S(1)}, u32[]{:S(2)}, u32[]{:S(2)}) collective-permute-start(bf16[2,256,384]{2,1,0:T(8,128)(2,1)S(1)} %get-tuple-element.50), channel_id=1, source_target_pairs={{2,0},{3,1},{4,2},{5,3},{6,4},{7,5},{8,6},{9,7},{10,8},{11,9},{12,... | collective-permute-start | bytes 1179656 | tf_op jit(solution)/shard_map/ppermute | solution.py:33
  38.6 0.7 %finish_keys_values.2 = (bf16[256,512]{1,0:T(8,128)(2,1)}, bf16[256,512]{1,0:T(8,128)(2,1)}) custom-call(f32[2,256,128]{2,1,0:T(8,128)S(1)} %get-tuple-element.53.refs_0_, bf16[2,256,128]{2,1,0:T(8,128)(2,1)S(1)} %collective-permute-done.5.refs_1_), custom_call_target="tpu_custom_call" | custom-call | tf_op jit(solution)/shard_map/finish_keys_values/pallas_call | solution.py:301
  39.3 3.8 %query_grads.1 = (bf16[256,4096]{1,0:T(8,128)(2,1)}, bf16[256,4096]{1,0:T(8,128)(2,1)}) custom-call(bf16[1,256,1024]{2,1,0:T(8,128)(2,1)S(1)} %get-tuple-element.33.refs_0_, bf16[1,2,1024,640]{3,2,1,0:T(8,128)(2,1)S(1)} %get-tuple-element.34.refs_1_, bf16[256,256]{1,0:T(8,128)(2,1)S(1)} %collective-permute-done.far.refs_2_, ...), custom_call_target="tpu_custom_call" | custom-call | tf_op jit(solution)/shard_map/query_grads/pallas_call | solution.py:268
  43.1 4.2 %collective-permute-done.7.refs_3_ = bf16[2,256,384]{2,1,0:T(8,128)(2,1)S(1)} collective-permute-done((bf16[2,256,384]{2,1,0:T(8,128)(2,1)S(1)}, bf16[2,256,384]{2,1,0:T(8,128)(2,1)S(1)}, u32[]{:S(2)}, u32[]{:S(2)}) %collective-permute-start.7) | collective-permute-done | bytes 393248 | tf_op jit(solution)/shard_map/ppermute | solution.py:33
  47.3 0.8 %finish_keys_values.3 = (bf16[256,512]{1,0:T(8,128)(2,1)}, bf16[256,512]{1,0:T(8,128)(2,1)}) custom-call(bf16[256,512]{1,0:T(8,128)(2,1)} %get-tuple-element.44.refs_0_, bf16[256,512]{1,0:T(8,128)(2,1)} %get-tuple-element.45.refs_1_, f32[2,256,384]{2,1,0:T(8,128)S(1)} %get-tuple-element.51.refs_2_, ...), custom_call_target="tpu_custom_call", output_to_operand_aliasing={{0}: (0, {}), {1}: (1, {})} | custom-call | tf_op jit(solution)/shard_map/finish_keys_values/pallas_call | solution.py:301
  (4 shorter events, 0.1 us)
Async XLA Ops:
  1.8 10.4 %collective-permute-start = (bf16[256,256]{1,0:T(8,128)(2,1)S(1)}, bf16[256,256]{1,0:T(8,128)(2,1)S(1)}, u32[]{:S(2)}, u32[]{:S(2)}) collective-permute-start(bf16[256,256]{1,0:T(8,128)(2,1)S(1)} %get-tuple-element.32.own.refs_4_), channel_id=1, source_target_pairs={{0,2},{1,3},{2,4},{3,5},{4,6},{5,7},{6,8},{7,9},{8,10},{9,11},{10,... | collective-permute-start | bytes 393224 | tf_op jit(solution)/shard_map/ppermute | solution.py:33
  4.8 15.0 %collective-permute-start.2 = (bf16[256,768]{1,0:T(8,128)(2,1)S(1)}, bf16[256,768]{1,0:T(8,128)(2,1)S(1)}, u32[]{:S(2)}, u32[]{:S(2)}) collective-permute-start(bf16[256,768]{1,0:T(8,128)(2,1)S(1)} %get-tuple-element.35.own.refs_9_), channel_id=1, source_target_pairs={{0,2},{1,3},{2,4},{3,5},{4,6},{5,7},{6,8},{7,9},{8,10},{9,11},{10,... | collective-permute-start | bytes 1179656 | tf_op jit(solution)/shard_map/ppermute | solution.py:33
  6.3 0.7 %copy-start = (s32[16]{0:T(128)S(1)}, s32[16]{0:T(128)}, u32[]{:S(2)}) copy-start(s32[16]{0:T(128)} %lengths_ref.1) | copy-start | bytes 196
  12.2 1.4 %collective-permute-start.1 = (bf16[256,256]{1,0:T(8,128)(2,1)S(1)}, bf16[256,256]{1,0:T(8,128)(2,1)S(1)}, u32[]{:S(2)}, u32[]{:S(2)}) collective-permute-start(bf16[256,256]{1,0:T(8,128)(2,1)S(1)} %broadcast_select_fusion.1), channel_id=1, source_target_pairs={{0,1},{1,0},{2,3},{3,2},{4,5},{5,4},{6,7},{7,6},{8,9},{9,8},{10,11... | collective-permute-start | bytes 393224 | tf_op jit(solution)/shard_map/ppermute | solution.py:33
  17.0 2.9 %collective-permute-start.4 = (bf16[2,256,128]{2,1,0:T(8,128)(2,1)S(1)}, bf16[2,256,128]{2,1,0:T(8,128)(2,1)S(1)}, u32[]{:S(2)}, u32[]{:S(2)}) collective-permute-start(bf16[2,256,128]{2,1,0:T(8,128)(2,1)S(1)} %slice_bitcast_fusion.1), channel_id=1, source_target_pairs={{0,1},{1,0},{2,3},{3,2},{4,5},{5,4},{6,7},{7,6},{8,9},{9,8},{10,11... | collective-permute-start | bytes 393224 | tf_op jit(solution)/shard_map/ppermute | solution.py:33
  19.8 2.1 %collective-permute-start.3 = (bf16[256,768]{1,0:T(8,128)(2,1)S(1)}, bf16[256,768]{1,0:T(8,128)(2,1)S(1)}, u32[]{:S(2)}, u32[]{:S(2)}) collective-permute-start(bf16[256,768]{1,0:T(8,128)(2,1)S(1)} %broadcast_select_fusion), channel_id=1, source_target_pairs={{0,1},{1,0},{2,3},{3,2},{4,5},{5,4},{6,7},{7,6},{8,9},{9,8},{10,11... | collective-permute-start | bytes 1179656 | tf_op jit(solution)/shard_map/ppermute | solution.py:33
  20.0 12.1 %collective-permute-start.5 = (bf16[2,256,128]{2,1,0:T(8,128)(2,1)S(1)}, bf16[2,256,128]{2,1,0:T(8,128)(2,1)S(1)}, u32[]{:S(2)}, u32[]{:S(2)}) collective-permute-start(bf16[2,256,128]{2,1,0:T(8,128)(2,1)S(1)} %get-tuple-element.52), channel_id=1, source_target_pairs={{2,0},{3,1},{4,2},{5,3},{6,4},{7,5},{8,6},{9,7},{10,8},{11,9},{12,... | collective-permute-start | bytes 393224 | tf_op jit(solution)/shard_map/ppermute | solution.py:33
  32.1 1.8 %collective-permute-start.6 = (bf16[2,256,384]{2,1,0:T(8,128)(2,1)S(1)}, bf16[2,256,384]{2,1,0:T(8,128)(2,1)S(1)}, u32[]{:S(2)}, u32[]{:S(2)}) collective-permute-start(bf16[2,256,384]{2,1,0:T(8,128)(2,1)S(1)} %slice_bitcast_fusion), channel_id=1, source_target_pairs={{0,1},{1,0},{2,3},{3,2},{4,5},{5,4},{6,7},{7,6},{8,9},{9,8},{10,11... | collective-permute-start | bytes 1179656 | tf_op jit(solution)/shard_map/ppermute | solution.py:33
  34.1 13.2 %collective-permute-start.7 = (bf16[2,256,384]{2,1,0:T(8,128)(2,1)S(1)}, bf16[2,256,384]{2,1,0:T(8,128)(2,1)S(1)}, u32[]{:S(2)}, u32[]{:S(2)}) collective-permute-start(bf16[2,256,384]{2,1,0:T(8,128)(2,1)S(1)} %get-tuple-element.50), channel_id=1, source_target_pairs={{2,0},{3,1},{4,2},{5,3},{6,4},{7,5},{8,6},{9,7},{10,8},{11,9},{12,... | collective-permute-start | bytes 1179656 | tf_op jit(solution)/shard_map/ppermute | solution.py:33

commit v6 on v5

--- a/solution.py
+++ b/solution.py
@@ -63,8 +63,9 @@
 
 
 def prepare_kernel(count, lengths_ref, first_ref, q_hbm, do_hbm, bias_ref, q_ref, do_ref, sems):
+    span = pl.ds(0, q_ref.shape[1])
     fetches = [
-        pltpu.make_async_copy(whole, held, sems.at[index])
+        pltpu.make_async_copy(whole.at[:, span], held, sems.at[index])
         for index, (whole, held) in enumerate(((q_hbm, q_ref), (do_hbm, do_ref)))
     ]
     for fetch in fetches:
@@ -89,7 +90,7 @@
         fetch.wait()
 
 
-def prepared(lengths, first, q, do):
+def prepared(lengths, first, q, do, width):
     rows = q.shape[0]
     smem = pl.BlockSpec(memory_space=pltpu.SMEM)
     far_away = pl.BlockSpec(memory_space=pltpu.HBM)
@@ -100,8 +101,8 @@
         out_specs=[whole] * 3,
         out_shape=[
             jax.ShapeDtypeStruct((rows // TILE, TILE, 2 * rows + TILE), jnp.float32),
-            jax.ShapeDtypeStruct(q.shape, q.dtype),
-            jax.ShapeDtypeStruct(do.shape, do.dtype),
+            jax.ShapeDtypeStruct((rows, width), q.dtype),
+            jax.ShapeDtypeStruct((rows, width), do.dtype),
         ],
         scratch_shapes=[pltpu.SemaphoreType.DMA((2,))],
         compiler_params=pltpu.CompilerParams(vmem_limit_bytes=SMALL_LIMIT),
@@ -113,7 +114,15 @@
     return pl.ds(pl.multiple_of(block * width, width), width)
 
 
-def attention_kernel(base, skipped, first_ref, bias, q_ref, do_ref, far, near, own, *refs):
+def attention_kernel(base, skipped, fetching, first_ref, bias, q_ref, do_ref, far, near, own, *refs):
+    fetches = []
+    if fetching:
+        q_hbm, do_hbm, *refs, sems = refs
+        q_rest, do_rest = refs[4:6]
+        refs = refs[:4] + refs[6:]
+        span = pl.ds(q_ref.shape[1], q_rest.shape[1])
+        for index, (whole, held) in enumerate(((q_hbm, q_rest), (do_hbm, do_rest))):
+            fetches.append(pltpu.make_async_copy(whole.at[:, span], held, sems.at[index]))
     o_ref, ds_ref, back_ref, own_ref, k_all, v_all, dk_sum, dv_sum = refs
     group = pl.program_id(0)
     groups, tiles, _, _ = ds_ref.shape
@@ -122,6 +131,11 @@
     wide = o_ref.shape[2]
     heads = wide // HEAD_DIM
     per_call = min(HEADS_AT_ONCE, heads)
+    @pl.when(group == 0)
+    def _():
+        for fetch in fetches:
+            fetch.start()
+
     k_col = lanes(skipped + group)
     v_col = lanes(sent + skipped + group)
     for place, part in enumerate((far, near, own)):
@@ -207,31 +221,41 @@
     def _():
         all_units(rows)
 
-
-def attention(base, groups, skipped, head_cols, first, bias, q, do, far, near, own):
+    @pl.when(group == groups - 1)
+    def _():
+        for fetch in fetches:
+            fetch.wait()
+
+
+def attention(base, groups, skipped, head_cols, first, bias, q, do, far, near, own, whole_q=None, whole_do=None):
     rows = q.shape[0]
     tiles, _, band = bias.shape
     whole = pl.BlockSpec(memory_space=pltpu.VMEM)
+    fetching = whole_q is not None
+    far_away = pl.BlockSpec(memory_space=pltpu.HBM)
+    rest = (rows, whole_q.shape[1] - q.shape[1] if fetching else 0)
     return pl.pallas_call(
-        functools.partial(attention_kernel, base, skipped),
+        functools.partial(attention_kernel, base, skipped, fetching),
         grid=(groups,),
-        in_specs=[pl.BlockSpec(memory_space=pltpu.SMEM), whole, whole, whole, whole, whole, whole],
-        out_specs=[whole] * 4,
+        in_specs=[pl.BlockSpec(memory_space=pltpu.SMEM), whole, whole, whole, whole, whole, whole] + [far_away, far_away] * fetching,
+        out_specs=[whole] * (6 if fetching else 4),
         out_shape=[
             jax.ShapeDtypeStruct((groups, rows, head_cols), jnp.bfloat16),
             jax.ShapeDtypeStruct((groups, tiles, head_cols // HEAD_DIM * TILE, band), jnp.bfloat16),
             jax.ShapeDtypeStruct((2, 2, rows, groups * HEAD_DIM), jnp.bfloat16),
             jax.ShapeDtypeStruct((2, rows, groups * HEAD_DIM), jnp.float32),
-        ],
+        ]
+        + [jax.ShapeDtypeStruct(rest, q.dtype)] * (2 if fetching else 0),
         scratch_shapes=[
             pltpu.VMEM((3 * rows, HEAD_DIM), jnp.bfloat16),
             pltpu.VMEM((3 * rows, HEAD_DIM), jnp.bfloat16),
             pltpu.VMEM((HEAD_DIM, 3 * rows), jnp.float32),
             pltpu.VMEM((HEAD_DIM, 3 * rows), jnp.float32),
-        ],
+        ]
+        + [pltpu.SemaphoreType.DMA((2,))] * fetching,
         compiler_params=pltpu.CompilerParams(vmem_limit_bytes=VMEM_LIMIT),
         name="attention",
-    )(first, bias, q, do, far, near, own)
+    )(first, bias, q, do, far, near, own, *((whole_q, whole_do) if fetching else ()))
 
 
 def query_kernel(calls, skips, *refs):
@@ -322,6 +346,8 @@
     first = jnp.reshape(place * rows, (1,))
     ahead = [(source, (source + 2) % count) for source in range(count)]
     behind = [((source + 2) % count, source) for source in range(count)]
+    ahead_open = ahead[: count - 2]
+    behind_open = behind[: count - 2]
     swap = [(source, source ^ 1) for source in range(count)]
     known = groups == sum(SENT)
     sent = SENT if known else (groups,)
@@ -331,10 +357,11 @@
 
     q_here, do_here, k_here, v_here = (in_hbm(x) for x in (queries, grad_out, keys, values))
     own = list(packed(k_here, v_here, [start * HEAD_DIM for start in starts], [size * HEAD_DIM for size in sent]))
-    far = [permuted(block, ahead) for block in own]
-    bias, q_here, do_here = prepared(episode_lengths, first, q_here, do_here)
+    far = [permuted(block, ahead_open if index else ahead) for index, block in enumerate(own)]
+    head_cols = queries.shape[1] // groups
+    bias, q_part, do_part = prepared(episode_lengths, first, q_here, do_here, calls[0] * head_cols)
     own[0], bias = lax.optimization_barrier((own[0], bias))
-    near = [permuted(jnp.where(odd == 1, there, here), swap) for there, here in zip(far, own)]
+    near = []
     grads = None
     parts = []
     waiting = []
@@ -344,9 +371,20 @@
     for size in calls:
         chunk = max(index for index, start in enumerate(starts) if start <= base)
         skips.append(base - starts[chunk])
-        out, ds, back, kept = attention(
-            base, size, skips[-1], queries.shape[1] // groups, first, bias, q_here, do_here, far[chunk], near[chunk], own[chunk]
-        )
+        if chunk == len(near):
+            there = far[chunk]
+            if stored:
+                there, ds = lax.optimization_barrier((there, stored[-1][1]))
+                stored[-1] = (stored[-1][0], ds) + stored[-1][2:]
+            near.append(permuted(jnp.where(odd == 1, there, own[chunk]), swap))
+        if base == 0 and size < groups:
+            out, ds, back, kept, q_part, do_part = attention(
+                0, size, skips[-1], head_cols, first, bias, q_part, do_part, far[chunk], near[chunk], own[chunk], q_here, do_here
+            )
+        else:
+            out, ds, back, kept = attention(
+                base - (calls[0] if base else 0), size, skips[-1], head_cols, first, bias, q_part, do_part, far[chunk], near[chunk], own[chunk]
+            )
         stored.append((out, ds, far[chunk], near[chunk], own[chunk]))
         waiting.append((back, kept))
         base += size
@@ -361,7 +399,7 @@
         none = jnp.zeros_like(beside)
         onward = back[0].astype(jnp.float32) + jnp.where(odd == 1, beside, none).astype(jnp.float32)
         kept = kept + jnp.where(odd == 1, none, beside).astype(jnp.float32)
-        parts.append([begun, kept, permuted(onward.astype(jnp.bfloat16), behind)])
+        parts.append([begun, kept, permuted(onward.astype(jnp.bfloat16), behind_open if parts else behind)])
         begun = base
     attn_out, grad_queries = query_grads(calls, skips, queries.shape, stored)
     for begun, kept, returned in parts:

time: 48.4 us -> 48.2 us (level)
  starting transfers between devices: 11.6 us -> 13.1 us
  Pallas kernels: 22.7 us -> 21.4 us
  waiting for transfers between devices: 12 us -> 11.5 us
    ppermute x8, starting transfers between devices: 11.6 us -> 13.1 us  [permuted(): return lax.ppermute(value, 'seq', pairs)]
    pallas_call x1, Pallas kernels: 2.78 us -> 1.81 us  [prepared(): pl.pallas_call(functools.partial(prepare_kernel, lengths.shape[0]), in_sp...]
    ppermute x8, waiting for transfers between devices: 12 us -> 11.5 us  [permuted(): return lax.ppermute(value, 'seq', pairs)]
  transfers between devices with their start and end apart: 8 -> 8, of which waited for: 5 -> 6; matrix products, arithmetic and copies ran while one was open for 0% -> 0% of each run, Pallas kernels for 43% -> 41%
where the time goes in v6:
time: 48.2 us; the launch traced here: 48 us
  Pallas kernels  21.4 us (44%)
  starting transfers between devices  13.1 us (27%)
  waiting for transfers between devices  11.5 us (24%)
  between operations  0.93 us (2%)
  local copies, waits for them, and re-layouts  0.7 us (1%)
    pallas_call x2, Pallas kernels, attention(): pl.pallas_call(functools.partial(attention_kernel, base, skipped, fetchin...  13.2 us
    ppermute x8, starting transfers between devices, permuted(): return lax.ppermute(value, 'seq', pairs)  13.1 us
    ppermute x8, waiting for transfers between devices, permuted(): return lax.ppermute(value, 'seq', pairs)  11.5 us
    pallas_call x1, Pallas kernels, query_grads(): pl.pallas_call(functools.partial(query_kernel, calls, skips), in_specs=[p...  3.84 us
    pallas_call x1, Pallas kernels, prepared(): pl.pallas_call(functools.partial(prepare_kernel, lengths.shape[0]), in_sp...  1.81 us
    pallas_call x2, Pallas kernels, finished(): pl.pallas_call(functools.partial(finish_kernel, base, aliased), in_specs=...  1.48 us
    pallas_call x1, Pallas kernels, packed(): pl.pallas_call(functools.partial(pack_kernel, starts, sizes), in_specs=[p...  1.13 us
  transfers between devices with their start and end apart: 8, of which 6 were waited for; matrix products, arithmetic and copies ran while one was open for 0% of the time, Pallas kernels for 41%

profile of v6, /device:TPU:0, one launch (start us, length us, event | category | flops | bytes accessed | tf_op | source)
XLA Modules:
  0.0 48.0 jit_solution(16689628728345341020)
XLA Ops:
  0.6 1.1 %pack_keys_values.1 = (bf16[256,256]{1,0:T(8,128)(2,1)S(1)}, bf16[256,768]{1,0:T(8,128)(2,1)S(1)}) custom-call(bf16[256,512]{1,0:T(8,128)(2,1)} %k_hbm.1, bf16[256,512]{1,0:T(8,128)(2,1)} %v_hbm.1), custom_call_target="tpu_custom_call" | custom-call | tf_op jit(solution)/shard_map/pack_keys_values/pallas_call | solution.py:54
  1.8 3.0 %collective-permute-start = (bf16[256,256]{1,0:T(8,128)(2,1)S(1)}, bf16[256,256]{1,0:T(8,128)(2,1)S(1)}, u32[]{:S(2)}, u32[]{:S(2)}) collective-permute-start(bf16[256,256]{1,0:T(8,128)(2,1)S(1)} %get-tuple-element.36.own.refs_4_), channel_id=1, source_target_pairs={{0,2},{1,3},{2,4},{3,5},{4,6},{5,7},{6,8},{7,9},{8,10},{9,11},{10,... | collective-permute-start | bytes 393224 | tf_op jit(solution)/shard_map/ppermute | solution.py:33
  4.8 3.4 %collective-permute-start.2 = (bf16[256,768]{1,0:T(8,128)(2,1)S(1)}, bf16[256,768]{1,0:T(8,128)(2,1)S(1)}, u32[]{:S(2)}, u32[]{:S(2)}) collective-permute-start(bf16[256,768]{1,0:T(8,128)(2,1)S(1)} %get-tuple-element.38.own.refs_9_), channel_id=1, source_target_pairs={{0,2},{1,3},{2,4},{3,5},{4,6},{5,7},{6,8},{7,9},{8,10},{9,11},{10,... | collective-permute-start | bytes 1179656 | tf_op jit(solution)/shard_map/ppermute | solution.py:33
  8.2 0.0 copy-start
  8.3 0.6 %copy-done = s32[16]{0:T(128)S(1)} copy-done((s32[16]{0:T(128)S(1)}, s32[16]{0:T(128)}, u32[]{:S(2)}) %copy-start) | copy-done | bytes 88
  8.9 1.8 %prepare.1 = (f32[2,128,640]{2,1,0:T(8,128)S(1)}, bf16[256,1024]{1,0:T(8,128)(2,1)S(1)}, bf16[256,1024]{1,0:T(8,128)(2,1)S(1)}) custom-call(s32[16]{0:T(128)S(1)} %copy-done, s32[1]{0:T(128)} %bitcast.first_ref, bf16[256,4096]{1,0:T(8,128)(2,1)} %refs_0_.1, bf16[256,4096]{1,0:T(8,128)(2,1)} %refs_1_.1), custom_call_target="tpu_custom_call" | custom-call | tf_op jit(solution)/shard_map/prepare/pallas_call | solution.py:98
  10.7 0.6 %collective-permute-done.far.refs_2_ = bf16[256,256]{1,0:T(8,128)(2,1)S(1)} collective-permute-done((bf16[256,256]{1,0:T(8,128)(2,1)S(1)}, bf16[256,256]{1,0:T(8,128)(2,1)S(1)}, u32[]{:S(2)}, u32[]{:S(2)}) %collective-permute-start) | collective-permute-done | bytes 131104 | tf_op jit(solution)/shard_map/ppermute | solution.py:33
  11.3 0.1 collective-permute-start.1
  11.4 1.3 %collective-permute-done.1.near.refs_3_ = bf16[256,256]{1,0:T(8,128)(2,1)S(1)} collective-permute-done((bf16[256,256]{1,0:T(8,128)(2,1)S(1)}, bf16[256,256]{1,0:T(8,128)(2,1)S(1)}, u32[]{:S(2)}, u32[]{:S(2)}) %collective-permute-start.1) | collective-permute-done | bytes 131104 | tf_op jit(solution)/shard_map/ppermute | solution.py:33
  12.8 3.2 %attention.2 = (bf16[1,256,1024]{2,1,0:T(8,128)(2,1)S(1)}, bf16[1,2,1024,640]{3,2,1,0:T(8,128)(2,1)S(1)}, bf16[2,2,256,128]{3,2,1,0:T(8,128)(2,1)S(1)}, f32[2,25...) custom-call(s32[1]{0:T(128)} %bitcast.first_ref, ...), custom_call_target="tpu_custom_call" | custom-call | tf_op jit(solution)/shard_map/attention/pallas_call | solution.py:237
  16.0 0.2 collective-permute-start.4
  16.2 0.1 collective-permute-done.2.far.refs_7_
  16.3 0.4 collective-permute-start.3
  16.7 0.7 %collective-permute-done.4 = bf16[2,256,128]{2,1,0:T(8,128)(2,1)S(1)} collective-permute-done((bf16[2,256,128]{2,1,0:T(8,128)(2,1)S(1)}, bf16[2,256,128]{2,1,0:T(8,128)(2,1)S(1)}, u32[]{:S(2)}, u32[]{:S(2)}) %collective-permute-start.4) | collective-permute-done | bytes 131104 | tf_op jit(solution)/shard_map/ppermute | solution.py:33
  17.4 0.1 fusion.1
  17.5 4.5 %collective-permute-start.5 = (bf16[2,256,128]{2,1,0:T(8,128)(2,1)S(1)}, bf16[2,256,128]{2,1,0:T(8,128)(2,1)S(1)}, u32[]{:S(2)}, u32[]{:S(2)}) collective-permute-start(bf16[2,256,128]{2,1,0:T(8,128)(2,1)S(1)} %get-tuple-element.60), channel_id=1, source_target_pairs={{2,0},{3,1},{4,2},{5,3},{6,4},{7,5},{8,6},{9,7},{10,8},{11,9},{12,... | collective-permute-start | bytes 393224 | tf_op jit(solution)/shard_map/ppermute | solution.py:33
  21.9 0.0 collective-permute-done.3.near.refs_8_
  21.9 10.0 %attention.3 = (bf16[3,256,1024]{2,1,0:T(8,128)(2,1)S(1)}, bf16[3,2,1024,640]{3,2,1,0:T(8,128)(2,1)S(1)}, bf16[2,2,256,384]{3,2,1,0:T(8,128)(2,1)S(1)}, f32[2,256,384]{2,1,0:T(8,128)S(1)}) custom-call(s32[1]{0:T(128)} %bitcast.first_ref, f32[2,128,640]{2,1,0:T(8,128)S(1)} %get-tuple-element.33.bias, bf16[256,3072]{1,0:T(8,128)(2,1)S(1)} %get-tuple-element.41.q_ref, ...), custom_call_target="tpu_custom_call" | custom-call | tf_op jit(solution)/shard_map/attention/pallas_call | solution.py:237
  31.9 0.0 collective-permute-done.5.refs_1_
  32.0 0.3 collective-permute-start.6
  32.3 1.5 %collective-permute-done.6 = bf16[2,256,384]{2,1,0:T(8,128)(2,1)S(1)} collective-permute-done((bf16[2,256,384]{2,1,0:T(8,128)(2,1)S(1)}, bf16[2,256,384]{2,1,0:T(8,128)(2,1)S(1)}, u32[]{:S(2)}, u32[]{:S(2)}) %collective-permute-start.6) | collective-permute-done | bytes 393248 | tf_op jit(solution)/shard_map/ppermute | solution.py:33
  33.8 0.2 fusion
  34.0 1.3 %collective-permute-start.7 = (bf16[2,256,384]{2,1,0:T(8,128)(2,1)S(1)}, bf16[2,256,384]{2,1,0:T(8,128)(2,1)S(1)}, u32[]{:S(2)}, u32[]{:S(2)}) collective-permute-start(bf16[2,256,384]{2,1,0:T(8,128)(2,1)S(1)} %get-tuple-element.58), channel_id=1, source_target_pairs={{2,0},{3,1},{4,2},{5,3},{6,4},{7,5},{8,6},{9,7},{10,8},{11,9},{12,... | collective-permute-start | bytes 1179656 | tf_op jit(solution)/shard_map/ppermute | solution.py:33
  35.3 0.7 %finish_keys_values.2 = (bf16[256,512]{1,0:T(8,128)(2,1)}, bf16[256,512]{1,0:T(8,128)(2,1)}) custom-call(f32[2,256,128]{2,1,0:T(8,128)S(1)} %get-tuple-element.61.refs_0_, bf16[2,256,128]{2,1,0:T(8,128)(2,1)S(1)} %collective-permute-done.5.refs_1_), custom_call_target="tpu_custom_call" | custom-call | tf_op jit(solution)/shard_map/finish_keys_values/pallas_call | solution.py:325
  36.0 3.8 %query_grads.1 = (bf16[256,4096]{1,0:T(8,128)(2,1)}, bf16[256,4096]{1,0:T(8,128)(2,1)}) custom-call(bf16[1,256,1024]{2,1,0:T(8,128)(2,1)S(1)} %get-tuple-element.37.refs_0_, bf16[1,2,1024,640]{3,2,1,0:T(8,128)(2,1)S(1)} %get-tuple-element.40.refs_1_, bf16[256,256]{1,0:T(8,128)(2,1)S(1)} %collective-permute-done.far.refs_2_, ...), custom_call_target="tpu_custom_call" | custom-call | tf_op jit(solution)/shard_map/query_grads/pallas_call | solution.py:292
  39.8 7.3 %collective-permute-done.7.refs_3_ = bf16[2,256,384]{2,1,0:T(8,128)(2,1)S(1)} collective-permute-done((bf16[2,256,384]{2,1,0:T(8,128)(2,1)S(1)}, bf16[2,256,384]{2,1,0:T(8,128)(2,1)S(1)}, u32[]{:S(2)}, u32[]{:S(2)}) %collective-permute-start.7) | collective-permute-done | bytes 393248 | tf_op jit(solution)/shard_map/ppermute | solution.py:33
  47.1 0.8 %finish_keys_values.3 = (bf16[256,512]{1,0:T(8,128)(2,1)}, bf16[256,512]{1,0:T(8,128)(2,1)}) custom-call(bf16[256,512]{1,0:T(8,128)(2,1)} %get-tuple-element.52.refs_0_, bf16[256,512]{1,0:T(8,128)(2,1)} %get-tuple-element.53.refs_1_, f32[2,256,384]{2,1,0:T(8,128)S(1)} %get-tuple-element.59.refs_2_, ...), custom_call_target="tpu_custom_call", output_to_operand_aliasing={{0}: (0, {}), {1}: (1, {})} | custom-call | tf_op jit(solution)/shard_map/finish_keys_values/pallas_call | solution.py:325
  (4 shorter events, 0.1 us)
Async XLA Ops:
  1.8 9.6 %collective-permute-start = (bf16[256,256]{1,0:T(8,128)(2,1)S(1)}, bf16[256,256]{1,0:T(8,128)(2,1)S(1)}, u32[]{:S(2)}, u32[]{:S(2)}) collective-permute-start(bf16[256,256]{1,0:T(8,128)(2,1)S(1)} %get-tuple-element.36.own.refs_4_), channel_id=1, source_target_pairs={{0,2},{1,3},{2,4},{3,5},{4,6},{5,7},{6,8},{7,9},{8,10},{9,11},{10,... | collective-permute-start | bytes 393224 | tf_op jit(solution)/shard_map/ppermute | solution.py:33
  4.8 11.5 %collective-permute-start.2 = (bf16[256,768]{1,0:T(8,128)(2,1)S(1)}, bf16[256,768]{1,0:T(8,128)(2,1)S(1)}, u32[]{:S(2)}, u32[]{:S(2)}) collective-permute-start(bf16[256,768]{1,0:T(8,128)(2,1)S(1)} %get-tuple-element.38.own.refs_9_), channel_id=1, source_target_pairs={{0,2},{1,3},{2,4},{3,5},{4,6},{5,7},{6,8},{7,9},{8,10},{9,11},{10,... | collective-permute-start | bytes 1179656 | tf_op jit(solution)/shard_map/ppermute | solution.py:33
  8.2 0.7 %copy-start = (s32[16]{0:T(128)S(1)}, s32[16]{0:T(128)}, u32[]{:S(2)}) copy-start(s32[16]{0:T(128)} %lengths_ref.1) | copy-start | bytes 196
  11.3 1.4 %collective-permute-start.1 = (bf16[256,256]{1,0:T(8,128)(2,1)S(1)}, bf16[256,256]{1,0:T(8,128)(2,1)S(1)}, u32[]{:S(2)}, u32[]{:S(2)}) collective-permute-start(bf16[256,256]{1,0:T(8,128)(2,1)S(1)} %broadcast_select_fusion.1), channel_id=1, source_target_pairs={{0,1},{1,0},{2,3},{3,2},{4,5},{5,4},{6,7},{7,6},{8,9},{9,8},{10,11... | collective-permute-start | bytes 393224 | tf_op jit(solution)/shard_map/ppermute | solution.py:33
  16.0 1.4 %collective-permute-start.4 = (bf16[2,256,128]{2,1,0:T(8,128)(2,1)S(1)}, bf16[2,256,128]{2,1,0:T(8,128)(2,1)S(1)}, u32[]{:S(2)}, u32[]{:S(2)}) collective-permute-start(bf16[2,256,128]{2,1,0:T(8,128)(2,1)S(1)} %slice_bitcast_fusion.1), channel_id=1, source_target_pairs={{0,1},{1,0},{2,3},{3,2},{4,5},{5,4},{6,7},{7,6},{8,9},{9,8},{10,11... | collective-permute-start | bytes 393224 | tf_op jit(solution)/shard_map/ppermute | solution.py:33
  16.3 5.6 %collective-permute-start.3 = (bf16[256,768]{1,0:T(8,128)(2,1)S(1)}, bf16[256,768]{1,0:T(8,128)(2,1)S(1)}, u32[]{:S(2)}, u32[]{:S(2)}) collective-permute-start(bf16[256,768]{1,0:T(8,128)(2,1)S(1)} %broadcast_select_fusion), channel_id=1, source_target_pairs={{0,1},{1,0},{2,3},{3,2},{4,5},{5,4},{6,7},{7,6},{8,9},{9,8},{10,11... | collective-permute-start | bytes 1179656 | tf_op jit(solution)/shard_map/ppermute | solution.py:33
  17.5 14.4 %collective-permute-start.5 = (bf16[2,256,128]{2,1,0:T(8,128)(2,1)S(1)}, bf16[2,256,128]{2,1,0:T(8,128)(2,1)S(1)}, u32[]{:S(2)}, u32[]{:S(2)}) collective-permute-start(bf16[2,256,128]{2,1,0:T(8,128)(2,1)S(1)} %get-tuple-element.60), channel_id=1, source_target_pairs={{2,0},{3,1},{4,2},{5,3},{6,4},{7,5},{8,6},{9,7},{10,8},{11,9},{12,... | collective-permute-start | bytes 393224 | tf_op jit(solution)/shard_map/ppermute | solution.py:33
  32.0 1.8 %collective-permute-start.6 = (bf16[2,256,384]{2,1,0:T(8,128)(2,1)S(1)}, bf16[2,256,384]{2,1,0:T(8,128)(2,1)S(1)}, u32[]{:S(2)}, u32[]{:S(2)}) collective-permute-start(bf16[2,256,384]{2,1,0:T(8,128)(2,1)S(1)} %slice_bitcast_fusion), channel_id=1, source_target_pairs={{0,1},{1,0},{2,3},{3,2},{4,5},{5,4},{6,7},{7,6},{8,9},{9,8},{10,11... | collective-permute-start | bytes 1179656 | tf_op jit(solution)/shard_map/ppermute | solution.py:33
  34.0 13.1 %collective-permute-start.7 = (bf16[2,256,384]{2,1,0:T(8,128)(2,1)S(1)}, bf16[2,256,384]{2,1,0:T(8,128)(2,1)S(1)}, u32[]{:S(2)}, u32[]{:S(2)}) collective-permute-start(bf16[2,256,384]{2,1,0:T(8,128)(2,1)S(1)} %get-tuple-element.58), channel_id=1, source_target_pairs={{2,0},{3,1},{4,2},{5,3},{6,4},{7,5},{8,6},{9,7},{10,8},{11,9},{12,... | collective-permute-start | bytes 1179656 | tf_op jit(solution)/shard_map/ppermute | solution.py:33

commit v7 on v6

--- a/solution.py
+++ b/solution.py
@@ -189,16 +189,19 @@
             dv_sum[:, keys] += matmul(stacked(do_ref, unit), weight, TN)
             dk_sum[:, keys] += matmul(stacked(q_ref, unit), ds, TN)
 
-        ahead = scores(units[0])
+        last = len(units) - 1
+        weight = softmax(units[0], scores(units[0])).astype(jnp.bfloat16)
+        ahead = scores(units[1]) if last else None
         before = None
         for index, unit in enumerate(units):
-            now = ahead
-            if index + 1 < len(units):
-                ahead = scores(units[index + 1])
-            weight = softmax(unit, now).astype(jnp.bfloat16)
+            if index < last:
+                following = softmax(units[index + 1], ahead).astype(jnp.bfloat16)
+            if index + 1 < last:
+                ahead = scores(units[index + 2])
             if before is not None:
                 sums(*before)
             before = (unit, weight, score_grads(unit, weight))
+            weight = following if index < last else None
         sums(*before)
         if lowest:
             for tile in range(tiles):

time: 48.2 us -> 48.3 us (level)
  no operation moved by 1% of the time
where the time goes in v7:
time: 48.3 us; the launch traced here: 48 us
  Pallas kernels  21.5 us (45%)
  starting transfers between devices  13.1 us (27%)
  waiting for transfers between devices  11.5 us (24%)
  between operations  0.93 us (2%)
  local copies, waits for them, and re-layouts  0.7 us (1%)
    pallas_call x2, Pallas kernels, attention(): pl.pallas_call(functools.partial(attention_kernel, base, skipped, fetchin...  13.2 us
    ppermute x8, starting transfers between devices, permuted(): return lax.ppermute(value, 'seq', pairs)  13.1 us
    ppermute x8, waiting for transfers between devices, permuted(): return lax.ppermute(value, 'seq', pairs)  11.5 us
    pallas_call x1, Pallas kernels, query_grads(): pl.pallas_call(functools.partial(query_kernel, calls, skips), in_specs=[p...  3.84 us
    pallas_call x1, Pallas kernels, prepared(): pl.pallas_call(functools.partial(prepare_kernel, lengths.shape[0]), in_sp...  1.81 us
    pallas_call x2, Pallas kernels, finished(): pl.pallas_call(functools.partial(finish_kernel, base, aliased), in_specs=...  1.48 us
    pallas_call x1, Pallas kernels, packed(): pl.pallas_call(functools.partial(pack_kernel, starts, sizes), in_specs=[p...  1.13 us
  transfers between devices with their start and end apart: 8, of which 6 were waited for; matrix products, arithmetic and copies ran while one was open for 0% of the time, Pallas kernels for 41%

profile of v7, /device:TPU:0, one launch (start us, length us, event | category | flops | bytes accessed | tf_op | source)
XLA Modules:
  0.0 48.0 jit_solution(7549477549897327589)
XLA Ops:
  0.6 1.1 %pack_keys_values.1 = (bf16[256,256]{1,0:T(8,128)(2,1)S(1)}, bf16[256,768]{1,0:T(8,128)(2,1)S(1)}) custom-call(bf16[256,512]{1,0:T(8,128)(2,1)} %k_hbm.1, bf16[256,512]{1,0:T(8,128)(2,1)} %v_hbm.1), custom_call_target="tpu_custom_call" | custom-call | tf_op jit(solution)/shard_map/pack_keys_values/pallas_call | solution.py:54
  1.8 3.0 %collective-permute-start = (bf16[256,256]{1,0:T(8,128)(2,1)S(1)}, bf16[256,256]{1,0:T(8,128)(2,1)S(1)}, u32[]{:S(2)}, u32[]{:S(2)}) collective-permute-start(bf16[256,256]{1,0:T(8,128)(2,1)S(1)} %get-tuple-element.36.own.refs_4_), channel_id=1, source_target_pairs={{0,2},{1,3},{2,4},{3,5},{4,6},{5,7},{6,8},{7,9},{8,10},{9,11},{10,... | collective-permute-start | bytes 393224 | tf_op jit(solution)/shard_map/ppermute | solution.py:33
  4.8 3.4 %collective-permute-start.2 = (bf16[256,768]{1,0:T(8,128)(2,1)S(1)}, bf16[256,768]{1,0:T(8,128)(2,1)S(1)}, u32[]{:S(2)}, u32[]{:S(2)}) collective-permute-start(bf16[256,768]{1,0:T(8,128)(2,1)S(1)} %get-tuple-element.38.own.refs_9_), channel_id=1, source_target_pairs={{0,2},{1,3},{2,4},{3,5},{4,6},{5,7},{6,8},{7,9},{8,10},{9,11},{10,... | collective-permute-start | bytes 1179656 | tf_op jit(solution)/shard_map/ppermute | solution.py:33
  8.2 0.0 copy-start
  8.3 0.6 %copy-done = s32[16]{0:T(128)S(1)} copy-done((s32[16]{0:T(128)S(1)}, s32[16]{0:T(128)}, u32[]{:S(2)}) %copy-start) | copy-done | bytes 88
  8.9 1.8 %prepare.1 = (f32[2,128,640]{2,1,0:T(8,128)S(1)}, bf16[256,1024]{1,0:T(8,128)(2,1)S(1)}, bf16[256,1024]{1,0:T(8,128)(2,1)S(1)}) custom-call(s32[16]{0:T(128)S(1)} %copy-done, s32[1]{0:T(128)} %bitcast.first_ref, bf16[256,4096]{1,0:T(8,128)(2,1)} %refs_0_.1, bf16[256,4096]{1,0:T(8,128)(2,1)} %refs_1_.1), custom_call_target="tpu_custom_call" | custom-call | tf_op jit(solution)/shard_map/prepare/pallas_call | solution.py:98
  10.7 0.6 %collective-permute-done.far.refs_2_ = bf16[256,256]{1,0:T(8,128)(2,1)S(1)} collective-permute-done((bf16[256,256]{1,0:T(8,128)(2,1)S(1)}, bf16[256,256]{1,0:T(8,128)(2,1)S(1)}, u32[]{:S(2)}, u32[]{:S(2)}) %collective-permute-start) | collective-permute-done | bytes 131104 | tf_op jit(solution)/shard_map/ppermute | solution.py:33
  11.3 0.1 collective-permute-start.1
  11.4 1.3 %collective-permute-done.1.near.refs_3_ = bf16[256,256]{1,0:T(8,128)(2,1)S(1)} collective-permute-done((bf16[256,256]{1,0:T(8,128)(2,1)S(1)}, bf16[256,256]{1,0:T(8,128)(2,1)S(1)}, u32[]{:S(2)}, u32[]{:S(2)}) %collective-permute-start.1) | collective-permute-done | bytes 131104 | tf_op jit(solution)/shard_map/ppermute | solution.py:33
  12.8 3.2 %attention.2 = (bf16[1,256,1024]{2,1,0:T(8,128)(2,1)S(1)}, bf16[1,2,1024,640]{3,2,1,0:T(8,128)(2,1)S(1)}, bf16[2,2,256,128]{3,2,1,0:T(8,128)(2,1)S(1)}, f32[2,25...) custom-call(s32[1]{0:T(128)} %bitcast.first_ref, ...), custom_call_target="tpu_custom_call" | custom-call | tf_op jit(solution)/shard_map/attention/pallas_call | solution.py:240
  16.0 0.2 collective-permute-start.4
  16.2 0.1 collective-permute-done.2.far.refs_7_
  16.3 0.4 collective-permute-start.3
  16.7 0.7 %collective-permute-done.4 = bf16[2,256,128]{2,1,0:T(8,128)(2,1)S(1)} collective-permute-done((bf16[2,256,128]{2,1,0:T(8,128)(2,1)S(1)}, bf16[2,256,128]{2,1,0:T(8,128)(2,1)S(1)}, u32[]{:S(2)}, u32[]{:S(2)}) %collective-permute-start.4) | collective-permute-done | bytes 131104 | tf_op jit(solution)/shard_map/ppermute | solution.py:33
  17.4 0.1 fusion.1
  17.5 4.4 %collective-permute-start.5 = (bf16[2,256,128]{2,1,0:T(8,128)(2,1)S(1)}, bf16[2,256,128]{2,1,0:T(8,128)(2,1)S(1)}, u32[]{:S(2)}, u32[]{:S(2)}) collective-permute-start(bf16[2,256,128]{2,1,0:T(8,128)(2,1)S(1)} %get-tuple-element.60), channel_id=1, source_target_pairs={{2,0},{3,1},{4,2},{5,3},{6,4},{7,5},{8,6},{9,7},{10,8},{11,9},{12,... | collective-permute-start | bytes 393224 | tf_op jit(solution)/shard_map/ppermute | solution.py:33
  21.9 0.0 collective-permute-done.3.near.refs_8_
  21.9 10.0 %attention.3 = (bf16[3,256,1024]{2,1,0:T(8,128)(2,1)S(1)}, bf16[3,2,1024,640]{3,2,1,0:T(8,128)(2,1)S(1)}, bf16[2,2,256,384]{3,2,1,0:T(8,128)(2,1)S(1)}, f32[2,256,384]{2,1,0:T(8,128)S(1)}) custom-call(s32[1]{0:T(128)} %bitcast.first_ref, f32[2,128,640]{2,1,0:T(8,128)S(1)} %get-tuple-element.33.bias, bf16[256,3072]{1,0:T(8,128)(2,1)S(1)} %get-tuple-element.41.q_ref, ...), custom_call_target="tpu_custom_call" | custom-call | tf_op jit(solution)/shard_map/attention/pallas_call | solution.py:240
  31.9 0.0 collective-permute-done.5.refs_1_
  32.0 0.3 collective-permute-start.6
  32.3 1.5 %collective-permute-done.6 = bf16[2,256,384]{2,1,0:T(8,128)(2,1)S(1)} collective-permute-done((bf16[2,256,384]{2,1,0:T(8,128)(2,1)S(1)}, bf16[2,256,384]{2,1,0:T(8,128)(2,1)S(1)}, u32[]{:S(2)}, u32[]{:S(2)}) %collective-permute-start.6) | collective-permute-done | bytes 393248 | tf_op jit(solution)/shard_map/ppermute | solution.py:33
  33.8 0.2 fusion
  34.0 1.3 %collective-permute-start.7 = (bf16[2,256,384]{2,1,0:T(8,128)(2,1)S(1)}, bf16[2,256,384]{2,1,0:T(8,128)(2,1)S(1)}, u32[]{:S(2)}, u32[]{:S(2)}) collective-permute-start(bf16[2,256,384]{2,1,0:T(8,128)(2,1)S(1)} %get-tuple-element.58), channel_id=1, source_target_pairs={{2,0},{3,1},{4,2},{5,3},{6,4},{7,5},{8,6},{9,7},{10,8},{11,9},{12,... | collective-permute-start | bytes 1179656 | tf_op jit(solution)/shard_map/ppermute | solution.py:33
  35.3 0.7 %finish_keys_values.2 = (bf16[256,512]{1,0:T(8,128)(2,1)}, bf16[256,512]{1,0:T(8,128)(2,1)}) custom-call(f32[2,256,128]{2,1,0:T(8,128)S(1)} %get-tuple-element.61.refs_0_, bf16[2,256,128]{2,1,0:T(8,128)(2,1)S(1)} %collective-permute-done.5.refs_1_), custom_call_target="tpu_custom_call" | custom-call | tf_op jit(solution)/shard_map/finish_keys_values/pallas_call | solution.py:328
  36.0 3.8 %query_grads.1 = (bf16[256,4096]{1,0:T(8,128)(2,1)}, bf16[256,4096]{1,0:T(8,128)(2,1)}) custom-call(bf16[1,256,1024]{2,1,0:T(8,128)(2,1)S(1)} %get-tuple-element.37.refs_0_, bf16[1,2,1024,640]{3,2,1,0:T(8,128)(2,1)S(1)} %get-tuple-element.40.refs_1_, bf16[256,256]{1,0:T(8,128)(2,1)S(1)} %collective-permute-done.far.refs_2_, ...), custom_call_target="tpu_custom_call" | custom-call | tf_op jit(solution)/shard_map/query_grads/pallas_call | solution.py:295
  39.8 7.3 %collective-permute-done.7.refs_3_ = bf16[2,256,384]{2,1,0:T(8,128)(2,1)S(1)} collective-permute-done((bf16[2,256,384]{2,1,0:T(8,128)(2,1)S(1)}, bf16[2,256,384]{2,1,0:T(8,128)(2,1)S(1)}, u32[]{:S(2)}, u32[]{:S(2)}) %collective-permute-start.7) | collective-permute-done | bytes 393248 | tf_op jit(solution)/shard_map/ppermute | solution.py:33
  47.1 0.8 %finish_keys_values.3 = (bf16[256,512]{1,0:T(8,128)(2,1)}, bf16[256,512]{1,0:T(8,128)(2,1)}) custom-call(bf16[256,512]{1,0:T(8,128)(2,1)} %get-tuple-element.52.refs_0_, bf16[256,512]{1,0:T(8,128)(2,1)} %get-tuple-element.53.refs_1_, f32[2,256,384]{2,1,0:T(8,128)S(1)} %get-tuple-element.59.refs_2_, ...), custom_call_target="tpu_custom_call", output_to_operand_aliasing={{0}: (0, {}), {1}: (1, {})} | custom-call | tf_op jit(solution)/shard_map/finish_keys_values/pallas_call | solution.py:328
  (4 shorter events, 0.1 us)
Async XLA Ops:
  1.8 9.6 %collective-permute-start = (bf16[256,256]{1,0:T(8,128)(2,1)S(1)}, bf16[256,256]{1,0:T(8,128)(2,1)S(1)}, u32[]{:S(2)}, u32[]{:S(2)}) collective-permute-start(bf16[256,256]{1,0:T(8,128)(2,1)S(1)} %get-tuple-element.36.own.refs_4_), channel_id=1, source_target_pairs={{0,2},{1,3},{2,4},{3,5},{4,6},{5,7},{6,8},{7,9},{8,10},{9,11},{10,... | collective-permute-start | bytes 393224 | tf_op jit(solution)/shard_map/ppermute | solution.py:33
  4.8 11.5 %collective-permute-start.2 = (bf16[256,768]{1,0:T(8,128)(2,1)S(1)}, bf16[256,768]{1,0:T(8,128)(2,1)S(1)}, u32[]{:S(2)}, u32[]{:S(2)}) collective-permute-start(bf16[256,768]{1,0:T(8,128)(2,1)S(1)} %get-tuple-element.38.own.refs_9_), channel_id=1, source_target_pairs={{0,2},{1,3},{2,4},{3,5},{4,6},{5,7},{6,8},{7,9},{8,10},{9,11},{10,... | collective-permute-start | bytes 1179656 | tf_op jit(solution)/shard_map/ppermute | solution.py:33
  8.2 0.7 %copy-start = (s32[16]{0:T(128)S(1)}, s32[16]{0:T(128)}, u32[]{:S(2)}) copy-start(s32[16]{0:T(128)} %lengths_ref.1) | copy-start | bytes 196
  11.3 1.4 %collective-permute-start.1 = (bf16[256,256]{1,0:T(8,128)(2,1)S(1)}, bf16[256,256]{1,0:T(8,128)(2,1)S(1)}, u32[]{:S(2)}, u32[]{:S(2)}) collective-permute-start(bf16[256,256]{1,0:T(8,128)(2,1)S(1)} %broadcast_select_fusion.1), channel_id=1, source_target_pairs={{0,1},{1,0},{2,3},{3,2},{4,5},{5,4},{6,7},{7,6},{8,9},{9,8},{10,11... | collective-permute-start | bytes 393224 | tf_op jit(solution)/shard_map/ppermute | solution.py:33
  16.0 1.4 %collective-permute-start.4 = (bf16[2,256,128]{2,1,0:T(8,128)(2,1)S(1)}, bf16[2,256,128]{2,1,0:T(8,128)(2,1)S(1)}, u32[]{:S(2)}, u32[]{:S(2)}) collective-permute-start(bf16[2,256,128]{2,1,0:T(8,128)(2,1)S(1)} %slice_bitcast_fusion.1), channel_id=1, source_target_pairs={{0,1},{1,0},{2,3},{3,2},{4,5},{5,4},{6,7},{7,6},{8,9},{9,8},{10,11... | collective-permute-start | bytes 393224 | tf_op jit(solution)/shard_map/ppermute | solution.py:33
  16.3 5.6 %collective-permute-start.3 = (bf16[256,768]{1,0:T(8,128)(2,1)S(1)}, bf16[256,768]{1,0:T(8,128)(2,1)S(1)}, u32[]{:S(2)}, u32[]{:S(2)}) collective-permute-start(bf16[256,768]{1,0:T(8,128)(2,1)S(1)} %broadcast_select_fusion), channel_id=1, source_target_pairs={{0,1},{1,0},{2,3},{3,2},{4,5},{5,4},{6,7},{7,6},{8,9},{9,8},{10,11... | collective-permute-start | bytes 1179656 | tf_op jit(solution)/shard_map/ppermute | solution.py:33
  17.5 14.4 %collective-permute-start.5 = (bf16[2,256,128]{2,1,0:T(8,128)(2,1)S(1)}, bf16[2,256,128]{2,1,0:T(8,128)(2,1)S(1)}, u32[]{:S(2)}, u32[]{:S(2)}) collective-permute-start(bf16[2,256,128]{2,1,0:T(8,128)(2,1)S(1)} %get-tuple-element.60), channel_id=1, source_target_pairs={{2,0},{3,1},{4,2},{5,3},{6,4},{7,5},{8,6},{9,7},{10,8},{11,9},{12,... | collective-permute-start | bytes 393224 | tf_op jit(solution)/shard_map/ppermute | solution.py:33
  32.0 1.8 %collective-permute-start.6 = (bf16[2,256,384]{2,1,0:T(8,128)(2,1)S(1)}, bf16[2,256,384]{2,1,0:T(8,128)(2,1)S(1)}, u32[]{:S(2)}, u32[]{:S(2)}) collective-permute-start(bf16[2,256,384]{2,1,0:T(8,128)(2,1)S(1)} %slice_bitcast_fusion), channel_id=1, source_target_pairs={{0,1},{1,0},{2,3},{3,2},{4,5},{5,4},{6,7},{7,6},{8,9},{9,8},{10,11... | collective-permute-start | bytes 1179656 | tf_op jit(solution)/shard_map/ppermute | solution.py:33
  34.0 13.1 %collective-permute-start.7 = (bf16[2,256,384]{2,1,0:T(8,128)(2,1)S(1)}, bf16[2,256,384]{2,1,0:T(8,128)(2,1)S(1)}, u32[]{:S(2)}, u32[]{:S(2)}) collective-permute-start(bf16[2,256,384]{2,1,0:T(8,128)(2,1)S(1)} %get-tuple-element.58), channel_id=1, source_target_pairs={{2,0},{3,1},{4,2},{5,3},{6,4},{7,5},{8,6},{9,7},{10,8},{11,9},{12,... | collective-permute-start | bytes 1179656 | tf_op jit(solution)/shard_map/ppermute | solution.py:33

commit v8 on v6

--- a/solution.py
+++ b/solution.py
@@ -213,11 +213,18 @@
             back_ref[place, 0, :, here] = (dk_sum[:, span].T * FACTOR).astype(jnp.bfloat16)
             back_ref[place, 1, :, here] = dv_sum[:, span].T.astype(jnp.bfloat16)
 
-    @pl.when(first_ref[0] >= 2 * rows)
+    def later(index, carry):
+        begin, start = carry
+        return begin + first_ref[index + 1], jnp.where(begin <= first_ref[0], begin, start)
+
+    _, start = lax.fori_loop(0, first_ref.shape[0] - 1, later, (jnp.int32(0), jnp.int32(0)))
+    reaches_far = start < first_ref[0] - rows
+
+    @pl.when(reaches_far)
     def _():
         all_units(0)
 
-    @pl.when(first_ref[0] < 2 * rows)
+    @pl.when(jnp.logical_not(reaches_far))
     def _():
         all_units(rows)
 
@@ -359,6 +366,7 @@
     own = list(packed(k_here, v_here, [start * HEAD_DIM for start in starts], [size * HEAD_DIM for size in sent]))
     far = [permuted(block, ahead_open if index else ahead) for index, block in enumerate(own)]
     head_cols = queries.shape[1] // groups
+    begins = jnp.concatenate([first, episode_lengths])
     bias, q_part, do_part = prepared(episode_lengths, first, q_here, do_here, calls[0] * head_cols)
     own[0], bias = lax.optimization_barrier((own[0], bias))
     near = []
@@ -379,11 +387,11 @@
             near.append(permuted(jnp.where(odd == 1, there, own[chunk]), swap))
         if base == 0 and size < groups:
             out, ds, back, kept, q_part, do_part = attention(
-                0, size, skips[-1], head_cols, first, bias, q_part, do_part, far[chunk], near[chunk], own[chunk], q_here, do_here
+                0, size, skips[-1], head_cols, begins, bias, q_part, do_part, far[chunk], near[chunk], own[chunk], q_here, do_here
             )
         else:
             out, ds, back, kept = attention(
-                base - (calls[0] if base else 0), size, skips[-1], head_cols, first, bias, q_part, do_part, far[chunk], near[chunk], own[chunk]
+                base - (calls[0] if base else 0), size, skips[-1], head_cols, begins, bias, q_part, do_part, far[chunk], near[chunk], own[chunk]
             )
         stored.append((out, ds, far[chunk], near[chunk], own[chunk]))
         waiting.append((back, kept))

time: 48.2 us -> 49.1 us (1.019)
  Pallas kernels: 21.4 us -> 22.9 us
  starting transfers between devices: 13.1 us -> 12.5 us
    pallas_call x2, Pallas kernels: 13.2 us -> 14.7 us  [attention(): pl.pallas_call(functools.partial(attention_kernel, base, skipped, fetchin...]
    ppermute x8, starting transfers between devices: 13.1 us -> 12.5 us  [permuted(): return lax.ppermute(value, 'seq', pairs)]
  transfers between devices with their start and end apart: 8 -> 8, of which waited for: 6 -> 5; matrix products, arithmetic and copies ran while one was open for 0% -> 0% of each run, Pallas kernels for 41% -> 43%
where the time goes in v8:
time: 49.1 us; the launch traced here: 48.9 us
  Pallas kernels  22.9 us (47%)
  starting transfers between devices  12.5 us (25%)
  waiting for transfers between devices  11.4 us (23%)
  between operations  0.93 us (2%)
  local copies, waits for them, and re-layouts  0.71 us (1%)
    pallas_call x2, Pallas kernels, attention(): pl.pallas_call(functools.partial(attention_kernel, base, skipped, fetchin...  14.7 us
    ppermute x8, starting transfers between devices, permuted(): return lax.ppermute(value, 'seq', pairs)  12.5 us
    ppermute x8, waiting for transfers between devices, permuted(): return lax.ppermute(value, 'seq', pairs)  11.4 us
    pallas_call x1, Pallas kernels, query_grads(): pl.pallas_call(functools.partial(query_kernel, calls, skips), in_specs=[p...  3.84 us
    pallas_call x1, Pallas kernels, prepared(): pl.pallas_call(functools.partial(prepare_kernel, lengths.shape[0]), in_sp...  1.81 us
    pallas_call x2, Pallas kernels, finished(): pl.pallas_call(functools.partial(finish_kernel, base, aliased), in_specs=...  1.48 us
    pallas_call x1, Pallas kernels, packed(): pl.pallas_call(functools.partial(pack_kernel, starts, sizes), in_specs=[p...  1.13 us
  transfers between devices with their start and end apart: 8, of which 5 were waited for; matrix products, arithmetic and copies ran while one was open for 0% of the time, Pallas kernels for 43%

profile of v8, /device:TPU:0, one launch (start us, length us, event | category | flops | bytes accessed | tf_op | source)
XLA Modules:
  0.0 48.9 jit_solution(11234143633410239246)
XLA Ops:
  0.6 1.1 %pack_keys_values.1 = (bf16[256,256]{1,0:T(8,128)(2,1)S(1)}, bf16[256,768]{1,0:T(8,128)(2,1)S(1)}) custom-call(bf16[256,512]{1,0:T(8,128)(2,1)} %k_hbm.1, bf16[256,512]{1,0:T(8,128)(2,1)} %v_hbm.1), custom_call_target="tpu_custom_call" | custom-call | tf_op jit(solution)/shard_map/pack_keys_values/pallas_call | solution.py:54
  1.8 3.0 %collective-permute-start = (bf16[256,256]{1,0:T(8,128)(2,1)S(1)}, bf16[256,256]{1,0:T(8,128)(2,1)S(1)}, u32[]{:S(2)}, u32[]{:S(2)}) collective-permute-start(bf16[256,256]{1,0:T(8,128)(2,1)S(1)} %get-tuple-element.36.own.refs_4_), channel_id=1, source_target_pairs={{0,2},{1,3},{2,4},{3,5},{4,6},{5,7},{6,8},{7,9},{8,10},{9,11},{10,... | collective-permute-start | bytes 393224 | tf_op jit(solution)/shard_map/ppermute | solution.py:33
  4.8 3.4 %collective-permute-start.2 = (bf16[256,768]{1,0:T(8,128)(2,1)S(1)}, bf16[256,768]{1,0:T(8,128)(2,1)S(1)}, u32[]{:S(2)}, u32[]{:S(2)}) collective-permute-start(bf16[256,768]{1,0:T(8,128)(2,1)S(1)} %get-tuple-element.38.own.refs_9_), channel_id=1, source_target_pairs={{0,2},{1,3},{2,4},{3,5},{4,6},{5,7},{6,8},{7,9},{8,10},{9,11},{10,... | collective-permute-start | bytes 1179656 | tf_op jit(solution)/shard_map/ppermute | solution.py:33
  8.2 0.0 copy-start
  8.2 0.6 %copy-done = s32[16]{0:T(128)S(1)} copy-done((s32[16]{0:T(128)S(1)}, s32[16]{0:T(128)}, u32[]{:S(2)}) %copy-start) | copy-done | bytes 88
  8.9 0.0 copy-start.1
  8.9 1.8 %prepare.1 = (f32[2,128,640]{2,1,0:T(8,128)S(1)}, bf16[256,1024]{1,0:T(8,128)(2,1)S(1)}, bf16[256,1024]{1,0:T(8,128)(2,1)S(1)}) custom-call(s32[16]{0:T(128)S(1)} %copy-done, s32[1]{0:T(128)} %bitcast.first_ref, bf16[256,4096]{1,0:T(8,128)(2,1)} %refs_0_.1, bf16[256,4096]{1,0:T(8,128)(2,1)} %refs_1_.1), custom_call_target="tpu_custom_call" | custom-call | tf_op jit(solution)/shard_map/prepare/pallas_call | solution.py:98
  10.7 0.6 %collective-permute-done.far.refs_2_ = bf16[256,256]{1,0:T(8,128)(2,1)S(1)} collective-permute-done((bf16[256,256]{1,0:T(8,128)(2,1)S(1)}, bf16[256,256]{1,0:T(8,128)(2,1)S(1)}, u32[]{:S(2)}, u32[]{:S(2)}) %collective-permute-start) | collective-permute-done | bytes 131104 | tf_op jit(solution)/shard_map/ppermute | solution.py:33
  11.3 0.1 collective-permute-start.1
  11.4 0.0 copy-done.1
  11.4 0.1 pad_add_fusion.first_ref
  11.5 1.2 %collective-permute-done.1.near.refs_3_ = bf16[256,256]{1,0:T(8,128)(2,1)S(1)} collective-permute-done((bf16[256,256]{1,0:T(8,128)(2,1)S(1)}, bf16[256,256]{1,0:T(8,128)(2,1)S(1)}, u32[]{:S(2)}, u32[]{:S(2)}) %collective-permute-start.1) | collective-permute-done | bytes 131104 | tf_op jit(solution)/shard_map/ppermute | solution.py:33
  12.8 3.9 %attention.2 = (bf16[1,256,1024]{2,1,0:T(8,128)(2,1)S(1)}, bf16[1,2,1024,640]{3,2,1,0:T(8,128)(2,1)S(1)}, bf16[2,2,256,128]{3,2,1,0:T(8,128)(2,1)S(1)}, f32[2,25...) custom-call(s32[17]{0:T(128)S(1)} %pad_add_fusion.first_ref, ...), custom_call_target="tpu_custom_call" | custom-call | tf_op jit(solution)/shard_map/attention/pallas_call | solution.py:244
  16.6 0.2 collective-permute-start.4
  16.8 0.0 collective-permute-done.2.far.refs_7_
  16.9 0.4 collective-permute-start.3
  17.3 0.7 %collective-permute-done.4 = bf16[2,256,128]{2,1,0:T(8,128)(2,1)S(1)} collective-permute-done((bf16[2,256,128]{2,1,0:T(8,128)(2,1)S(1)}, bf16[2,256,128]{2,1,0:T(8,128)(2,1)S(1)}, u32[]{:S(2)}, u32[]{:S(2)}) %collective-permute-start.4) | collective-permute-done | bytes 131104 | tf_op jit(solution)/shard_map/ppermute | solution.py:33
  18.0 0.1 fusion.1
  18.1 3.8 %collective-permute-start.5 = (bf16[2,256,128]{2,1,0:T(8,128)(2,1)S(1)}, bf16[2,256,128]{2,1,0:T(8,128)(2,1)S(1)}, u32[]{:S(2)}, u32[]{:S(2)}) collective-permute-start(bf16[2,256,128]{2,1,0:T(8,128)(2,1)S(1)} %get-tuple-element.60), channel_id=1, source_target_pairs={{2,0},{3,1},{4,2},{5,3},{6,4},{7,5},{8,6},{9,7},{10,8},{11,9},{12,... | collective-permute-start | bytes 393224 | tf_op jit(solution)/shard_map/ppermute | solution.py:33
  21.9 0.0 collective-permute-done.3.near.refs_8_
  21.9 10.8 %attention.3 = (bf16[3,256,1024]{2,1,0:T(8,128)(2,1)S(1)}, bf16[3,2,1024,640]{3,2,1,0:T(8,128)(2,1)S(1)}, bf16[2,2,256,384]{3,2,1,0:T(8,128)(2,1)S(1)}, f32[2,256,384]{2,1,0:T(8,128)S(1)}) custom-call(s32[17]{0:T(128)S(1)} %pad_add_fusion.first_ref, f32[2,128,640]{2,1,0:T(8,128)S(1)} %get-tuple-element.33.bias, ...), custom_call_target="tpu_custom_call" | custom-call | tf_op jit(solution)/shard_map/attention/pallas_call | solution.py:244
  32.8 0.0 collective-permute-done.5.refs_1_
  32.8 0.3 collective-permute-start.6
  33.1 1.5 %collective-permute-done.6 = bf16[2,256,384]{2,1,0:T(8,128)(2,1)S(1)} collective-permute-done((bf16[2,256,384]{2,1,0:T(8,128)(2,1)S(1)}, bf16[2,256,384]{2,1,0:T(8,128)(2,1)S(1)}, u32[]{:S(2)}, u32[]{:S(2)}) %collective-permute-start.6) | collective-permute-done | bytes 393248 | tf_op jit(solution)/shard_map/ppermute | solution.py:33
  34.6 0.2 fusion
  34.8 1.3 %collective-permute-start.7 = (bf16[2,256,384]{2,1,0:T(8,128)(2,1)S(1)}, bf16[2,256,384]{2,1,0:T(8,128)(2,1)S(1)}, u32[]{:S(2)}, u32[]{:S(2)}) collective-permute-start(bf16[2,256,384]{2,1,0:T(8,128)(2,1)S(1)} %get-tuple-element.58), channel_id=1, source_target_pairs={{2,0},{3,1},{4,2},{5,3},{6,4},{7,5},{8,6},{9,7},{10,8},{11,9},{12,... | collective-permute-start | bytes 1179656 | tf_op jit(solution)/shard_map/ppermute | solution.py:33
  36.1 0.7 %finish_keys_values.2 = (bf16[256,512]{1,0:T(8,128)(2,1)}, bf16[256,512]{1,0:T(8,128)(2,1)}) custom-call(f32[2,256,128]{2,1,0:T(8,128)S(1)} %get-tuple-element.61.refs_0_, bf16[2,256,128]{2,1,0:T(8,128)(2,1)S(1)} %collective-permute-done.5.refs_1_), custom_call_target="tpu_custom_call" | custom-call | tf_op jit(solution)/shard_map/finish_keys_values/pallas_call | solution.py:332
  36.8 3.8 %query_grads.1 = (bf16[256,4096]{1,0:T(8,128)(2,1)}, bf16[256,4096]{1,0:T(8,128)(2,1)}) custom-call(bf16[1,256,1024]{2,1,0:T(8,128)(2,1)S(1)} %get-tuple-element.37.refs_0_, bf16[1,2,1024,640]{3,2,1,0:T(8,128)(2,1)S(1)} %get-tuple-element.40.refs_1_, bf16[256,256]{1,0:T(8,128)(2,1)S(1)} %collective-permute-done.far.refs_2_, ...), custom_call_target="tpu_custom_call" | custom-call | tf_op jit(solution)/shard_map/query_grads/pallas_call | solution.py:299
  40.6 7.3 %collective-permute-done.7.refs_3_ = bf16[2,256,384]{2,1,0:T(8,128)(2,1)S(1)} collective-permute-done((bf16[2,256,384]{2,1,0:T(8,128)(2,1)S(1)}, bf16[2,256,384]{2,1,0:T(8,128)(2,1)S(1)}, u32[]{:S(2)}, u32[]{:S(2)}) %collective-permute-start.7) | collective-permute-done | bytes 393248 | tf_op jit(solution)/shard_map/ppermute | solution.py:33
  47.9 0.8 %finish_keys_values.3 = (bf16[256,512]{1,0:T(8,128)(2,1)}, bf16[256,512]{1,0:T(8,128)(2,1)}) custom-call(bf16[256,512]{1,0:T(8,128)(2,1)} %get-tuple-element.52.refs_0_, bf16[256,512]{1,0:T(8,128)(2,1)} %get-tuple-element.53.refs_1_, f32[2,256,384]{2,1,0:T(8,128)S(1)} %get-tuple-element.59.refs_2_, ...), custom_call_target="tpu_custom_call", output_to_operand_aliasing={{0}: (0, {}), {1}: (1, {})} | custom-call | tf_op jit(solution)/shard_map/finish_keys_values/pallas_call | solution.py:332
  (4 shorter events, 0.1 us)
Async XLA Ops:
  1.8 9.6 %collective-permute-start = (bf16[256,256]{1,0:T(8,128)(2,1)S(1)}, bf16[256,256]{1,0:T(8,128)(2,1)S(1)}, u32[]{:S(2)}, u32[]{:S(2)}) collective-permute-start(bf16[256,256]{1,0:T(8,128)(2,1)S(1)} %get-tuple-element.36.own.refs_4_), channel_id=1, source_target_pairs={{0,2},{1,3},{2,4},{3,5},{4,6},{5,7},{6,8},{7,9},{8,10},{9,11},{10,... | collective-permute-start | bytes 393224 | tf_op jit(solution)/shard_map/ppermute | solution.py:33
  4.8 12.1 %collective-permute-start.2 = (bf16[256,768]{1,0:T(8,128)(2,1)S(1)}, bf16[256,768]{1,0:T(8,128)(2,1)S(1)}, u32[]{:S(2)}, u32[]{:S(2)}) collective-permute-start(bf16[256,768]{1,0:T(8,128)(2,1)S(1)} %get-tuple-element.38.own.refs_9_), channel_id=1, source_target_pairs={{0,2},{1,3},{2,4},{3,5},{4,6},{5,7},{6,8},{7,9},{8,10},{9,11},{10,... | collective-permute-start | bytes 1179656 | tf_op jit(solution)/shard_map/ppermute | solution.py:33
  8.2 0.7 %copy-start = (s32[16]{0:T(128)S(1)}, s32[16]{0:T(128)}, u32[]{:S(2)}) copy-start(s32[16]{0:T(128)} %lengths_ref.1) | copy-start | bytes 196
  8.9 2.5 %copy-start.1 = (s32[16]{0:T(128)S(1)}, s32[16]{0:T(128)}, u32[]{:S(2)}) copy-start(s32[16]{0:T(128)} %lengths_ref.1) | copy-start | bytes 196
  11.3 1.4 %collective-permute-start.1 = (bf16[256,256]{1,0:T(8,128)(2,1)S(1)}, bf16[256,256]{1,0:T(8,128)(2,1)S(1)}, u32[]{:S(2)}, u32[]{:S(2)}) collective-permute-start(bf16[256,256]{1,0:T(8,128)(2,1)S(1)} %broadcast_select_fusion.1), channel_id=1, source_target_pairs={{0,1},{1,0},{2,3},{3,2},{4,5},{5,4},{6,7},{7,6},{8,9},{9,8},{10,11... | collective-permute-start | bytes 393224 | tf_op jit(solution)/shard_map/ppermute | solution.py:33
  16.6 1.4 %collective-permute-start.4 = (bf16[2,256,128]{2,1,0:T(8,128)(2,1)S(1)}, bf16[2,256,128]{2,1,0:T(8,128)(2,1)S(1)}, u32[]{:S(2)}, u32[]{:S(2)}) collective-permute-start(bf16[2,256,128]{2,1,0:T(8,128)(2,1)S(1)} %slice_bitcast_fusion.1), channel_id=1, source_target_pairs={{0,1},{1,0},{2,3},{3,2},{4,5},{5,4},{6,7},{7,6},{8,9},{9,8},{10,11... | collective-permute-start | bytes 393224 | tf_op jit(solution)/shard_map/ppermute | solution.py:33
  16.9 5.0 %collective-permute-start.3 = (bf16[256,768]{1,0:T(8,128)(2,1)S(1)}, bf16[256,768]{1,0:T(8,128)(2,1)S(1)}, u32[]{:S(2)}, u32[]{:S(2)}) collective-permute-start(bf16[256,768]{1,0:T(8,128)(2,1)S(1)} %broadcast_select_fusion), channel_id=1, source_target_pairs={{0,1},{1,0},{2,3},{3,2},{4,5},{5,4},{6,7},{7,6},{8,9},{9,8},{10,11... | collective-permute-start | bytes 1179656 | tf_op jit(solution)/shard_map/ppermute | solution.py:33
  18.1 14.7 %collective-permute-start.5 = (bf16[2,256,128]{2,1,0:T(8,128)(2,1)S(1)}, bf16[2,256,128]{2,1,0:T(8,128)(2,1)S(1)}, u32[]{:S(2)}, u32[]{:S(2)}) collective-permute-start(bf16[2,256,128]{2,1,0:T(8,128)(2,1)S(1)} %get-tuple-element.60), channel_id=1, source_target_pairs={{2,0},{3,1},{4,2},{5,3},{6,4},{7,5},{8,6},{9,7},{10,8},{11,9},{12,... | collective-permute-start | bytes 393224 | tf_op jit(solution)/shard_map/ppermute | solution.py:33
  32.8 1.8 %collective-permute-start.6 = (bf16[2,256,384]{2,1,0:T(8,128)(2,1)S(1)}, bf16[2,256,384]{2,1,0:T(8,128)(2,1)S(1)}, u32[]{:S(2)}, u32[]{:S(2)}) collective-permute-start(bf16[2,256,384]{2,1,0:T(8,128)(2,1)S(1)} %slice_bitcast_fusion), channel_id=1, source_target_pairs={{0,1},{1,0},{2,3},{3,2},{4,5},{5,4},{6,7},{7,6},{8,9},{9,8},{10,11... | collective-permute-start | bytes 1179656 | tf_op jit(solution)/shard_map/ppermute | solution.py:33
  34.8 13.1 %collective-permute-start.7 = (bf16[2,256,384]{2,1,0:T(8,128)(2,1)S(1)}, bf16[2,256,384]{2,1,0:T(8,128)(2,1)S(1)}, u32[]{:S(2)}, u32[]{:S(2)}) collective-permute-start(bf16[2,256,384]{2,1,0:T(8,128)(2,1)S(1)} %get-tuple-element.58), channel_id=1, source_target_pairs={{2,0},{3,1},{4,2},{5,3},{6,4},{7,5},{8,6},{9,7},{10,8},{11,9},{12,... | collective-permute-start | bytes 1179656 | tf_op jit(solution)/shard_map/ppermute | solution.py:33
